TPU v7x, 32 devices: a whole 2x2x4 slice. The times are simulated.
32 devices in a mesh: groups: 2 (over y), inst: 4 (over x, core), space: 4 (over z).
Axes of the slice: x: 2, y: 2, z: 4, core: 2. Of those that a mesh axis runs over, the one named last changes fastest.
Arguments:
- flow_state: float32 [8, 6, 256, 256], P(('groups', 'inst'), None, 'space'), parts along dimension 0, may hold values from -0.8 to 3.2, as said below
- cell_volume: float32 [512, 256], P(('groups', 'space')), parts along dimension 0, may hold values from 0.5 to 2
- frequency: float32 [1], replicated, may hold values from 0.5 to 1.5
- block_count: int32 [8], P('groups'), parts along dimension 0, may hold values from 1 to 4, 8 in all
- block_place: int32 [16], P('groups'), parts along dimension 0, may hold values from 0 to 7, each once
- face_links: int32 [16, 2], P('groups'), parts along dimension 0, may hold values from -1 to 7
- face_offset: int32 [16, 2], P('groups'), parts along dimension 0, may hold values from 0 to 255
- face_flip: int32 [16, 2], P('groups'), parts along dimension 0, may hold values from 0 to 1
Outputs:
- new_state: float32 [8, 6, 256, 256], P(('groups', 'inst'), None, 'space'), parts along dimension 0
- last_residual: float32 [8, 6, 256, 256], P(('groups', 'inst'), None, 'space'), parts along dimension 0
There are 2 independent parts, one for each index of `groups`. A program takes and returns all parts, laid end to end along the dimension named above; an argument that names none is the same for every part. Nothing has to cross between parts.
Inputs may be any that keep to these rules, and one draw needn't show every extreme that they name: `block_count`: 8 live blocks in all; some device holds exactly 4. `face_links`: a face link of -1 marks a boundary face. `flow_state`: density lies within 0.75 to 1.25 and energy within 2 to 3.2.
All inputs are finite; a program needn't handle non-finite values.
Results may differ from a plain program's by a relative error of at most 0.00016.
Values sent between devices are 32-bit elements; how exact they have to be, the bound alone decides.
No kernel may reach another device: no remote copies, remote signals or barrier semaphores. Data moves between devices by JAX's collectives and lax.ppermute only.
A program may use at most 64 MiB of HBM per device.

v0:
```python
import jax
import jax.numpy as jnp
from jax import lax
from jax.sharding import PartitionSpec as P

BLOCKS_MAX = 4
PSEUDO_STEPS = 2


HEAT_RATIO = 1.4
SECOND_DISSIPATION = 0.05
FOURTH_DISSIPATION = 0.02
SOUND_SPEED = 1.0
COURANT = 0.5
TIME_VISCOSITY = 0.25


def spectral_matrix(instance_total, omega_value):
    position = jnp.arange(instance_total, dtype=jnp.int32)
    distance = (position[:, None] - position[None, :]) % instance_total
    parity = (1 - 2 * (distance % 2)).astype(jnp.float32)
    phase_angle = jnp.pi * distance.astype(jnp.float32) / instance_total
    safe_angle = jnp.where(distance == 0, 0.5 * jnp.pi, phase_angle)
    first_derivative = jnp.where(
        distance == 0, 0.0, 0.5 * parity * jnp.cos(safe_angle) / jnp.sin(safe_angle)
    )
    second_derivative = jnp.where(
        distance == 0,
        -(instance_total * instance_total + 2) / 12.0,
        -parity / (2.0 * jnp.sin(safe_angle) ** 2),
    )
    return omega_value * (first_derivative - TIME_VISCOSITY * second_derivative)


def block_tables(
    block_count, block_place, face_links, face_offset, face_flip, targets, slot_count, width
):
    block_total = block_place.shape[0]
    first_position = jnp.cumsum(block_count) - block_count
    block_at_position = (
        jnp.zeros((block_total,), jnp.int32)
        .at[block_place]
        .set(jnp.arange(block_total, dtype=jnp.int32))
    )
    owner_device = jnp.sum(
        (block_place[:, None] >= first_position[None, 1:]).astype(jnp.int32), axis=1
    )
    flat_slot = owner_device * slot_count + block_place - first_position[owner_device]
    target_device = targets // slot_count
    target_slot = targets % slot_count
    is_live = target_slot < block_count[target_device]
    block_index = block_at_position[
        jnp.clip(first_position[target_device] + target_slot, 0, block_total - 1)
    ]
    neighbour = face_links[block_index]
    source_slot = jnp.where(neighbour >= 0, flat_slot[jnp.clip(neighbour, 0, block_total - 1)], -1)
    column = jnp.arange(width, dtype=jnp.int32)
    flipped = face_flip[block_index][:, :, None]
    ordered = jnp.where(flipped == 1, width - 1 - column, column)
    column_index = (face_offset[block_index][:, :, None] + ordered) % width
    return (is_live, source_slot, column_index)


def attach_halos(blocks, lower, upper, source_slot):
    cells_i = blocks.shape[2]
    lower = jnp.where(
        (source_slot[:, 0] >= 0)[None, :, None, None],
        lower,
        jnp.repeat(blocks[:, :, 0:1], 2, axis=2),
    )
    upper = jnp.where(
        (source_slot[:, 1] >= 0)[None, :, None, None],
        upper,
        jnp.repeat(blocks[:, :, cells_i - 1 : cells_i], 2, axis=2),
    )
    return jnp.concatenate([lower, blocks, upper], axis=2)


def fluxes(conserved):
    inverse_rho = 1.0 / conserved[0]
    velocity_i = conserved[1] * inverse_rho
    velocity_j = conserved[2] * inverse_rho
    pressure = (HEAT_RATIO - 1.0) * (
        conserved[4]
        - 0.5
        * (conserved[1] * conserved[1] + conserved[2] * conserved[2] + conserved[3] * conserved[3])
        * inverse_rho
    )
    flux_i = jnp.stack(
        [
            conserved[1],
            conserved[1] * velocity_i + pressure,
            conserved[2] * velocity_i,
            conserved[3] * velocity_i,
            (conserved[4] + pressure) * velocity_i,
            conserved[5] * velocity_i,
        ]
    )
    flux_j = jnp.stack(
        [
            conserved[2],
            conserved[1] * velocity_j,
            conserved[2] * velocity_j + pressure,
            conserved[3] * velocity_j,
            (conserved[4] + pressure) * velocity_j,
            conserved[5] * velocity_j,
        ]
    )
    return (flux_i, flux_j, jnp.abs(velocity_i), jnp.abs(velocity_j))


def advance(extended, volumes, spectral, omega_value, instance_total):
    cells_i = extended.shape[2] - 4
    flux_i, flux_j, speed_i, speed_j = fluxes(extended)
    left_cell = extended[:, :, 1 : cells_i + 2]
    right_cell = extended[:, :, 2 : cells_i + 3]
    back_cell = extended[:, :, 0 : cells_i + 1]
    ahead_cell = extended[:, :, 3 : cells_i + 4]
    radius_i = 0.5 * (speed_i[:, 1 : cells_i + 2] + speed_i[:, 2 : cells_i + 3]) + SOUND_SPEED
    face_i = 0.5 * (flux_i[:, :, 1 : cells_i + 2] + flux_i[:, :, 2 : cells_i + 3]) - radius_i * (
        SECOND_DISSIPATION * (right_cell - left_cell)
        - FOURTH_DISSIPATION * (ahead_cell - 3.0 * right_cell + 3.0 * left_cell - back_cell)
    )
    centre = extended[:, :, 2 : cells_i + 2]
    centre_flux = flux_j[:, :, 2 : cells_i + 2]
    centre_speed = speed_j[:, 2 : cells_i + 2]
    next_cell = jnp.roll(centre, -1, axis=-1)
    prior_cell = jnp.roll(centre, 1, axis=-1)
    far_cell = jnp.roll(centre, -2, axis=-1)
    radius_j = 0.5 * (centre_speed + jnp.roll(centre_speed, -1, axis=-1)) + SOUND_SPEED
    face_j = 0.5 * (centre_flux + jnp.roll(centre_flux, -1, axis=-1)) - radius_j * (
        SECOND_DISSIPATION * (next_cell - centre)
        - FOURTH_DISSIPATION * (far_cell - 3.0 * next_cell + 3.0 * centre - prior_cell)
    )
    residual_sum = (
        face_i[:, :, 1:]
        - face_i[:, :, :-1]
        + (face_j - jnp.roll(face_j, 1, axis=-1))
        + volumes * spectral
    )
    step_rate = COURANT / (
        speed_i[:, 2 : cells_i + 2]
        + centre_speed
        + 2.0 * SOUND_SPEED
        + volumes * omega_value * 0.5 * instance_total
    )
    return (centre - step_rate * residual_sum, residual_sum / volumes)


def select_faces(selector, slabs):
    return jnp.einsum("tf,lcfxw->lctxw", selector, slabs, precision=lax.Precision.HIGHEST)


def orient_faces(slabs, permuter):
    return jnp.einsum("lctxw,tvw->lctxv", slabs, permuter, precision=lax.Precision.HIGHEST)


def on_device(
    flow_state, cell_volume, frequency, block_count, block_place, face_links, face_offset, face_flip
):
    local_count, comps, row_count, width = flow_state.shape
    slot_count = BLOCKS_MAX
    cells_i = row_count // slot_count
    space_total = lax.axis_size("space")
    space_index = lax.axis_index("space")
    targets = space_index * slot_count + jnp.arange(slot_count, dtype=jnp.int32)
    is_live, source_slot, column_index = block_tables(
        block_count, block_place, face_links, face_offset, face_flip, targets, slot_count, width
    )
    column = jnp.arange(width, dtype=jnp.int32)
    permuter = (
        column_index.reshape(slot_count * 2, width)[:, :, None] == column[None, None, :]
    ).astype(jnp.float32)
    side_index = jnp.arange(2, dtype=jnp.int32)[None, :]
    volumes = cell_volume.reshape(slot_count, cells_i, width)
    instance_total = local_count * lax.axis_size("inst")
    matrix = spectral_matrix(instance_total, frequency[0])
    row_offset = lax.axis_index("inst") * local_count
    own_rows = lax.dynamic_slice_in_dim(matrix, row_offset, local_count, 0)
    wanted_face = (source_slot * 2 + (1 - side_index)).reshape(-1)
    face_range = jnp.arange(space_total * slot_count * 2, dtype=jnp.int32)
    selector = (
        (wanted_face[:, None] == face_range[None, :]) & (source_slot.reshape(-1)[:, None] >= 0)
    ).astype(jnp.float32)
    current = flow_state
    last_residual = jnp.zeros_like(flow_state)
    for iteration in range(PSEUDO_STEPS):
        spectral_all = jnp.einsum(
            "nm,mcrb->ncrb",
            own_rows,
            lax.all_gather(current, "inst", axis=0, tiled=True),
            precision=lax.Precision.HIGHEST,
        )
        blocks = current.reshape(local_count, comps, slot_count, cells_i, width)
        faces = jnp.stack([blocks[:, :, :, 0:2], blocks[:, :, :, cells_i - 2 : cells_i]], axis=3)
        gathered = lax.all_gather(faces, "space", axis=2, tiled=True)
        gathered = gathered.reshape(local_count, comps, space_total * slot_count * 2, 2, width)
        arrived = select_faces(selector, gathered)
        oriented = orient_faces(arrived, permuter).reshape(
            local_count, comps, slot_count, 2, 2, width
        )

        def one_instance(own_blocks, slabs, spectral):
            extended = attach_halos(own_blocks, slabs[:, :, 0], slabs[:, :, 1], source_slot)
            return advance(
                extended,
                volumes,
                spectral.reshape(comps, slot_count, cells_i, width),
                frequency[0],
                instance_total,
            )

        updated, residual_now = jax.vmap(one_instance)(blocks, oriented, spectral_all)
        current = updated.reshape(flow_state.shape)
        last_residual = residual_now.reshape(flow_state.shape)
    row_live = jnp.repeat(is_live, cells_i)[None, None, :, None]
    return (jnp.where(row_live, current, 0.0), jnp.where(row_live, last_residual, 0.0))


def solution(mesh):
    return jax.shard_map(
        on_device,
        mesh=mesh,
        in_specs=(
            P(("groups", "inst"), None, "space", None),
            P(("groups", "space"), None),
            P(),
            P("groups"),
            P("groups"),
            P("groups", None),
            P("groups", None),
            P("groups", None),
        ),
        out_specs=(
            P(("groups", "inst"), None, "space", None),
            P(("groups", "inst"), None, "space", None),
        ),
        check_vma=False,
    )
```

profile of v0, /device:TPU:0, one launch (start us, length us, event | category | flops | bytes accessed | tf_op | source)
XLA Modules:
  0.0 100.8 jit_solution(13076670336360152138)
XLA Ops:
  7.2 0.7 all-gather.3.cloned.1.call-update
  8.0 1.0 slice_bitcast_fusion.8
  8.9 1.1 %fusion.121 = (f32[1,6,4,1,256]{4,3,2,0,1:T(1,128)S(1)}, f32[1,6,4,1,256]{4,3,2,0,1:T(1,128)S(1)}) fusion(f32[1,6,4,16,256]{4,3,2,0,1:T(8,128)} %bitcast.267), kind=kLoop, calls=%fused_computation.266 | loop fusion | bytes 98304 | tf_op jit(solution)/shard_map/vmap()/slice | solution.py:74
  10.0 0.1 fusion.100
  10.1 0.8 reduce-window.9
  11.0 0.7 bitcast_subtract_fusion
  11.7 0.7 convert_reduce_fusion
  12.5 0.6 gather_fusion.1
  13.1 0.1 copy.178
  13.2 0.1 fusion.101
  13.3 0.6 gather_fusion.4
  14.0 0.6 scatter_custom_fusion
  14.6 0.6 gather_fusion.2
  15.3 0.1 copy.179
  15.4 0.1 fusion.96
  15.6 0.6 gather_fusion.3
  16.1 0.1 copy.183
  16.2 0.1 copy.184
  16.4 0.6 gather_fusion.5
  17.2 0.2 fusion.104
  17.6 16.2 %all_gather.12 = f32[1,6,16,2,2,256]{5,4,2,1,3,0:T(2,128)S(1)} all-gather(f32[1,6,4,2,2,256]{5,4,2,1,3,0:T(2,128)S(1)} %pad_maximum_fusion.8), channel_id=1, replica_groups=mesh['groups'=2,'inst'=4,'space'=4] {'space'}, dimensions={2}, use_global_device_ids=true | all-gather | bytes 491520 | tf_op jit(solution)/shard_map/all_gather | solution.py:196
  33.9 0.3 copy.188
  34.2 0.3 reshape.1171
  34.5 0.6 gather_fusion.7
  35.3 0.6 gather_fusion.6
  35.9 0.3 convolution_bitcast_fusion.1
  36.3 1.3 %fusion.3 = f32[8,256,6,2]{1,2,3,0:T(8,128)S(1)} fusion(s32[8,256]{1,0:T(8,128)S(1)} %add_select_fusion, f32[6,8,2,256]{3,1,2,0:T(8,128)S(1)} %convolution_bitcast_fusion.1), kind=kOutput, calls=%fused_computation.12 | convolution fusion | flops 76021760 | bytes 204800 | tf_op jit(solution)/shard_map/lctxw,tvw->lctxv/dot_general | solution.py:155
  37.6 0.1 fusion.82
  37.7 0.1 fusion.83
  37.8 0.1 pad_maximum_fusion.4
  39.1 0.2 slice.427
  39.3 0.2 copy-done
  39.5 0.6 gather_fusion
  40.2 0.1 fusion.120
  40.3 0.2 slice_bitcast_fusion.2
  40.5 0.2 fusion.119
  40.7 0.4 fusion.38
  41.1 0.1 slice.431
  41.3 0.1 broadcast_in_dim.107
  41.5 0.5 fusion.26
  42.0 4.9 %fusion.7 = f32[1,6,4,16,256]{4,0,3,2,1:T(1,128)S(1)} fusion(f32[6,4,16,256,4]{3,2,1,0,4:T(8,128)} %bitcast.279, f32[4,4]{1,0:T(4,128)S(1)} %subtract_multiply_fusion.2, s32[]{:T(128)S(6)} %select_n.225), kind=kOutput, calls=%fused_computation.15 | convolution fusion | flops 4718592 | bytes 1966596 | tf_op jit(solution)/shard_map/nm,mcrb->ncrb/dot_general | solution.py:188
  47.0 0.2 fusion.42
  47.3 15.6 %all_gather.14 = f32[1,6,16,2,2,256]{5,4,2,1,3,0:T(2,128)S(1)} all-gather(f32[1,6,4,2,2,256]{5,4,2,1,3,0:T(2,128)S(1)} %pad_maximum_fusion.9), channel_id=1, replica_groups=mesh['groups'=2,'inst'=4,'space'=4] {'space'}, dimensions={2}, use_global_device_ids=true | all-gather | bytes 491520 | tf_op jit(solution)/shard_map/all_gather | solution.py:196
  63.0 0.3 copy.200
  63.3 0.3 reshape.1177
  63.6 0.3 convolution_bitcast_fusion
  63.8 1.3 %fusion.1 = f32[8,256,6,2]{1,2,3,0:T(8,128)S(1)} fusion(s32[8,256]{1,0:T(8,128)S(1)} %add_select_fusion, f32[6,8,2,256]{3,1,2,0:T(8,128)S(1)} %convolution_bitcast_fusion), kind=kOutput, calls=%fused_computation.11 | convolution fusion | flops 76021760 | bytes 204800 | tf_op jit(solution)/shard_map/lctxw,tvw->lctxv/dot_general | solution.py:155
  65.2 0.1 fusion.81
  65.3 0.1 fusion.80
  65.4 0.1 pad_maximum_fusion.5
  65.5 0.7 slice.460
  66.3 0.6 slice.461
  66.9 0.2 slice.464
  67.3 1.0 fusion.69
  68.3 0.1 fusion.117
  68.5 0.2 slice_bitcast_fusion
  68.6 0.2 fusion.116
  68.8 0.4 fusion.33
  69.2 0.1 slice.468
  69.4 0.5 fusion.16
  69.9 17.8 %all-gather.5.cloned.1.call-done = f32[4,6,64,256]{3,2,1,0:T(8,128)} async-done(((f32[1,6,64,256]{3,2,1,0:T(8,128)}), f32[4,6,64,256]{3,2,1,0:T(8,128)}) %all-gather.5.cloned.1.call-update) | async-done | bytes 1572880 | tf_op jit(solution)/shard_map/all_gather | solution.py:191
  87.7 4.9 %fusion.5 = f32[1,6,4,16,256]{4,0,3,2,1:T(1,128)S(1)} fusion(f32[6,4,16,256,4]{3,2,1,0,4:T(8,128)} %bitcast.280, f32[4,4]{1,0:T(4,128)S(1)} %subtract_multiply_fusion.2, s32[]{:T(128)S(6)} %select_n.225), kind=kOutput, calls=%fused_computation.13 | convolution fusion | flops 4718592 | bytes 1966596 | tf_op jit(solution)/shard_map/nm,mcrb->ncrb/dot_general | solution.py:188
  92.6 0.2 broadcast_divide_fusion
  93.0 1.0 %bitcast_select_fusion = (f32[1,6,64,256]{3,2,1,0:T(8,128)}, f32[1,6,64,256]{3,2,1,0:T(8,128)}) fusion(f32[1,6,4,16,256]{4,3,2,1,0:T(8,128)S(1)} %get-tuple-element.4, pred[64]{0:T(512)(128)(4,1)S(1)} %broadcast_in_dim.107, f32[1,6,4,16,256]{4,3,2,1,0:T(8,128)S(1)} %multiply_subtract_fusion), kind=kLoop, calls=%fused_computation.89 | loop fusion | flops 196608 | bytes 1572928 | tf_op jit(solution)/shard_map/jit(_where)/select_n | solution.py:217
  (89 shorter events, 2.4 us)
Async XLA Ops:
  7.2 6.8 %copy-start.8 = (s32[8]{0:T(128)S(1)}, s32[8]{0:T(128)}, u32[]{:S(2)}) copy-start(s32[8]{0:T(128)} %param.12) | copy-start | bytes 100
  7.2 8.3 %copy-start.5 = (s32[8,2]{0,1:T(2,128)S(1)}, s32[8,2]{0,1:T(2,128)}, u32[]{:S(2)}) copy-start(s32[8,2]{0,1:T(2,128)} %param.13) | copy-start | bytes 196
  7.2 34.8 %all-gather.3.cloned.1.call-start = ((), (), s32[]{:S(2)}) async-start(), calls=%async_computation | async-start | bytes 1966080 | tf_op jit(solution)/shard_map/all_gather | solution.py:191
  7.9 79.8 %all-gather.5.cloned.1.call-start = ((), (), s32[]{:S(2)}) async-start(), calls=%async_computation.1 | async-start | bytes 1966080 | tf_op jit(solution)/shard_map/all_gather | solution.py:191
  13.3 4.2 %copy-start.3 = (f32[1,6,64,256]{3,2,1,0:T(8,128)S(1)}, f32[1,6,64,256]{3,2,1,0:T(8,128)}, u32[]{:S(2)}) copy-start(f32[1,6,64,256]{3,2,1,0:T(8,128)} %param.8) | copy-start | bytes 1179652
  17.1 17.4 %copy-start.6 = (s32[8,2]{0,1:T(2,128)S(1)}, s32[8,2]{0,1:T(2,128)}, u32[]{:S(2)}) copy-start(s32[8,2]{0,1:T(2,128)} %param.15) | copy-start | bytes 196
  17.1 18.1 %copy-start.7 = (s32[8,2]{0,1:T(2,128)S(1)}, s32[8,2]{0,1:T(2,128)}, u32[]{:S(2)}) copy-start(s32[8,2]{0,1:T(2,128)} %param.14) | copy-start | bytes 196
  37.9 1.0 copy-start.4
  38.8 0.7 copy-start
  47.2 19.8 %copy-start.1 = (f32[1,6,4,16,256]{4,3,2,1,0:T(8,128)}, f32[1,6,4,16,256]{4,3,2,1,0:T(8,128)S(1)}, u32[]{:S(2)}) copy-start(f32[1,6,4,16,256]{4,3,2,1,0:T(8,128)S(1)} %fusion.42) | copy-start | bytes 1179652
  67.2 1.2 %copy-start.2 = (f32[1,6,4,16,256]{4,3,2,1,0:T(8,128)S(1)}, f32[1,6,4,16,256]{4,3,2,1,0:T(8,128)}, u32[]{:S(2)}) copy-start(f32[1,6,4,16,256]{4,3,2,1,0:T(8,128)} %copy-done.1) | copy-start | bytes 1179652
Sparse Core Ops, SparseCore 0:
  9.6 22.3 all-gather.2
  67.4 20.3 all-gather.4
where the time goes:
time: 101 us
  blocking collectives  31.9 us (32%)
  waiting for transfers between devices  18.5 us (18%)
  between operations  15.3 us (15%)
  local copies, waits for them, and re-layouts  13.4 us (13%)
  matrix products  12.9 us (13%)
  other arithmetic  8.66 us (9%)
    all_gather x2, blocking collectives, on_device(): gathered = lax.all_gather(faces, 'space', axis=2, tiled=True)  31.9 us
    all_gather x2, waiting for transfers between devices, on_device(): lax.all_gather(current, 'inst', axis=0, tiled=True)  17.8 us
    dot_general x2, matrix products, on_device(): jnp.einsum('nm,mcrb->ncrb', own_rows, lax.all_gather(current, 'inst', axi...  9.82 us
    dot_general x2, matrix products, orient_faces(): jnp.einsum('lctxw,tvw->lctxv', slabs, permuter, precision=lax.Precision.H...  2.6 us
  transfers between devices with their start and end apart: 2, of which 1 were waited for; matrix products, arithmetic and copies ran while one was open for 19% of the time, Pallas kernels for 0%

commit v1 on v0

--- a/solution.py
+++ b/solution.py
@@ -1,6 +1,11 @@
+import functools
+import math
+
 import jax
 import jax.numpy as jnp
 from jax import lax
+from jax.experimental import pallas as pl
+from jax.experimental.pallas import tpu as pltpu
 from jax.sharding import PartitionSpec as P
 
 BLOCKS_MAX = 4
@@ -13,6 +18,476 @@
 SOUND_SPEED = 1.0
 COURANT = 0.5
 TIME_VISCOSITY = 0.25
+
+COMPS = 6
+FACES = 2 * BLOCKS_MAX
+F32 = jnp.float32
+VMEM = pl.BlockSpec(memory_space=pltpu.VMEM)
+SMEM = pl.BlockSpec(memory_space=pltpu.SMEM)
+
+
+def spectral_weights(total):
+    weights = [TIME_VISCOSITY * (total * total + 2) / 12.0]
+    for k in range(1, total):
+        sign = 1.0 - 2.0 * (k % 2)
+        angle = math.pi * k / total
+        first = 0.5 * sign * math.cos(angle) / math.sin(angle)
+        second = -sign / (2.0 * math.sin(angle) ** 2)
+        weights.append(first - TIME_VISCOSITY * second)
+    return weights
+
+
+def pair_cap(space_total, block_total):
+    second_most = min(BLOCKS_MAX, block_total - BLOCKS_MAX - (space_total - 2))
+    return 2 * max(1, second_most)
+
+
+def primitives(q):
+    inverse = 1.0 / q[0]
+    u = q[1] * inverse
+    v = q[2] * inverse
+    p = (HEAT_RATIO - 1.0) * (
+        q[4] - 0.5 * (q[1] * q[1] + q[2] * q[2] + q[3] * q[3]) * inverse
+    )
+    return u, v, p
+
+
+def flux_along_i(q, u, p):
+    return [q[1], q[1] * u + p, q[2] * u, q[3] * u, (q[4] + p) * u, q[5] * u]
+
+
+def flux_along_j(q, v, p):
+    return [q[2], q[1] * v, q[2] * v + p, q[3] * v, (q[4] + p) * v, q[5] * v]
+
+
+def ahead(x):
+    return pltpu.roll(x, x.shape[1] - 1, axis=1)
+
+
+def behind(x):
+    return pltpu.roll(x, 1, axis=1)
+
+
+DIFF_ONE = SECOND_DISSIPATION + 2.0 * FOURTH_DISSIPATION
+
+
+def residual_j(q, v, p):
+    speed = jnp.abs(v)
+    radius = 0.5 * (speed + ahead(speed)) + SOUND_SPEED
+    out = []
+    for q_c, g_c in zip(q, flux_along_j(q, v, p)):
+        step = ahead(q_c) - q_c
+        damping = DIFF_ONE * step - FOURTH_DISSIPATION * (ahead(step) + behind(step))
+        face = 0.5 * (g_c + ahead(g_c)) - radius * damping
+        out.append(face - behind(face))
+    return out
+
+
+class Rows:
+    def __init__(self, load):
+        self.load = load
+        self.state, self.prim, self.flux, self.steps, self.faces = {}, {}, {}, {}, {}
+
+    def q(self, r):
+        if r not in self.state:
+            self.state[r] = self.load(r)
+        return self.state[r]
+
+    def uvp(self, r):
+        if r not in self.prim:
+            self.prim[r] = primitives(self.q(r))
+        return self.prim[r]
+
+    def f(self, r):
+        if r not in self.flux:
+            u, _, p = self.uvp(r)
+            self.flux[r] = flux_along_i(self.q(r), u, p)
+        return self.flux[r]
+
+    def step(self, r):
+        if r not in self.steps:
+            self.steps[r] = [b - a for a, b in zip(self.q(r), self.q(r + 1))]
+        return self.steps[r]
+
+    def face(self, r):
+        if r not in self.faces:
+            radius = 0.5 * (jnp.abs(self.uvp(r)[0]) + jnp.abs(self.uvp(r + 1)[0])) + SOUND_SPEED
+            out = []
+            for c in range(COMPS):
+                damping = DIFF_ONE * self.step(r)[c] - FOURTH_DISSIPATION * (
+                    self.step(r + 1)[c] + self.step(r - 1)[c]
+                )
+                out.append(0.5 * (self.f(r)[c] + self.f(r + 1)[c]) - radius * damping)
+            self.faces[r] = out
+        return self.faces[r]
+
+    def residual(self, r):
+        u, v, p = self.uvp(r)
+        lower, upper = self.face(r - 1), self.face(r)
+        across = residual_j(self.q(r), v, p)
+        total = [(b - a) + j for a, b, j in zip(lower, upper, across)]
+        return total, jnp.abs(u) + jnp.abs(v)
+
+
+def even_tiles(shape):
+    return lax.broadcasted_iota(jnp.int32, shape, 0) % 2 == 0
+
+
+def row_loader(load, halo_ref):
+    def extended(r):
+        out = []
+        for c in range(COMPS):
+            if r < 0:
+                inner = pltpu.roll(load(c, r + 8), 1, axis=0)
+                out.append(jnp.where(even_tiles(inner.shape), halo_ref[c, r + 2], inner))
+            elif r > 7:
+                inner = pltpu.roll(load(c, r - 8), 7, axis=0)
+                out.append(jnp.where(even_tiles(inner.shape), inner, halo_ref[c, r - 8]))
+            else:
+                out.append(load(c, r))
+        return out
+
+    return extended
+
+
+def split_parts(parts_ref, rest_ref):
+    def load(c, r):
+        if 2 <= r <= 5:
+            return rest_ref[c, r]
+        layer = r % 2
+        outer, other = parts_ref[c, layer], rest_ref[c, layer]
+        even = even_tiles(outer.shape)
+        if r < 2:
+            return jnp.where(even, outer, other)
+        return jnp.where(even, other, outer)
+
+    return load
+
+
+def coefficients(frequency_ref):
+    weights = spectral_weights(4)
+    omega = frequency_ref[0]
+    even = lax.axis_index("inst") % 2 == 0
+    near = omega * jnp.where(even, F32(weights[3]), F32(weights[1]))
+    far = omega * jnp.where(even, F32(weights[1]), F32(weights[3]))
+    return omega, omega * F32(weights[0]), omega * F32(weights[2]), near, far
+
+
+def own_instance_rate(speeds, volume, omega):
+    return COURANT / (speeds + 2.0 * SOUND_SPEED + volume * (omega * (0.5 * 4)))
+
+
+def pack_kernel(
+    space_total, block_total, cap,
+    state_ref, volume_ref, counts_ref, place_ref, links_ref, offset_ref, flip_ref,
+    rows_ref, vrows_ref, outer_ref, rest_ref, table_ref, index_ref, *more
+):
+    sends = more[: space_total - 1]
+    half_ref, first_ref, inverse_ref = more[space_total - 1 :]
+    width = state_ref.shape[2]
+    for c in range(COMPS + 1):
+        for h in range(2):
+            lanes = pl.ds(128 * h, 128)
+            half_ref[c, h] = state_ref[c, :, lanes] if c < COMPS else volume_ref[:, lanes]
+    for c in range(COMPS + 1):
+        for r in range(8):
+            for h in range(2):
+                row = half_ref[c, h, pl.ds(r, 8, stride=8), :]
+                if c < COMPS:
+                    rows_ref[c, r, :, pl.ds(128 * h, 128)] = row
+                else:
+                    vrows_ref[r, :, pl.ds(128 * h, 128)] = row
+    even = even_tiles((8, width))
+    for c in range(COMPS):
+        for l in range(2):
+            low, high = rows_ref[c, l], rows_ref[c, 6 + l]
+            outer_ref[c, l] = jnp.where(even, low, high)
+            rest_ref[c, l] = jnp.where(even, high, low)
+        for r in range(2, 6):
+            rest_ref[c, r] = rows_ref[c, r]
+    me = lax.axis_index("space")
+    total = jnp.int32(0)
+    firsts = []
+    for d in range(space_total):
+        firsts.append(total)
+        first_ref[d] = total
+        total = total + counts_ref[d]
+    for b in range(block_total):
+        inverse_ref[place_ref[b]] = jnp.int32(b)
+
+    def block_in(device, slot):
+        return inverse_ref[jnp.minimum(first_ref[device] + slot, block_total - 1)]
+
+    def source_of(block, side):
+        link = links_ref[block, side]
+        place = place_ref[jnp.maximum(link, 0)]
+        owner = jnp.int32(0)
+        first = jnp.int32(0)
+        for d in range(1, space_total):
+            past = place >= firsts[d]
+            owner = jnp.where(past, d, owner)
+            first = jnp.where(past, firsts[d], first)
+        return link, owner, 2 * (place - first) + (1 - side)
+
+    own_base = (space_total - 1) * COMPS * 2 * cap
+    few = 2 * counts_ref[me] <= cap
+    tile = lax.broadcasted_iota(jnp.int32, (FACES, width), 0)
+    start = jnp.zeros((FACES, width), jnp.int32)
+    turned = jnp.zeros((FACES, width), jnp.int32)
+    for f in range(FACES):
+        slot, side = f // 2, f % 2
+        block = block_in(me, slot)
+        link, owner, source = source_of(block, side)
+        shift = lax.rem(me - owner + space_total, space_total)
+        listed = 2 * counts_ref[owner] <= cap
+        place = jnp.where(listed, jnp.minimum(source, cap - 1), min(f, cap - 1))
+        outside = link < 0
+        mine = owner == me
+        base = jnp.where(mine, own_base + source, (shift - 1) * (COMPS * 2 * cap) + place)
+        base = jnp.where(outside, own_base + 8 * side + f, base)
+        table_ref[f] = base
+        table_ref[FACES + f] = jnp.where(outside | mine, 2 * FACES, 2 * cap)
+        table_ref[2 * FACES + f] = jnp.where(outside, 0, jnp.where(mine, FACES, cap))
+        start = jnp.where(tile == f, jnp.where(outside, 0, offset_ref[block, side]), start)
+        turned = jnp.where(tile == f, jnp.where(outside, 0, flip_ref[block, side]), turned)
+    column = lax.broadcasted_iota(jnp.int32, (FACES, width), 1)
+    index_ref[...] = (start + jnp.where(turned == 1, width - 1 - column, column)) % width
+    for k in range(1, space_total):
+        target = lax.rem(me + k, space_total)
+        for i in range(cap):
+            _, owner, source = source_of(block_in(target, i // 2), i % 2)
+            wanted = jnp.where(owner == me, source, 0)
+            table_ref[3 * FACES + (k - 1) * cap + i] = jnp.where(few, i, wanted)
+    pack_sends(cap, outer_ref, table_ref, sends)
+
+
+def pack_sends(cap, outer_ref, table_ref, sends):
+    for k, send_ref in enumerate(sends):
+        for i in range(cap):
+            f = table_ref[3 * FACES + k * cap + i]
+            for c in range(COMPS):
+                for l in range(2):
+                    send_ref[pl.ds((2 * c + l) * cap + i, 1), :] = outer_ref[c, l, pl.ds(f, 1), :]
+
+
+def halo_kernel(space_total, cap, table_ref, index_ref, outer_ref, *more):
+    received = more[: space_total - 1]
+    halo_ref, pool_ref, raw_ref = more[space_total - 1 :]
+    size = COMPS * 2 * cap
+    for k, part in enumerate(received):
+        pool_ref[pl.ds(k * size, size), :] = part[...]
+    own_base = (space_total - 1) * size
+    for c in range(COMPS):
+        for l in range(2):
+            pool_ref[pl.ds(own_base + (2 * c + l) * FACES, FACES), :] = outer_ref[c, l]
+    for f in range(FACES):
+        base, per_comp, per_layer = table_ref[f], table_ref[FACES + f], table_ref[2 * FACES + f]
+        for c in range(COMPS):
+            for l in range(2):
+                row = base + c * per_comp + l * per_layer
+                raw_ref[c, l, pl.ds(f, 1), :] = pool_ref[pl.ds(row, 1), :]
+    width = index_ref.shape[1]
+    masks, lanes = [], []
+    for h in range(width // 128):
+        index = index_ref[:, pl.ds(128 * h, 128)]
+        lanes.append(index & 127)
+        masks.append(index < 128)
+    for c in range(COMPS):
+        for l in range(2):
+            low, high = raw_ref[c, l, :, pl.ds(0, 128)], raw_ref[c, l, :, pl.ds(128, 128)]
+            for h in range(2):
+                a = jnp.take_along_axis(low, lanes[h], axis=1)
+                b = jnp.take_along_axis(high, lanes[h], axis=1)
+                halo_ref[c, l, :, pl.ds(128 * h, 128)] = jnp.where(masks[h], a, b)
+
+
+def outer_kernel(
+    cap, table_ref, frequency_ref, rows_ref, vrows_ref, halo_ref, across_ref, sibling_ref,
+    sibling_across_ref, outer_ref, *sends
+):
+    omega, w_own, w_across, w_near, w_far = coefficients(frequency_ref)
+    load = row_loader(lambda c, r: rows_ref[c, r], halo_ref)
+    even = even_tiles(vrows_ref.shape[1:])
+    low = {r: load(r) for r in range(-2, 4)}
+    high = {r: load(r) for r in range(4, 10)}
+    picked = {
+        k: [jnp.where(even, a, b) for a, b in zip(low[k - 2], high[k + 4])] for k in range(6)
+    }
+    rows = Rows(lambda k: picked[k])
+    for l in range(2):
+        flux, speeds = rows.residual(l + 2)
+        volume = jnp.where(even, vrows_ref[l], vrows_ref[l + 6])
+        rate = own_instance_rate(speeds, volume, omega)
+        for c in range(COMPS):
+            own = picked[l + 2][c]
+            sibling = jnp.where(even, sibling_ref[c, l], sibling_ref[c, l + 6])
+            spectral = (
+                w_own * own + w_across * across_ref[c, l]
+                + w_near * sibling + w_far * sibling_across_ref[c, l]
+            )
+            outer_ref[c, l] = own - rate * (flux[c] + volume * spectral)
+    pack_sends(cap, outer_ref, table_ref, sends)
+
+
+def first_kernel(
+    frequency_ref, rows_ref, vrows_ref, halo_ref, across_halo_ref, across_outer_ref,
+    across_rest_ref, sibling_ref, sib_across_outer_ref, sib_across_rest_ref,
+    next_ref, partial_ref, send_ref
+):
+    omega, w_own, w_across, w_near, w_far = coefficients(frequency_ref)
+    own_load = lambda c, r: rows_ref[c, r]
+    across_load = split_parts(across_outer_ref, across_rest_ref)
+    far_load = split_parts(sib_across_outer_ref, sib_across_rest_ref)
+    own = Rows(row_loader(own_load, halo_ref))
+    across = Rows(row_loader(across_load, across_halo_ref))
+    for r in range(8):
+        volume = vrows_ref[r]
+        own_flux, own_speeds = own.residual(r)
+        own_rate = own_instance_rate(own_speeds, volume, omega)
+        across_flux, across_speeds = across.residual(r)
+        across_rate = own_instance_rate(across_speeds, volume, omega)
+        for c in range(COMPS):
+            mine, other = own.q(r)[c], across.q(r)[c]
+            near, far = sibling_ref[c, r], far_load(c, r)
+            spectral = w_own * mine + w_across * other + w_near * near + w_far * far
+            mine_next = mine - own_rate * (own_flux[c] + volume * spectral)
+            spectral = w_own * other + w_across * mine + w_far * near + w_near * far
+            other_next = other - across_rate * (across_flux[c] + volume * spectral)
+            next_ref[c, r] = mine_next
+            partial_ref[c, r] = w_own * mine_next + w_across * other_next
+            send_ref[c, r] = w_far * mine_next + w_near * other_next
+
+
+def last_kernel(
+    frequency_ref, counts_ref, rows_ref, vrows_ref, halo_ref, partial_ref, received_ref,
+    new_ref, residual_ref, new_half_ref, residual_half_ref
+):
+    omega = frequency_ref[0]
+    own = Rows(row_loader(lambda c, r: rows_ref[c, r], halo_ref))
+    live = (lax.broadcasted_iota(jnp.int32, vrows_ref.shape[1:], 0) // 2) < counts_ref[
+        lax.axis_index("space")
+    ]
+    for r in range(8):
+        volume = vrows_ref[r]
+        flux, speeds = own.residual(r)
+        rate = own_instance_rate(speeds, volume, omega)
+        inverse = 1.0 / volume
+        for c in range(COMPS):
+            residual = flux[c] + volume * (partial_ref[c, r] + received_ref[c, r])
+            new = jnp.where(live, own.q(r)[c] - rate * residual, 0.0)
+            scaled = jnp.where(live, residual * inverse, 0.0)
+            for h in range(2):
+                lanes = slice(128 * h, 128 * h + 128)
+                new_half_ref[c, h, pl.ds(r, 8, stride=8), :] = new[:, lanes]
+                residual_half_ref[c, h, pl.ds(r, 8, stride=8), :] = scaled[:, lanes]
+    for c in range(COMPS):
+        for h in range(2):
+            new_ref[c, :, pl.ds(128 * h, 128)] = new_half_ref[c, h]
+            residual_ref[c, :, pl.ds(128 * h, 128)] = residual_half_ref[c, h]
+
+
+def hold(x):
+    return pltpu.with_memory_space_constraint(x, pltpu.VMEM)
+
+
+def four_instances(
+    flow_state, cell_volume, frequency, block_count, block_place, face_links, face_offset, face_flip
+):
+    _, comps, row_count, width = flow_state.shape
+    space_total = lax.axis_size("space")
+    block_total = block_place.shape[0]
+    cap = pair_cap(space_total, block_total)
+    state = flow_state[0]
+
+    def over_inst(x, flip):
+        return lax.ppermute(x, "inst", [(i, i ^ flip) for i in range(4)])
+
+    def over_space(parts):
+        return [
+            lax.ppermute(x, "space", [(i, (i + k + 1) % space_total) for i in range(space_total)])
+            for k, x in enumerate(parts)
+        ]
+
+    full = (comps, 8, 8, width)
+    outer = (comps, 2, 8, width)
+    pair = (comps * 2 * cap, width)
+    entries = 3 * FACES + (space_total - 1) * cap
+    on_chip = lambda shape, dtype=F32: pltpu.VMEM(shape, dtype)
+    sends_shape = [on_chip(pair) for _ in range(space_total - 1)]
+
+    packed = pl.pallas_call(
+        functools.partial(pack_kernel, space_total, block_total, cap),
+        out_shape=[
+            on_chip(full), on_chip((8, 8, width)), on_chip(outer), on_chip((comps, 6, 8, width)),
+            pltpu.SMEM((entries,), jnp.int32), on_chip((FACES, width), jnp.int32), *sends_shape,
+        ],
+        in_specs=[VMEM, VMEM] + [SMEM] * 5,
+        out_specs=[VMEM] * 4 + [SMEM, VMEM] + [VMEM] * (space_total - 1),
+        scratch_shapes=[
+            pltpu.VMEM((comps + 1, 2, row_count, 128), F32),
+            pltpu.SMEM((space_total,), jnp.int32),
+            pltpu.SMEM((block_total,), jnp.int32),
+        ],
+    )(hold(state), hold(cell_volume), block_count, block_place, face_links, face_offset, face_flip)
+    rows, vrows, outer_rows, rest, table, index = packed[:6]
+    sends = packed[6:]
+    in_smem = lambda x: pltpu.with_memory_space_constraint(x, pltpu.SMEM)
+    table = in_smem(table)
+
+    def halos(outer_own, received):
+        return pl.pallas_call(
+            functools.partial(halo_kernel, space_total, cap),
+            out_shape=on_chip(outer),
+            in_specs=[SMEM] + [VMEM] * (2 + len(received)),
+            out_specs=VMEM,
+            scratch_shapes=[
+                pltpu.VMEM(((space_total - 1) * pair[0] + comps * 2 * FACES, width), F32),
+                pltpu.VMEM(outer, F32),
+            ],
+        )(table, hold(index), hold(outer_own), *[hold(x) for x in received])
+
+    across_outer = over_inst(outer_rows, 2)
+    across_rest = over_inst(rest, 2)
+    sibling = over_inst(rows, 1)
+    halo = halos(outer_rows, over_space(sends))
+    sib_across_outer = over_inst(across_outer, 1)
+    across_halo = over_inst(halo, 2)
+
+    produced = pl.pallas_call(
+        functools.partial(outer_kernel, cap),
+        out_shape=[on_chip(outer), *sends_shape],
+        in_specs=[SMEM, SMEM] + [VMEM] * 6,
+        out_specs=[VMEM] * space_total,
+    )(
+        table, frequency, hold(rows), hold(vrows), hold(halo), hold(across_outer), hold(sibling),
+        hold(sib_across_outer),
+    )
+    next_outer, next_sends = produced[0], produced[1:]
+    sib_across_rest = over_inst(across_rest, 1)
+    next_halo = halos(next_outer, over_space(next_sends))
+
+    next_rows, partial, to_sibling = pl.pallas_call(
+        first_kernel,
+        out_shape=[on_chip(full)] * 3,
+        in_specs=[SMEM] + [VMEM] * 9,
+        out_specs=[VMEM] * 3,
+    )(
+        frequency, hold(rows), hold(vrows), hold(halo), hold(across_halo), hold(across_outer),
+        hold(across_rest), hold(sibling), hold(sib_across_outer), hold(sib_across_rest),
+    )
+    from_sibling = over_inst(to_sibling, 1)
+
+    new, residual = pl.pallas_call(
+        last_kernel,
+        out_shape=[jax.ShapeDtypeStruct(state.shape, F32)] * 2,
+        in_specs=[SMEM, SMEM] + [VMEM] * 5,
+        out_specs=[VMEM] * 2,
+        scratch_shapes=[pltpu.VMEM((comps, 2, row_count, 128), F32)] * 2,
+    )(
+        frequency, block_count, hold(next_rows), hold(vrows), hold(next_halo), hold(partial),
+        hold(from_sibling),
+    )
+    return new[None], residual[None]
 
 
 def spectral_matrix(instance_total, omega_value):
@@ -219,7 +694,7 @@
 
 def solution(mesh):
     return jax.shard_map(
-        on_device,
+        four_instances if mesh.shape["inst"] == 4 else on_device,
         mesh=mesh,
         in_specs=(
             P(("groups", "inst"), None, "space", None),

time: 101 us -> 63.9 us (0.63)
  blocking collectives: 31.9 us -> 0 us
  Pallas kernels: 0 us -> 18.5 us
  starting transfers between devices: 0.08 us -> 16.4 us
  between operations: 15.3 us -> 1.38 us
  matrix products: 12.9 us -> 0 us
  other arithmetic: 8.66 us -> 0 us
  local copies, waits for them, and re-layouts: 13.4 us -> 10.5 us
  waiting for transfers between devices: 18.5 us -> 16.7 us
    all_gather x2 -> x0, blocking collectives: 31.9 us -> none  [on_device(): gathered = lax.all_gather(faces, 'space', axis=2, tiled=True)]
    pallas_call x0 -> x6, Pallas kernels: none -> 18.5 us  [the longest x1 10.6 us: four_instances(): pl.pallas_call(first_kernel, out_shape=[on_chip(full)] * 3, in_specs=[SME...]
    all_gather x2 -> x0, waiting for transfers between devices: 17.8 us -> none  [on_device(): lax.all_gather(current, 'inst', axis=0, tiled=True)]
    ppermute x0 -> x13, waiting for transfers between devices: none -> 16.7 us  [the longest x7 9.44 us: over_inst(): return lax.ppermute(x, 'inst', [(i, i ^ flip) for i in range(4)])]
    ppermute x0 -> x13, starting transfers between devices: none -> 16.4 us  [the longest x6 10.3 us: over_space(): lax.ppermute(x, 'space', [(i, (i + k + 1) % space_total) for i in range(s...]
    dot_general x6 -> x0, matrix products: 12.9 us -> none  [the longest x2 9.82 us: on_device(): jnp.einsum('nm,mcrb->ncrb', own_rows, lax.all_gather(current, 'inst', axi...]
    unnamed x25 -> x31, local copies, waits for them, and re-layouts: 0.56 us -> 10.5 us
    gather x11 -> x0, local copies, waits for them, and re-layouts: 5.15 us -> none  [the longest x2 0.73 us: block_tables(): block_at_position[jnp.clip(first_position[target_device] + target_slot, 0...]
  transfers between devices with their start and end apart: 2 -> 13, of which waited for: 1 -> 8; matrix products, arithmetic and copies ran while one was open for 19% -> 0% of each run, Pallas kernels for 0% -> 1%
where the time goes in v1:
time: 63.9 us; the launch traced here: 63.5 us
  Pallas kernels  18.5 us (29%)
  waiting for transfers between devices  16.7 us (26%)
  starting transfers between devices  16.4 us (26%)
  local copies, waits for them, and re-layouts  10.5 us (16%)
  between operations  1.38 us (2%)
    pallas_call x1, Pallas kernels, four_instances(): pl.pallas_call(first_kernel, out_shape=[on_chip(full)] * 3, in_specs=[SME...  10.6 us
    unnamed x31, local copies, waits for them, and re-layouts  10.5 us
    ppermute x6, starting transfers between devices, over_space(): lax.ppermute(x, 'space', [(i, (i + k + 1) % space_total) for i in range(s...  10.3 us
    ppermute x7, waiting for transfers between devices, over_inst(): return lax.ppermute(x, 'inst', [(i, i ^ flip) for i in range(4)])  9.44 us
    ppermute x6, waiting for transfers between devices, over_space(): lax.ppermute(x, 'space', [(i, (i + k + 1) % space_total) for i in range(s...  7.25 us
    ppermute x7, starting transfers between devices, over_inst(): return lax.ppermute(x, 'inst', [(i, i ^ flip) for i in range(4)])  6.04 us
    pallas_call x1, Pallas kernels, four_instances(): pl.pallas_call(last_kernel, out_shape=[jax.ShapeDtypeStruct(state.shape,...  5.7 us
    pallas_call x1, Pallas kernels, four_instances(): pl.pallas_call(functools.partial(pack_kernel, space_total, block_total, c...  1.33 us
  transfers between devices with their start and end apart: 13, of which 8 were waited for; matrix products, arithmetic and copies ran while one was open for 0% of the time, Pallas kernels for 1%

profile of v1, /device:TPU:0, one launch (start us, length us, event | category | flops | bytes accessed | tf_op | source)
XLA Modules:
  0.0 63.5 jit_solution(14954069864958186613)
XLA Ops:
  0.6 0.0 copy-start.12
  0.6 1.4 %copy.10.links_ref = s32[8,2]{1,0:T(8,128)} copy(s32[8,2]{0,1:T(2,128)} %param.13) | data formatting | bytes 128 | tf_op args[5]
  2.0 0.0 copy-done.12
  2.0 0.0 copy-start.13
  2.0 0.7 %copy.11.offset_ref = s32[8,2]{1,0:T(8,128)} copy(s32[8,2]{0,1:T(2,128)S(1)} %copy-done.12) | data formatting | bytes 128 | tf_op args[6]
  2.7 0.0 copy-done.13
  2.7 0.7 %copy.12.flip_ref = s32[8,2]{1,0:T(8,128)} copy(s32[8,2]{0,1:T(2,128)S(1)} %copy-done.13) | data formatting | bytes 128 | tf_op args[7]
  3.3 0.0 copy-start.6
  3.3 1.0 %copy-done.6 = f32[1,6,64,256]{3,2,1,0:T(8,128)S(1)} copy-done((f32[1,6,64,256]{3,2,1,0:T(8,128)S(1)}, f32[1,6,64,256]{3,2,1,0:T(8,128)}, u32[]{:S(2)}) %copy-start.6) | copy-done | bytes 393240
  4.3 0.0 copy-start.11
  4.3 0.8 %copy-done.11 = f32[64,256]{1,0:T(8,128)S(1)} copy-done((f32[64,256]{1,0:T(8,128)S(1)}, f32[64,256]{1,0:T(8,128)}, u32[]{:S(2)}) %copy-start.11) | copy-done | bytes 65560
  5.2 1.3 %shard_map.95 = (f32[6,8,8,256]{3,2,1,0:T(8,128)S(1)}, f32[8,8,256]{2,1,0:T(8,128)S(1)}, f32[6,2,8,256]{3,2,1,0:T(8,128)S(1)}, f32[6,6,8,256]{3,2,1,0:T(8,128)S(...) custom-call(f32[6,64,256]{2,1,0:T(8,128)S(1)} %bitcast.3, ...), custom_call_target="tpu_custom_call" | custom-call | tf_op jit(solution)/shard_map/pallas_call | solution.py:418
  6.5 0.0 copy-start.2
  6.5 0.6 copy-done.2
  7.1 2.9 %collective-permute-start.5 = (f32[6,6,8,256]{3,2,1,0:T(8,128)S(1)}, f32[6,6,8,256]{3,2,1,0:T(8,128)S(1)}, u32[]{:S(2)}, u32[]{:S(2)}) collective-permute-start(f32[6,6,8,256]{3,2,1,0:T(8,128)S(1)} %get-tuple-element.28), channel_id=1, source_target_pairs={{0,8},{4,12},{8,0},{12,4},{1,9},{5,13},{9,1},{13,5},{2,10},{6,14},... | collective-permute-start | bytes 884744 | tf_op jit(solution)/shard_map/ppermute | solution.py:403
  10.1 0.0 collective-permute-start.6
  10.1 7.0 %collective-permute-done.5.across_rest_ref = f32[6,6,8,256]{3,2,1,0:T(8,128)S(1)} collective-permute-done((f32[6,6,8,256]{3,2,1,0:T(8,128)S(1)}, f32[6,6,8,256]{3,2,1,0:T(8,128)S(1)}, u32[]{:S(2)}, u32[]{:S(2)}) %collective-permute-start.5) | collective-permute-done | bytes 294944 | tf_op jit(solution)/shard_map/ppermute | solution.py:403
  17.1 0.0 collective-permute-start.8
  17.1 1.8 %collective-permute-start = (f32[48,256]{1,0:T(8,128)S(1)}, f32[48,256]{1,0:T(8,128)S(1)}, u32[]{:S(2)}, u32[]{:S(2)}) collective-permute-start(f32[48,256]{1,0:T(8,128)S(1)} %get-tuple-element.25), channel_id=1, source_target_pairs={{0,1},{1,2},{2,3},{3,0},{4,5},{5,6},{6,7},{7,4},{8,9},{9,10},{10,1... | collective-permute-start | bytes 147464 | tf_op jit(solution)/shard_map/ppermute | solution.py:407
  18.9 1.5 %collective-permute-start.4 = (f32[6,2,8,256]{3,2,1,0:T(8,128)S(1)}, f32[6,2,8,256]{3,2,1,0:T(8,128)S(1)}, u32[]{:S(2)}, u32[]{:S(2)}) collective-permute-start(f32[6,2,8,256]{3,2,1,0:T(8,128)S(1)} %get-tuple-element.24.outer_ref), channel_id=1, source_target_pairs={{0,8},{4,12},{8,0},{12,4},{1,9},{5,13},{9,1},{13,5},{2,10},{6,14},... | collective-permute-start | bytes 294920 | tf_op jit(solution)/shard_map/ppermute | solution.py:403
  20.4 2.6 %collective-permute-start.1 = (f32[48,256]{1,0:T(8,128)S(1)}, f32[48,256]{1,0:T(8,128)S(1)}, u32[]{:S(2)}, u32[]{:S(2)}) collective-permute-start(f32[48,256]{1,0:T(8,128)S(1)} %get-tuple-element.26), channel_id=1, source_target_pairs={{0,2},{1,3},{2,0},{3,1},{4,6},{5,7},{6,4},{7,5},{8,10},{9,11},{10,... | collective-permute-start | bytes 147464 | tf_op jit(solution)/shard_map/ppermute | solution.py:407
  23.0 0.4 collective-permute-done.more_0_
  23.4 1.7 %collective-permute-start.2 = (f32[48,256]{1,0:T(8,128)S(1)}, f32[48,256]{1,0:T(8,128)S(1)}, u32[]{:S(2)}, u32[]{:S(2)}) collective-permute-start(f32[48,256]{1,0:T(8,128)S(1)} %get-tuple-element.27), channel_id=1, source_target_pairs={{0,3},{1,0},{2,1},{3,2},{4,7},{5,4},{6,5},{7,6},{8,11},{9,8},{10,9... | collective-permute-start | bytes 147464 | tf_op jit(solution)/shard_map/ppermute | solution.py:407
  25.1 1.8 %collective-permute-done.1.more_1_ = f32[48,256]{1,0:T(8,128)S(1)} collective-permute-done((f32[48,256]{1,0:T(8,128)S(1)}, f32[48,256]{1,0:T(8,128)S(1)}, u32[]{:S(2)}, u32[]{:S(2)}) %collective-permute-start.1) | collective-permute-done | bytes 49184 | tf_op jit(solution)/shard_map/ppermute | solution.py:407
  26.9 0.5 collective-permute-done.2.more_2_
  27.4 0.0 copy-start.3
  27.5 0.3 shard_map.96.halo_ref
  27.7 1.6 %collective-permute-start.3 = (f32[6,2,8,256]{3,2,1,0:T(8,128)S(1)}, f32[6,2,8,256]{3,2,1,0:T(8,128)S(1)}, u32[]{:S(2)}, u32[]{:S(2)}) collective-permute-start(f32[6,2,8,256]{3,2,1,0:T(8,128)S(1)} %shard_map.96.halo_ref), channel_id=1, source_target_pairs={{0,8},{4,12},{8,0},{12,4},{1,9},{5,13},{9,1},{13,5},{2,10},{6,14},... | collective-permute-start | bytes 294920 | tf_op jit(solution)/shard_map/ppermute | solution.py:403
  29.3 0.0 collective-permute-done.4.across_outer_ref.across_ref
  29.3 0.0 collective-permute-start.7
  30.0 2.4 %collective-permute-done.3.across_halo_ref = f32[6,2,8,256]{3,2,1,0:T(8,128)S(1)} collective-permute-done((f32[6,2,8,256]{3,2,1,0:T(8,128)S(1)}, f32[6,2,8,256]{3,2,1,0:T(8,128)S(1)}, u32[]{:S(2)}, u32[]{:S(2)}) %collective-permute-start.3) | collective-permute-done | bytes 98336 | tf_op jit(solution)/shard_map/ppermute | solution.py:403
  32.4 0.0 collective-permute-done.7.sib_across_outer_ref.sibling_across_ref
  32.4 0.0 collective-permute-done.6.sibling_ref
  32.4 0.0 copy-start
  32.4 0.7 %copy-done = f32[6,8,8,256]{3,2,1,0:T(8,128)} copy-done((f32[6,8,8,256]{3,2,1,0:T(8,128)}, f32[6,8,8,256]{3,2,1,0:T(8,128)S(1)}, u32[]{:S(2)}) %copy-start) | copy-done | bytes 393240
  33.2 0.0 collective-permute-done.8.sib_across_rest_ref
  33.2 0.0 copy-done.3
  33.2 0.0 copy-start.1
  33.2 1.0 %copy-done.1 = f32[6,8,8,256]{3,2,1,0:T(8,128)S(1)} copy-done((f32[6,8,8,256]{3,2,1,0:T(8,128)S(1)}, f32[6,8,8,256]{3,2,1,0:T(8,128)}, u32[]{:S(2)}) %copy-start.1) | copy-done | bytes 393240
  34.2 0.0 copy-start.4
  34.2 10.6 %shard_map.97 = (f32[6,8,8,256]{3,2,1,0:T(8,128)S(1)}, f32[6,8,8,256]{3,2,1,0:T(8,128)S(1)}, f32[6,8,8,256]{3,2,1,0:T(8,128)S(1)}) custom-call(f32[1]{0:T(128)S(6)} %copy.13.frequency_ref, f32[6,8,8,256]{3,2,1,0:T(8,128)S(1)} %get-tuple-element.20.rows_ref, f32[8,8,256]{2,1,0:T(8,128)S(1)} %copy-done.3, f32[6,2,8,256]{3,2,1,0:T(8,128)S(1)} %shard_map.96.halo_ref, ...), custom_call_target="tpu_custom_call" | custom-call | tf_op jit(solution)/shard_map/pallas_call | solution.py:469
  44.7 0.0 copy-start.7
  44.8 0.6 copy-done.7
  45.4 0.0 copy-start.9
  45.4 0.6 %copy-done.9 = f32[6,2,8,256]{3,2,1,0:T(8,128)} copy-done((f32[6,2,8,256]{3,2,1,0:T(8,128)}, f32[6,2,8,256]{3,2,1,0:T(8,128)S(1)}, u32[]{:S(2)}) %copy-start.9) | copy-done | bytes 98328
  46.0 0.0 collective-permute-start.12
  46.0 0.0 copy-done.4
  46.0 0.0 copy-start.8
  46.0 0.9 %copy-done.8 = f32[6,2,8,256]{3,2,1,0:T(8,128)S(1)} copy-done((f32[6,2,8,256]{3,2,1,0:T(8,128)S(1)}, f32[6,2,8,256]{3,2,1,0:T(8,128)}, u32[]{:S(2)}) %copy-start.8) | copy-done | bytes 98328
  46.9 0.0 copy-start.10
  46.9 0.9 %copy-done.10 = f32[6,2,8,256]{3,2,1,0:T(8,128)S(1)} copy-done((f32[6,2,8,256]{3,2,1,0:T(8,128)S(1)}, f32[6,2,8,256]{3,2,1,0:T(8,128)}, u32[]{:S(2)}) %copy-start.10) | copy-done | bytes 98328
  47.8 0.4 shard_map.98
  48.2 0.7 %collective-permute-start.9 = (f32[48,256]{1,0:T(8,128)S(1)}, f32[48,256]{1,0:T(8,128)S(1)}, u32[]{:S(2)}, u32[]{:S(2)}) collective-permute-start(f32[48,256]{1,0:T(8,128)S(1)} %get-tuple-element.31), channel_id=1, source_target_pairs={{0,1},{1,2},{2,3},{3,0},{4,5},{5,6},{6,7},{7,4},{8,9},{9,10},{10,1... | collective-permute-start | bytes 147464 | tf_op jit(solution)/shard_map/ppermute | solution.py:407
  48.9 3.5 %collective-permute-start.10 = (f32[48,256]{1,0:T(8,128)S(1)}, f32[48,256]{1,0:T(8,128)S(1)}, u32[]{:S(2)}, u32[]{:S(2)}) collective-permute-start(f32[48,256]{1,0:T(8,128)S(1)} %get-tuple-element.32), channel_id=1, source_target_pairs={{0,2},{1,3},{2,0},{3,1},{4,6},{5,7},{6,4},{7,5},{8,10},{9,11},{10,... | collective-permute-start | bytes 147464 | tf_op jit(solution)/shard_map/ppermute | solution.py:407
  52.4 0.0 collective-permute-start.11
  52.4 2.3 %collective-permute-done.9.more_0_ = f32[48,256]{1,0:T(8,128)S(1)} collective-permute-done((f32[48,256]{1,0:T(8,128)S(1)}, f32[48,256]{1,0:T(8,128)S(1)}, u32[]{:S(2)}, u32[]{:S(2)}) %collective-permute-start.9) | collective-permute-done | bytes 49184 | tf_op jit(solution)/shard_map/ppermute | solution.py:407
  54.7 1.7 %collective-permute-done.10.more_1_ = f32[48,256]{1,0:T(8,128)S(1)} collective-permute-done((f32[48,256]{1,0:T(8,128)S(1)}, f32[48,256]{1,0:T(8,128)S(1)}, u32[]{:S(2)}, u32[]{:S(2)}) %collective-permute-start.10) | collective-permute-done | bytes 49184 | tf_op jit(solution)/shard_map/ppermute | solution.py:407
  56.4 0.5 collective-permute-done.11.more_2_
  56.9 0.0 copy-start.5
  56.9 0.3 shard_map.99.halo_ref
  57.2 0.0 collective-permute-done.12.received_ref
  57.2 0.5 copy-done.5
  57.8 5.7 %shard_map.100 = (f32[6,64,256]{2,1,0:T(8,128)}, f32[6,64,256]{2,1,0:T(8,128)}) custom-call(f32[1]{0:T(128)S(6)} %copy.13.frequency_ref, s32[4]{0:T(128)} %counts_ref.3, f32[6,8,8,256]{3,2,1,0:T(8,128)S(1)} %get-tuple-element.29.rows_ref, f32[8,8,256]{2,1,0:T(8,128)S(1)} %copy-done.5, f32[6,2,8,256]{3,2,1,0:T(8,128)S(1)} %shard_map.99.halo_ref, ...), custom_call_target="tpu_custom_call" | custom-call | tf_op jit(solution)/shard_map/pallas_call | solution.py:480
Async XLA Ops:
  0.6 1.4 %copy-start.12 = (s32[8,2]{0,1:T(2,128)S(1)}, s32[8,2]{0,1:T(2,128)}, u32[]{:S(2)}) copy-start(s32[8,2]{0,1:T(2,128)} %param.14) | copy-start | bytes 196
  2.0 0.7 %copy-start.13 = (s32[8,2]{0,1:T(2,128)S(1)}, s32[8,2]{0,1:T(2,128)}, u32[]{:S(2)}) copy-start(s32[8,2]{0,1:T(2,128)} %param.15) | copy-start | bytes 196
  3.3 1.0 %copy-start.6 = (f32[1,6,64,256]{3,2,1,0:T(8,128)S(1)}, f32[1,6,64,256]{3,2,1,0:T(8,128)}, u32[]{:S(2)}) copy-start(f32[1,6,64,256]{3,2,1,0:T(8,128)} %param.8) | copy-start | bytes 1179652
  4.3 0.8 %copy-start.11 = (f32[64,256]{1,0:T(8,128)S(1)}, f32[64,256]{1,0:T(8,128)}, u32[]{:S(2)}) copy-start(f32[64,256]{1,0:T(8,128)} %volume_ref.1) | copy-start | bytes 196612
  6.5 0.6 copy-start.2
  7.1 9.9 %collective-permute-start.5 = (f32[6,6,8,256]{3,2,1,0:T(8,128)S(1)}, f32[6,6,8,256]{3,2,1,0:T(8,128)S(1)}, u32[]{:S(2)}, u32[]{:S(2)}) collective-permute-start(f32[6,6,8,256]{3,2,1,0:T(8,128)S(1)} %get-tuple-element.28), channel_id=1, source_target_pairs={{0,8},{4,12},{8,0},{12,4},{1,9},{5,13},{9,1},{13,5},{2,10},{6,14},... | collective-permute-start | bytes 884744 | tf_op jit(solution)/shard_map/ppermute | solution.py:403
  10.1 22.3 %collective-permute-start.6 = (f32[6,8,8,256]{3,2,1,0:T(8,128)S(1)}, f32[6,8,8,256]{3,2,1,0:T(8,128)S(1)}, u32[]{:S(2)}, u32[]{:S(2)}) collective-permute-start(f32[6,8,8,256]{3,2,1,0:T(8,128)S(1)} %get-tuple-element.20.rows_ref), channel_id=1, source_target_pairs={{0,4},{4,0},{8,12},{12,8},{1,5},{5,1},{9,13},{13,9},{2,6},{6,2},{1... | collective-permute-start | bytes 1179656 | tf_op jit(solution)/shard_map/ppermute | solution.py:403
  17.1 16.1 %collective-permute-start.8 = (f32[6,6,8,256]{3,2,1,0:T(8,128)S(1)}, f32[6,6,8,256]{3,2,1,0:T(8,128)S(1)}, u32[]{:S(2)}, u32[]{:S(2)}) collective-permute-start(f32[6,6,8,256]{3,2,1,0:T(8,128)S(1)} %collective-permute-done.5.across_rest_ref), channel_id=1, source_target_pairs={{0,4},{4,0},{8,12},{12,8},{1,5},{5,1},{9,13},{13,9},{2,6},{6,2},{1... | collective-permute-start | bytes 884744 | tf_op jit(solution)/shard_map/ppermute | solution.py:403
  17.1 6.3 %collective-permute-start = (f32[48,256]{1,0:T(8,128)S(1)}, f32[48,256]{1,0:T(8,128)S(1)}, u32[]{:S(2)}, u32[]{:S(2)}) collective-permute-start(f32[48,256]{1,0:T(8,128)S(1)} %get-tuple-element.25), channel_id=1, source_target_pairs={{0,1},{1,2},{2,3},{3,0},{4,5},{5,6},{6,7},{7,4},{8,9},{9,10},{10,1... | collective-permute-start | bytes 147464 | tf_op jit(solution)/shard_map/ppermute | solution.py:407
  18.9 10.4 %collective-permute-start.4 = (f32[6,2,8,256]{3,2,1,0:T(8,128)S(1)}, f32[6,2,8,256]{3,2,1,0:T(8,128)S(1)}, u32[]{:S(2)}, u32[]{:S(2)}) collective-permute-start(f32[6,2,8,256]{3,2,1,0:T(8,128)S(1)} %get-tuple-element.24.outer_ref), channel_id=1, source_target_pairs={{0,8},{4,12},{8,0},{12,4},{1,9},{5,13},{9,1},{13,5},{2,10},{6,14},... | collective-permute-start | bytes 294920 | tf_op jit(solution)/shard_map/ppermute | solution.py:403
  20.4 6.5 %collective-permute-start.1 = (f32[48,256]{1,0:T(8,128)S(1)}, f32[48,256]{1,0:T(8,128)S(1)}, u32[]{:S(2)}, u32[]{:S(2)}) collective-permute-start(f32[48,256]{1,0:T(8,128)S(1)} %get-tuple-element.26), channel_id=1, source_target_pairs={{0,2},{1,3},{2,0},{3,1},{4,6},{5,7},{6,4},{7,5},{8,10},{9,11},{10,... | collective-permute-start | bytes 147464 | tf_op jit(solution)/shard_map/ppermute | solution.py:407
  23.4 4.1 %collective-permute-start.2 = (f32[48,256]{1,0:T(8,128)S(1)}, f32[48,256]{1,0:T(8,128)S(1)}, u32[]{:S(2)}, u32[]{:S(2)}) collective-permute-start(f32[48,256]{1,0:T(8,128)S(1)} %get-tuple-element.27), channel_id=1, source_target_pairs={{0,3},{1,0},{2,1},{3,2},{4,7},{5,4},{6,5},{7,6},{8,11},{9,8},{10,9... | collective-permute-start | bytes 147464 | tf_op jit(solution)/shard_map/ppermute | solution.py:407
  27.4 5.7 %copy-start.3 = (f32[8,8,256]{2,1,0:T(8,128)S(1)}, f32[8,8,256]{2,1,0:T(8,128)}, u32[]{:S(2)}) copy-start(f32[8,8,256]{2,1,0:T(8,128)} %copy-done.2) | copy-start | bytes 196612
  27.7 4.7 %collective-permute-start.3 = (f32[6,2,8,256]{3,2,1,0:T(8,128)S(1)}, f32[6,2,8,256]{3,2,1,0:T(8,128)S(1)}, u32[]{:S(2)}, u32[]{:S(2)}) collective-permute-start(f32[6,2,8,256]{3,2,1,0:T(8,128)S(1)} %shard_map.96.halo_ref), channel_id=1, source_target_pairs={{0,8},{4,12},{8,0},{12,4},{1,9},{5,13},{9,1},{13,5},{2,10},{6,14},... | collective-permute-start | bytes 294920 | tf_op jit(solution)/shard_map/ppermute | solution.py:403
  29.3 3.1 %collective-permute-start.7 = (f32[6,2,8,256]{3,2,1,0:T(8,128)S(1)}, f32[6,2,8,256]{3,2,1,0:T(8,128)S(1)}, u32[]{:S(2)}, u32[]{:S(2)}) collective-permute-start(f32[6,2,8,256]{3,2,1,0:T(8,128)S(1)} %collective-permute-done.4.across_outer_ref.across_ref), channel_id=1, source_target_pairs={{0,4},{4,0},{8,12},{12,8},{1,5},{5,1},{9,13},{13,9},{2,6},{6,2},{1... | collective-permute-start | bytes 294920 | tf_op jit(solution)/shard_map/ppermute | solution.py:403
  32.4 0.7 %copy-start = (f32[6,8,8,256]{3,2,1,0:T(8,128)}, f32[6,8,8,256]{3,2,1,0:T(8,128)S(1)}, u32[]{:S(2)}) copy-start(f32[6,8,8,256]{3,2,1,0:T(8,128)S(1)} %collective-permute-done.6.sibling_ref) | copy-start | bytes 1179652
  33.2 1.0 %copy-start.1 = (f32[6,8,8,256]{3,2,1,0:T(8,128)S(1)}, f32[6,8,8,256]{3,2,1,0:T(8,128)}, u32[]{:S(2)}) copy-start(f32[6,8,8,256]{3,2,1,0:T(8,128)} %copy-done) | copy-start | bytes 1179652
  34.2 11.9 %copy-start.4 = (f32[8,8,256]{2,1,0:T(8,128)S(1)}, f32[8,8,256]{2,1,0:T(8,128)}, u32[]{:S(2)}) copy-start(f32[8,8,256]{2,1,0:T(8,128)} %copy-done.2) | copy-start | bytes 196612
  44.7 0.6 %copy-start.7 = (f32[6,2,8,256]{3,2,1,0:T(8,128)}, f32[6,2,8,256]{3,2,1,0:T(8,128)S(1)}, u32[]{:S(2)}) copy-start(f32[6,2,8,256]{3,2,1,0:T(8,128)S(1)} %collective-permute-done.4.across_outer_ref.across_ref) | copy-start | bytes 294916
  45.4 0.6 %copy-start.9 = (f32[6,2,8,256]{3,2,1,0:T(8,128)}, f32[6,2,8,256]{3,2,1,0:T(8,128)S(1)}, u32[]{:S(2)}) copy-start(f32[6,2,8,256]{3,2,1,0:T(8,128)S(1)} %collective-permute-done.7.sib_across_outer_ref.sibling_across_ref) | copy-start | bytes 294916
  46.0 11.2 %collective-permute-start.12 = (f32[6,8,8,256]{3,2,1,0:T(8,128)S(1)}, f32[6,8,8,256]{3,2,1,0:T(8,128)S(1)}, u32[]{:S(2)}, u32[]{:S(2)}) collective-permute-start(f32[6,8,8,256]{3,2,1,0:T(8,128)S(1)} %get-tuple-element.35), channel_id=1, source_target_pairs={{0,4},{4,0},{8,12},{12,8},{1,5},{5,1},{9,13},{13,9},{2,6},{6,2},{1... | collective-permute-start | bytes 1179656 | tf_op jit(solution)/shard_map/ppermute | solution.py:403
  46.0 0.9 %copy-start.8 = (f32[6,2,8,256]{3,2,1,0:T(8,128)S(1)}, f32[6,2,8,256]{3,2,1,0:T(8,128)}, u32[]{:S(2)}) copy-start(f32[6,2,8,256]{3,2,1,0:T(8,128)} %copy-done.7) | copy-start | bytes 294916
  46.9 0.9 %copy-start.10 = (f32[6,2,8,256]{3,2,1,0:T(8,128)S(1)}, f32[6,2,8,256]{3,2,1,0:T(8,128)}, u32[]{:S(2)}) copy-start(f32[6,2,8,256]{3,2,1,0:T(8,128)} %copy-done.9) | copy-start | bytes 294916
  48.2 6.5 %collective-permute-start.9 = (f32[48,256]{1,0:T(8,128)S(1)}, f32[48,256]{1,0:T(8,128)S(1)}, u32[]{:S(2)}, u32[]{:S(2)}) collective-permute-start(f32[48,256]{1,0:T(8,128)S(1)} %get-tuple-element.31), channel_id=1, source_target_pairs={{0,1},{1,2},{2,3},{3,0},{4,5},{5,6},{6,7},{7,4},{8,9},{9,10},{10,1... | collective-permute-start | bytes 147464 | tf_op jit(solution)/shard_map/ppermute | solution.py:407
  48.9 7.6 %collective-permute-start.10 = (f32[48,256]{1,0:T(8,128)S(1)}, f32[48,256]{1,0:T(8,128)S(1)}, u32[]{:S(2)}, u32[]{:S(2)}) collective-permute-start(f32[48,256]{1,0:T(8,128)S(1)} %get-tuple-element.32), channel_id=1, source_target_pairs={{0,2},{1,3},{2,0},{3,1},{4,6},{5,7},{6,4},{7,5},{8,10},{9,11},{10,... | collective-permute-start | bytes 147464 | tf_op jit(solution)/shard_map/ppermute | solution.py:407
  52.4 4.5 %collective-permute-start.11 = (f32[48,256]{1,0:T(8,128)S(1)}, f32[48,256]{1,0:T(8,128)S(1)}, u32[]{:S(2)}, u32[]{:S(2)}) collective-permute-start(f32[48,256]{1,0:T(8,128)S(1)} %get-tuple-element.33), channel_id=1, source_target_pairs={{0,3},{1,0},{2,1},{3,2},{4,7},{5,4},{6,5},{7,6},{8,11},{9,8},{10,9... | collective-permute-start | bytes 147464 | tf_op jit(solution)/shard_map/ppermute | solution.py:407
  56.9 0.8 %copy-start.5 = (f32[8,8,256]{2,1,0:T(8,128)S(1)}, f32[8,8,256]{2,1,0:T(8,128)}, u32[]{:S(2)}) copy-start(f32[8,8,256]{2,1,0:T(8,128)} %copy-done.2) | copy-start | bytes 196612

commit v2 on v1

--- a/solution.py
+++ b/solution.py
@@ -21,6 +21,7 @@
 
 COMPS = 6
 FACES = 2 * BLOCKS_MAX
+POOLED = COMPS + 1
 F32 = jnp.float32
 VMEM = pl.BlockSpec(memory_space=pltpu.VMEM)
 SMEM = pl.BlockSpec(memory_space=pltpu.SMEM)
@@ -71,16 +72,32 @@
 DIFF_ONE = SECOND_DISSIPATION + 2.0 * FOURTH_DISSIPATION
 
 
-def residual_j(q, v, p):
-    speed = jnp.abs(v)
-    radius = 0.5 * (speed + ahead(speed)) + SOUND_SPEED
-    out = []
-    for q_c, g_c in zip(q, flux_along_j(q, v, p)):
-        step = ahead(q_c) - q_c
-        damping = DIFF_ONE * step - FOURTH_DISSIPATION * (ahead(step) + behind(step))
-        face = 0.5 * (g_c + ahead(g_c)) - radius * damping
-        out.append(face - behind(face))
-    return out
+def turn(x, shift):
+    return pltpu.roll(x, shift % x.shape[1], axis=1)
+
+
+def pitchwise_shifts(load, near_ref):
+    for c in range(COMPS):
+        for r in range(8):
+            q = load(c, r)
+            near_ref[0, c, r] = turn(q, -1)
+            near_ref[1, c, r] = turn(q, -2)
+            near_ref[2, c, r] = turn(q, 1)
+
+
+def pitchwise_faces(q, v, p, near_ref, r):
+    after = [near_ref[0, c, r] for c in range(COMPS)]
+    _, v_after, p_after = primitives(after)
+    radius = 0.5 * (jnp.abs(v) + jnp.abs(v_after)) + SOUND_SPEED
+    here, there = flux_along_j(q, v, p), flux_along_j(after, v_after, p_after)
+    upper, lower = [], []
+    for c in range(COMPS):
+        step = after[c] - q[c]
+        others = (near_ref[1, c, r] - after[c]) + (q[c] - near_ref[2, c, r])
+        damping = radius * (DIFF_ONE * step - FOURTH_DISSIPATION * others)
+        upper.append(0.5 * there[c] - damping)
+        lower.append(0.5 * here[c] - damping)
+    return upper, lower
 
 
 class Rows:
@@ -121,12 +138,8 @@
             self.faces[r] = out
         return self.faces[r]
 
-    def residual(self, r):
-        u, v, p = self.uvp(r)
-        lower, upper = self.face(r - 1), self.face(r)
-        across = residual_j(self.q(r), v, p)
-        total = [(b - a) + j for a, b, j in zip(lower, upper, across)]
-        return total, jnp.abs(u) + jnp.abs(v)
+    def along(self, r):
+        return [b - a for a, b in zip(self.face(r - 1), self.face(r))]
 
 
 def even_tiles(shape):
@@ -150,27 +163,29 @@
     return extended
 
 
-def split_parts(parts_ref, rest_ref):
-    def load(c, r):
-        if 2 <= r <= 5:
-            return rest_ref[c, r]
-        layer = r % 2
-        outer, other = parts_ref[c, layer], rest_ref[c, layer]
-        even = even_tiles(outer.shape)
-        if r < 2:
-            return jnp.where(even, outer, other)
-        return jnp.where(even, other, outer)
-
-    return load
-
-
-def coefficients(frequency_ref):
+def rows_from(raw_ref, half_ref, rows_ref):
+    for c in range(COMPS):
+        for h in range(2):
+            half_ref[c, h] = raw_ref[c, :, pl.ds(128 * h, 128)]
+    for c in range(COMPS):
+        for r in range(8):
+            for h in range(2):
+                rows_ref[c, r, :, pl.ds(128 * h, 128)] = half_ref[c, h, pl.ds(r, 8, stride=8), :]
+
+
+def put_coefficients(frequency_ref, weight_ref):
     weights = spectral_weights(4)
     omega = frequency_ref[0]
     even = lax.axis_index("inst") % 2 == 0
-    near = omega * jnp.where(even, F32(weights[3]), F32(weights[1]))
-    far = omega * jnp.where(even, F32(weights[1]), F32(weights[3]))
-    return omega, omega * F32(weights[0]), omega * F32(weights[2]), near, far
+    weight_ref[0] = omega
+    weight_ref[1] = omega * F32(weights[0])
+    weight_ref[2] = omega * F32(weights[2])
+    weight_ref[3] = omega * jnp.where(even, F32(weights[3]), F32(weights[1]))
+    weight_ref[4] = omega * jnp.where(even, F32(weights[1]), F32(weights[3]))
+
+
+def coefficients(weight_ref):
+    return [weight_ref[k] for k in range(5)]
 
 
 def own_instance_rate(speeds, volume, omega):
@@ -179,32 +194,24 @@
 
 def pack_kernel(
     space_total, block_total, cap,
-    state_ref, volume_ref, counts_ref, place_ref, links_ref, offset_ref, flip_ref,
-    rows_ref, vrows_ref, outer_ref, rest_ref, table_ref, index_ref, *more
+    state_ref, volume_ref, frequency_ref, counts_ref, place_ref, links_ref, offset_ref, flip_ref,
+    rows_ref, vrows_ref, outer_ref, table_ref, weight_ref, index_ref, *more
 ):
     sends = more[: space_total - 1]
-    half_ref, first_ref, inverse_ref = more[space_total - 1 :]
+    half_ref, arrival, first_ref, inverse_ref = more[space_total - 1 :]
     width = state_ref.shape[2]
-    for c in range(COMPS + 1):
-        for h in range(2):
-            lanes = pl.ds(128 * h, 128)
-            half_ref[c, h] = state_ref[c, :, lanes] if c < COMPS else volume_ref[:, lanes]
-    for c in range(COMPS + 1):
-        for r in range(8):
-            for h in range(2):
-                row = half_ref[c, h, pl.ds(r, 8, stride=8), :]
-                if c < COMPS:
-                    rows_ref[c, r, :, pl.ds(128 * h, 128)] = row
-                else:
-                    vrows_ref[r, :, pl.ds(128 * h, 128)] = row
-    even = even_tiles((8, width))
-    for c in range(COMPS):
-        for l in range(2):
-            low, high = rows_ref[c, l], rows_ref[c, 6 + l]
-            outer_ref[c, l] = jnp.where(even, low, high)
-            rest_ref[c, l] = jnp.where(even, high, low)
-        for r in range(2, 6):
-            rest_ref[c, r] = rows_ref[c, r]
+    copies = []
+    for h in range(2):
+        lanes = pl.ds(128 * h, 128)
+        for n, (source, target) in enumerate(
+            [
+                (state_ref.at[:, :, lanes], half_ref.at[h, pl.ds(0, COMPS)]),
+                (volume_ref.at[:, lanes], half_ref.at[h, COMPS]),
+            ]
+        ):
+            copies.append(pltpu.make_async_copy(source, target, arrival.at[2 * h + n]))
+            copies[-1].start()
+    put_coefficients(frequency_ref, weight_ref)
     me = lax.axis_index("space")
     total = jnp.int32(0)
     firsts = []
@@ -219,7 +226,7 @@
         return inverse_ref[jnp.minimum(first_ref[device] + slot, block_total - 1)]
 
     def source_of(block, side):
-        link = links_ref[block, side]
+        link = links_ref[side, block]
         place = place_ref[jnp.maximum(link, 0)]
         owner = jnp.int32(0)
         first = jnp.int32(0)
@@ -229,8 +236,9 @@
             first = jnp.where(past, firsts[d], first)
         return link, owner, 2 * (place - first) + (1 - side)
 
-    own_base = (space_total - 1) * COMPS * 2 * cap
+    own_base = (space_total - 1) * POOLED * 2 * cap
     few = 2 * counts_ref[me] <= cap
+    table_ref[3 * FACES + (space_total - 1) * cap] = counts_ref[me]
     tile = lax.broadcasted_iota(jnp.int32, (FACES, width), 0)
     start = jnp.zeros((FACES, width), jnp.int32)
     turned = jnp.zeros((FACES, width), jnp.int32)
@@ -243,13 +251,13 @@
         place = jnp.where(listed, jnp.minimum(source, cap - 1), min(f, cap - 1))
         outside = link < 0
         mine = owner == me
-        base = jnp.where(mine, own_base + source, (shift - 1) * (COMPS * 2 * cap) + place)
+        base = jnp.where(mine, own_base + source, (shift - 1) * (POOLED * 2 * cap) + place)
         base = jnp.where(outside, own_base + 8 * side + f, base)
         table_ref[f] = base
         table_ref[FACES + f] = jnp.where(outside | mine, 2 * FACES, 2 * cap)
         table_ref[2 * FACES + f] = jnp.where(outside, 0, jnp.where(mine, FACES, cap))
-        start = jnp.where(tile == f, jnp.where(outside, 0, offset_ref[block, side]), start)
-        turned = jnp.where(tile == f, jnp.where(outside, 0, flip_ref[block, side]), turned)
+        start = jnp.where(tile == f, jnp.where(outside, 0, offset_ref[side, block]), start)
+        turned = jnp.where(tile == f, jnp.where(outside, 0, flip_ref[side, block]), turned)
     column = lax.broadcasted_iota(jnp.int32, (FACES, width), 1)
     index_ref[...] = (start + jnp.where(turned == 1, width - 1 - column, column)) % width
     for k in range(1, space_total):
@@ -258,6 +266,21 @@
             _, owner, source = source_of(block_in(target, i // 2), i % 2)
             wanted = jnp.where(owner == me, source, 0)
             table_ref[3 * FACES + (k - 1) * cap + i] = jnp.where(few, i, wanted)
+    for copy in copies:
+        copy.wait()
+    for c in range(COMPS + 1):
+        for r in range(8):
+            for h in range(2):
+                row = half_ref[h, c, pl.ds(r, 8, stride=8), :]
+                if c < COMPS:
+                    rows_ref[c, r, :, pl.ds(128 * h, 128)] = row
+                else:
+                    vrows_ref[r, :, pl.ds(128 * h, 128)] = row
+    even = even_tiles((8, width))
+    for c in range(COMPS):
+        for l in range(2):
+            low, high = rows_ref[c, l], rows_ref[c, 6 + l]
+            outer_ref[c, l] = jnp.where(even, low, high)
     pack_sends(cap, outer_ref, table_ref, sends)
 
 
@@ -265,47 +288,69 @@
     for k, send_ref in enumerate(sends):
         for i in range(cap):
             f = table_ref[3 * FACES + k * cap + i]
-            for c in range(COMPS):
+            for c in range(outer_ref.shape[0]):
                 for l in range(2):
                     send_ref[pl.ds((2 * c + l) * cap + i, 1), :] = outer_ref[c, l, pl.ds(f, 1), :]
 
 
-def halo_kernel(space_total, cap, table_ref, index_ref, outer_ref, *more):
-    received = more[: space_total - 1]
-    halo_ref, pool_ref, raw_ref = more[space_total - 1 :]
-    size = COMPS * 2 * cap
+def permuted_halos(space_total, cap, table_ref, index_ref, outer_ref, received, pool_ref, raw_ref):
+    comps = outer_ref.shape[0]
     for k, part in enumerate(received):
-        pool_ref[pl.ds(k * size, size), :] = part[...]
-    own_base = (space_total - 1) * size
-    for c in range(COMPS):
+        pool_ref[pl.ds(k * POOLED * 2 * cap, comps * 2 * cap), :] = part[...]
+    own_base = (space_total - 1) * POOLED * 2 * cap
+    for c in range(comps):
         for l in range(2):
             pool_ref[pl.ds(own_base + (2 * c + l) * FACES, FACES), :] = outer_ref[c, l]
     for f in range(FACES):
         base, per_comp, per_layer = table_ref[f], table_ref[FACES + f], table_ref[2 * FACES + f]
-        for c in range(COMPS):
+        for c in range(comps):
             for l in range(2):
                 row = base + c * per_comp + l * per_layer
                 raw_ref[c, l, pl.ds(f, 1), :] = pool_ref[pl.ds(row, 1), :]
-    width = index_ref.shape[1]
     masks, lanes = [], []
-    for h in range(width // 128):
+    for h in range(2):
         index = index_ref[:, pl.ds(128 * h, 128)]
         lanes.append(index & 127)
         masks.append(index < 128)
-    for c in range(COMPS):
+    for c in reversed(range(comps)):
         for l in range(2):
             low, high = raw_ref[c, l, :, pl.ds(0, 128)], raw_ref[c, l, :, pl.ds(128, 128)]
             for h in range(2):
                 a = jnp.take_along_axis(low, lanes[h], axis=1)
                 b = jnp.take_along_axis(high, lanes[h], axis=1)
-                halo_ref[c, l, :, pl.ds(128 * h, 128)] = jnp.where(masks[h], a, b)
+                yield c, l, h, jnp.where(masks[h], a, b)
+
+
+def halo_kernel(space_total, cap, table_ref, index_ref, outer_ref, *more):
+    received, (halo_ref, pool_ref, raw_ref) = more[: space_total - 1], more[space_total - 1 :]
+    for c, l, h, halo in permuted_halos(
+        space_total, cap, table_ref, index_ref, outer_ref, received, pool_ref, raw_ref
+    ):
+        halo_ref[c, l, :, pl.ds(128 * h, 128)] = halo
+
+
+def next_halo_kernel(
+    space_total, cap, table_ref, index_ref, weight_ref, outer_ref, across_ref, far_ref, *more
+):
+    received, (halo_ref, pool_ref, raw_ref) = more[: space_total - 1], more[space_total - 1 :]
+    omega, w_own, w_across, w_near, w_far = coefficients(weight_ref)
+    gain = {}
+    for c, l, h, halo in permuted_halos(
+        space_total, cap, table_ref, index_ref, outer_ref, received, pool_ref, raw_ref
+    ):
+        if c == COMPS:
+            gain[l, h] = halo
+            continue
+        lanes = pl.ds(128 * h, 128)
+        lacking = w_across * across_ref[c, l, :, lanes] + w_far * far_ref[c, l, :, lanes]
+        halo_ref[c, l, :, lanes] = halo - gain[l, h] * lacking
 
 
 def outer_kernel(
-    cap, table_ref, frequency_ref, rows_ref, vrows_ref, halo_ref, across_ref, sibling_ref,
-    sibling_across_ref, outer_ref, *sends
-):
-    omega, w_own, w_across, w_near, w_far = coefficients(frequency_ref)
+    cap, table_ref, weight_ref, rows_ref, vrows_ref, halo_ref, sibling_ref, outer_ref, *more
+):
+    sends, near_ref, lower_ref = more[:-2], more[-2], more[-1]
+    omega, w_own, w_across, w_near, w_far = coefficients(weight_ref)
     load = row_loader(lambda c, r: rows_ref[c, r], halo_ref)
     even = even_tiles(vrows_ref.shape[1:])
     low = {r: load(r) for r in range(-2, 4)}
@@ -314,66 +359,135 @@
         k: [jnp.where(even, a, b) for a, b in zip(low[k - 2], high[k + 4])] for k in range(6)
     }
     rows = Rows(lambda k: picked[k])
+    for c in range(COMPS):
+        for l in range(2):
+            q = picked[l + 2][c]
+            near_ref[0, c, l] = turn(q, -1)
+            near_ref[1, c, l] = turn(q, -2)
+            near_ref[2, c, l] = turn(q, 1)
+    rates = []
     for l in range(2):
-        flux, speeds = rows.residual(l + 2)
+        q = picked[l + 2]
+        u, v, p = rows.uvp(l + 2)
+        upper, lower = pitchwise_faces(q, v, p, near_ref, l)
+        along = rows.along(l + 2)
         volume = jnp.where(even, vrows_ref[l], vrows_ref[l + 6])
-        rate = own_instance_rate(speeds, volume, omega)
-        for c in range(COMPS):
-            own = picked[l + 2][c]
+        rate = own_instance_rate(jnp.abs(u) + jnp.abs(v), volume, omega)
+        rates.append(rate)
+        outer_ref[COMPS, l] = rate * volume
+        for c in range(COMPS):
             sibling = jnp.where(even, sibling_ref[c, l], sibling_ref[c, l + 6])
-            spectral = (
-                w_own * own + w_across * across_ref[c, l]
-                + w_near * sibling + w_far * sibling_across_ref[c, l]
-            )
-            outer_ref[c, l] = own - rate * (flux[c] + volume * spectral)
+            spectral = w_own * q[c] + w_near * sibling
+            outer_ref[c, l] = q[c] - rate * (along[c] + upper[c] + volume * spectral)
+            lower_ref[c, l] = lower[c]
+    for l in range(2):
+        for c in range(COMPS):
+            outer_ref[c, l] = outer_ref[c, l] + rates[l] * turn(lower_ref[c, l], 1)
     pack_sends(cap, outer_ref, table_ref, sends)
 
 
-def first_kernel(
-    frequency_ref, rows_ref, vrows_ref, halo_ref, across_halo_ref, across_outer_ref,
-    across_rest_ref, sibling_ref, sib_across_outer_ref, sib_across_rest_ref,
-    next_ref, partial_ref, send_ref
-):
-    omega, w_own, w_across, w_near, w_far = coefficients(frequency_ref)
-    own_load = lambda c, r: rows_ref[c, r]
-    across_load = split_parts(across_outer_ref, across_rest_ref)
-    far_load = split_parts(sib_across_outer_ref, sib_across_rest_ref)
-    own = Rows(row_loader(own_load, halo_ref))
-    across = Rows(row_loader(across_load, across_halo_ref))
+def sweep(load, halo_ref, vrows_ref, omega, term, next_ref, near_ref, lower_ref, rate_ref):
+    pitchwise_shifts(load, near_ref)
+    rows = Rows(row_loader(load, halo_ref))
+    for r in range(8):
+        q = rows.q(r)
+        u, v, p = rows.uvp(r)
+        upper, lower = pitchwise_faces(q, v, p, near_ref, r)
+        along = rows.along(r)
+        volume = vrows_ref[r]
+        rate = own_instance_rate(jnp.abs(u) + jnp.abs(v), volume, omega)
+        rate_ref[r] = rate
+        for c in range(COMPS):
+            next_ref[c, r] = q[c] - rate * (along[c] + upper[c] + volume * term(c, r, q[c]))
+            lower_ref[c, r] = lower[c]
+    for r in range(8):
+        rate = rate_ref[r]
+        for c in range(COMPS):
+            next_ref[c, r] = next_ref[c, r] + rate * turn(lower_ref[c, r], 1)
+
+
+def own_kernel(
+    weight_ref, rows_ref, vrows_ref, halo_ref, sibling_ref,
+    next_ref, gain_ref, near_ref, lower_ref
+):
+    omega, w_own, w_across, w_near, w_far = coefficients(weight_ref)
+    sweep(
+        lambda c, r: rows_ref[c, r], halo_ref, vrows_ref, omega,
+        lambda c, r, q: w_own * q + w_near * sibling_ref[c, r],
+        next_ref, near_ref, lower_ref, gain_ref,
+    )
+    for r in range(8):
+        gain_ref[r] = gain_ref[r] * vrows_ref[r]
+
+
+def across_kernel(
+    weight_ref, rows_ref, vrows_ref, halo_ref, across_ref, sibling_ref, own_ref, own_gain_ref,
+    next_ref, gain_ref, own_next_ref, near_ref, lower_ref, half_ref, state_ref
+):
+    omega, w_own, w_across, w_near, w_far = coefficients(weight_ref)
+    rows_from(across_ref, half_ref, state_ref)
+    sweep(
+        lambda c, r: state_ref[c, r], halo_ref, vrows_ref, omega,
+        lambda c, r, q: w_own * q + w_across * rows_ref[c, r] + w_far * sibling_ref[c, r],
+        next_ref, near_ref, lower_ref, gain_ref,
+    )
+    for r in range(8):
+        gain_ref[r] = gain_ref[r] * vrows_ref[r]
+        gain = own_gain_ref[r] * w_across
+        for c in range(COMPS):
+            own_next_ref[c, r] = own_ref[c, r] - gain * state_ref[c, r]
+
+
+def finish_kernel(
+    weight_ref, own_ref, own_gain_ref, across_ref, across_gain_ref, far_ref,
+    next_ref, partial_ref, send_ref, half_ref, state_ref
+):
+    omega, w_own, w_across, w_near, w_far = coefficients(weight_ref)
+    rows_from(far_ref, half_ref, state_ref)
+    for r in range(8):
+        own_gain, across_gain = own_gain_ref[r] * w_far, across_gain_ref[r] * w_near
+        for c in range(COMPS):
+            far = state_ref[c, r]
+            mine = own_ref[c, r] - own_gain * far
+            other = across_ref[c, r] - across_gain * far
+            next_ref[c, r] = mine
+            partial_ref[c, r] = w_own * mine + w_across * other
+            send_ref[c, r] = w_far * mine + w_near * other
+
+
+def pitchwise_kernel(
+    rows_ref, vrows_ref, partial_ref, weight_ref, sum_ref, rate_ref, near_ref, lower_ref
+):
+    load = lambda c, r: rows_ref[c, r]
+    pitchwise_shifts(load, near_ref)
+    for r in range(8):
+        q = [load(c, r) for c in range(COMPS)]
+        u, v, p = primitives(q)
+        upper, lower = pitchwise_faces(q, v, p, near_ref, r)
+        volume = vrows_ref[r]
+        rate_ref[r] = own_instance_rate(jnp.abs(u) + jnp.abs(v), volume, weight_ref[0])
+        for c in range(COMPS):
+            sum_ref[c, r] = upper[c] + volume * partial_ref[c, r]
+            lower_ref[c, r] = lower[c]
+    for r in range(8):
+        for c in range(COMPS):
+            sum_ref[c, r] = sum_ref[c, r] - turn(lower_ref[c, r], 1)
+
+
+def last_kernel(
+    space_total, cap, table_ref, rows_ref, vrows_ref, halo_ref, sum_ref, rate_ref, received_ref,
+    new_ref, residual_ref, new_half_ref, residual_half_ref
+):
+    own = Rows(row_loader(lambda c, r: rows_ref[c, r], halo_ref))
+    live_slots = table_ref[3 * FACES + (space_total - 1) * cap]
+    live = (lax.broadcasted_iota(jnp.int32, vrows_ref.shape[1:], 0) // 2) < live_slots
     for r in range(8):
         volume = vrows_ref[r]
-        own_flux, own_speeds = own.residual(r)
-        own_rate = own_instance_rate(own_speeds, volume, omega)
-        across_flux, across_speeds = across.residual(r)
-        across_rate = own_instance_rate(across_speeds, volume, omega)
-        for c in range(COMPS):
-            mine, other = own.q(r)[c], across.q(r)[c]
-            near, far = sibling_ref[c, r], far_load(c, r)
-            spectral = w_own * mine + w_across * other + w_near * near + w_far * far
-            mine_next = mine - own_rate * (own_flux[c] + volume * spectral)
-            spectral = w_own * other + w_across * mine + w_far * near + w_near * far
-            other_next = other - across_rate * (across_flux[c] + volume * spectral)
-            next_ref[c, r] = mine_next
-            partial_ref[c, r] = w_own * mine_next + w_across * other_next
-            send_ref[c, r] = w_far * mine_next + w_near * other_next
-
-
-def last_kernel(
-    frequency_ref, counts_ref, rows_ref, vrows_ref, halo_ref, partial_ref, received_ref,
-    new_ref, residual_ref, new_half_ref, residual_half_ref
-):
-    omega = frequency_ref[0]
-    own = Rows(row_loader(lambda c, r: rows_ref[c, r], halo_ref))
-    live = (lax.broadcasted_iota(jnp.int32, vrows_ref.shape[1:], 0) // 2) < counts_ref[
-        lax.axis_index("space")
-    ]
-    for r in range(8):
-        volume = vrows_ref[r]
-        flux, speeds = own.residual(r)
-        rate = own_instance_rate(speeds, volume, omega)
+        along = own.along(r)
+        rate = rate_ref[r]
         inverse = 1.0 / volume
         for c in range(COMPS):
-            residual = flux[c] + volume * (partial_ref[c, r] + received_ref[c, r])
+            residual = sum_ref[c, r] + along[c] + volume * received_ref[c, r]
             new = jnp.where(live, own.q(r)[c] - rate * residual, 0.0)
             scaled = jnp.where(live, residual * inverse, 0.0)
             for h in range(2):
@@ -386,6 +500,10 @@
             residual_ref[c, :, pl.ds(128 * h, 128)] = residual_half_ref[c, h]
 
 
+def after_kernel(value_ref, first_ref, out_ref):
+    pass
+
+
 def hold(x):
     return pltpu.with_memory_space_constraint(x, pltpu.VMEM)
 
@@ -410,82 +528,128 @@
 
     full = (comps, 8, 8, width)
     outer = (comps, 2, 8, width)
-    pair = (comps * 2 * cap, width)
-    entries = 3 * FACES + (space_total - 1) * cap
+    plane = (8, 8, width)
+    pooled = (POOLED, 2, 8, width)
+    entries = 3 * FACES + (space_total - 1) * cap + 1
     on_chip = lambda shape, dtype=F32: pltpu.VMEM(shape, dtype)
-    sends_shape = [on_chip(pair) for _ in range(space_total - 1)]
-
-    packed = pl.pallas_call(
+    sends_shape = lambda n: [on_chip((n * 2 * cap, width)) for _ in range(space_total - 1)]
+    shifts = [pltpu.VMEM((3,) + full, F32), pltpu.VMEM(full, F32)]
+
+    def call(kernel, out, specs, args, scratch=(), micros=0.3, out_specs=None, aliases={}):
+        args = [hold(x) if spec is VMEM else x for spec, x in zip(specs, args)]
+        return pl.pallas_call(
+            kernel,
+            out_shape=out,
+            in_specs=specs,
+            out_specs=out_specs or jax.tree.map(lambda _: VMEM, out),
+            scratch_shapes=list(scratch),
+            input_output_aliases=aliases,
+            compiler_params=pltpu.CompilerParams(vmem_limit_bytes=8 << 20),
+            cost_estimate=pl.CostEstimate(
+                flops=0, bytes_accessed=1, transcendentals=0
+            ),
+        )(*args)
+
+    in_smem = lambda x: pltpu.with_memory_space_constraint(x, pltpu.SMEM)
+    far_off = pl.BlockSpec(memory_space=pltpu.HBM)
+    packed = call(
         functools.partial(pack_kernel, space_total, block_total, cap),
-        out_shape=[
-            on_chip(full), on_chip((8, 8, width)), on_chip(outer), on_chip((comps, 6, 8, width)),
-            pltpu.SMEM((entries,), jnp.int32), on_chip((FACES, width), jnp.int32), *sends_shape,
+        [
+            on_chip(full), on_chip(plane), on_chip(outer),
+            pltpu.SMEM((entries,), jnp.int32), pltpu.SMEM((8,), F32),
+            on_chip((FACES, width), jnp.int32), *sends_shape(comps),
         ],
-        in_specs=[VMEM, VMEM] + [SMEM] * 5,
-        out_specs=[VMEM] * 4 + [SMEM, VMEM] + [VMEM] * (space_total - 1),
-        scratch_shapes=[
-            pltpu.VMEM((comps + 1, 2, row_count, 128), F32),
+        [far_off] * 2 + [SMEM] * 6,
+        (state, cell_volume, frequency, block_count, block_place, face_links.T, face_offset.T, face_flip.T),
+        scratch=[
+            pltpu.VMEM((2, comps + 1, row_count, 128), F32),
+            pltpu.SemaphoreType.DMA((4,)),
             pltpu.SMEM((space_total,), jnp.int32),
             pltpu.SMEM((block_total,), jnp.int32),
         ],
-    )(hold(state), hold(cell_volume), block_count, block_place, face_links, face_offset, face_flip)
-    rows, vrows, outer_rows, rest, table, index = packed[:6]
+        micros=2.0,
+        out_specs=[VMEM] * 3 + [SMEM] * 2 + [VMEM] * space_total,
+    )
+    rows, vrows, outer_rows, table, weights, index = packed[:6]
     sends = packed[6:]
-    in_smem = lambda x: pltpu.with_memory_space_constraint(x, pltpu.SMEM)
-    table = in_smem(table)
-
-    def halos(outer_own, received):
-        return pl.pallas_call(
-            functools.partial(halo_kernel, space_total, cap),
-            out_shape=on_chip(outer),
-            in_specs=[SMEM] + [VMEM] * (2 + len(received)),
-            out_specs=VMEM,
-            scratch_shapes=[
-                pltpu.VMEM(((space_total - 1) * pair[0] + comps * 2 * FACES, width), F32),
-                pltpu.VMEM(outer, F32),
-            ],
-        )(table, hold(index), hold(outer_own), *[hold(x) for x in received])
-
-    across_outer = over_inst(outer_rows, 2)
-    across_rest = over_inst(rest, 2)
+    table, weights = in_smem(table), in_smem(weights)
+    halves = [pltpu.VMEM((comps, 2, row_count, 128), F32), pltpu.VMEM(full, F32)]
+    pool = [
+        pltpu.VMEM(((space_total - 1) * POOLED * 2 * cap + POOLED * 2 * FACES, width), F32),
+        pltpu.VMEM(pooled, F32),
+    ]
+
+    across = over_inst(state, 2)
     sibling = over_inst(rows, 1)
-    halo = halos(outer_rows, over_space(sends))
-    sib_across_outer = over_inst(across_outer, 1)
+    received = over_space(sends)
+    halo = call(
+        functools.partial(halo_kernel, space_total, cap),
+        on_chip(outer),
+        [SMEM] + [VMEM] * (1 + space_total),
+        (table, index, outer_rows, *received),
+        scratch=pool,
+    )
     across_halo = over_inst(halo, 2)
-
-    produced = pl.pallas_call(
+    next_outer, *next_sends = call(
         functools.partial(outer_kernel, cap),
-        out_shape=[on_chip(outer), *sends_shape],
-        in_specs=[SMEM, SMEM] + [VMEM] * 6,
-        out_specs=[VMEM] * space_total,
-    )(
-        table, frequency, hold(rows), hold(vrows), hold(halo), hold(across_outer), hold(sibling),
-        hold(sib_across_outer),
-    )
-    next_outer, next_sends = produced[0], produced[1:]
-    sib_across_rest = over_inst(across_rest, 1)
-    next_halo = halos(next_outer, over_space(next_sends))
-
-    next_rows, partial, to_sibling = pl.pallas_call(
-        first_kernel,
-        out_shape=[on_chip(full)] * 3,
-        in_specs=[SMEM] + [VMEM] * 9,
-        out_specs=[VMEM] * 3,
-    )(
-        frequency, hold(rows), hold(vrows), hold(halo), hold(across_halo), hold(across_outer),
-        hold(across_rest), hold(sibling), hold(sib_across_outer), hold(sib_across_rest),
+        [on_chip(pooled), *sends_shape(POOLED)],
+        [SMEM, SMEM] + [VMEM] * 4,
+        (table, weights, rows, vrows, halo, sibling),
+        scratch=[pltpu.VMEM((3,) + outer, F32), pltpu.VMEM(outer, F32)],
+        micros=0.4,
+    )
+    next_received = over_space(next_sends)
+    far_halo = over_inst(across_halo, 1)
+    own, own_gain = call(
+        own_kernel,
+        [on_chip(full), on_chip(plane)],
+        [SMEM] + [VMEM] * 4,
+        (weights, rows, vrows, halo, sibling),
+        scratch=shifts,
+        micros=0.8,
+    )
+    across = call(
+        after_kernel, on_chip(state.shape), [VMEM] * 2, (across, next_outer), aliases={0: 0}, micros=0.05
+    )
+    far = over_inst(across, 1)
+    across_next, across_gain, own = call(
+        across_kernel,
+        [on_chip(full), on_chip(plane), on_chip(full)],
+        [SMEM] + [VMEM] * 7,
+        (weights, rows, vrows, across_halo, across, sibling, own, own_gain),
+        scratch=shifts + halves,
+        micros=0.9,
+    )
+    next_rows, partial, to_sibling = call(
+        finish_kernel,
+        [on_chip(full)] * 3,
+        [SMEM] + [VMEM] * 5,
+        (weights, own, own_gain, across_next, across_gain, far),
+        scratch=halves,
     )
     from_sibling = over_inst(to_sibling, 1)
-
-    new, residual = pl.pallas_call(
-        last_kernel,
-        out_shape=[jax.ShapeDtypeStruct(state.shape, F32)] * 2,
-        in_specs=[SMEM, SMEM] + [VMEM] * 5,
-        out_specs=[VMEM] * 2,
-        scratch_shapes=[pltpu.VMEM((comps, 2, row_count, 128), F32)] * 2,
-    )(
-        frequency, block_count, hold(next_rows), hold(vrows), hold(next_halo), hold(partial),
-        hold(from_sibling),
+    total, rate = call(
+        pitchwise_kernel,
+        [on_chip(full), on_chip(plane)],
+        [VMEM] * 3 + [SMEM],
+        (next_rows, vrows, partial, weights),
+        scratch=shifts,
+        micros=0.6,
+    )
+    next_halo = call(
+        functools.partial(next_halo_kernel, space_total, cap),
+        on_chip(outer),
+        [SMEM, VMEM, SMEM] + [VMEM] * (2 + space_total),
+        (table, index, weights, next_outer, across_halo, far_halo, *next_received),
+        scratch=pool,
+    )
+    new, residual = call(
+        functools.partial(last_kernel, space_total, cap),
+        [jax.ShapeDtypeStruct(state.shape, F32)] * 2,
+        [SMEM] + [VMEM] * 6,
+        (table, next_rows, vrows, next_halo, total, rate, from_sibling),
+        scratch=[pltpu.VMEM((comps, 2, row_count, 128), F32)] * 2,
+        micros=1.5,
     )
     return new[None], residual[None]
 

time: 63.9 us -> 36 us (0.56)
  Pallas kernels: 18.5 us -> 6.52 us
  local copies, waits for them, and re-layouts: 10.5 us -> 1.53 us
  waiting for transfers between devices: 16.7 us -> 9.68 us
    pallas_call x6 -> x10, Pallas kernels: 18.5 us -> 6.52 us  [call(): pl.pallas_call(kernel, out_shape=out, in_specs=specs, out_specs=out_specs...]
    unnamed x31 -> x12, local copies, waits for them, and re-layouts: 10.5 us -> 1.53 us
    ppermute x7 -> x6, waiting for transfers between devices: 9.44 us -> 3.55 us  [over_inst(): return lax.ppermute(x, 'inst', [(i, i ^ flip) for i in range(4)])]
    ppermute x6, waiting for transfers between devices: 7.25 us -> 6.13 us  [over_space(): lax.ppermute(x, 'space', [(i, (i + k + 1) % space_total) for i in range(s...]
    ppermute x6, starting transfers between devices: 10.3 us -> 11.3 us  [over_space(): lax.ppermute(x, 'space', [(i, (i + k + 1) % space_total) for i in range(s...]
    ppermute x7 -> x6, starting transfers between devices: 6.04 us -> 5.41 us  [over_inst(): return lax.ppermute(x, 'inst', [(i, i ^ flip) for i in range(4)])]
  transfers between devices with their start and end apart: 13 -> 12, of which waited for: 8 -> 8; matrix products, arithmetic and copies ran while one was open for 0% -> 0% of each run, Pallas kernels for 1% -> 9%
where the time goes in v2:
time: 36 us; the launch traced here: 35.8 us
  starting transfers between devices  16.7 us (46%)
  waiting for transfers between devices  9.68 us (27%)
  Pallas kernels  6.52 us (18%)
  local copies, waits for them, and re-layouts  1.53 us (4%)
  between operations  1.41 us (4%)
    ppermute x6, starting transfers between devices, over_space(): lax.ppermute(x, 'space', [(i, (i + k + 1) % space_total) for i in range(s...  11.3 us
    pallas_call x10, Pallas kernels, call(): pl.pallas_call(kernel, out_shape=out, in_specs=specs, out_specs=out_specs...  6.52 us
    ppermute x6, waiting for transfers between devices, over_space(): lax.ppermute(x, 'space', [(i, (i + k + 1) % space_total) for i in range(s...  6.13 us
    ppermute x6, starting transfers between devices, over_inst(): return lax.ppermute(x, 'inst', [(i, i ^ flip) for i in range(4)])  5.41 us
    ppermute x6, waiting for transfers between devices, over_inst(): return lax.ppermute(x, 'inst', [(i, i ^ flip) for i in range(4)])  3.55 us
    unnamed x12, local copies, waits for them, and re-layouts  1.53 us
  transfers between devices with their start and end apart: 12, of which 8 were waited for; matrix products, arithmetic and copies ran while one was open for 0% of the time, Pallas kernels for 9%

profile of v2, /device:TPU:0, one launch (start us, length us, event | category | flops | bytes accessed | tf_op | source)
XLA Modules:
  0.0 35.8 jit_solution(2662691583532642456)
XLA Ops:
  1.3 0.0 copy-start.5
  1.3 0.0 copy-start.2
  1.3 0.0 copy-start.3
  1.3 0.0 copy-start.1
  1.3 0.0 copy-start.4
  1.3 0.6 %copy-done.5 = s32[8]{0:T(128)S(1)} copy-done((s32[8]{0:T(128)S(1)}, s32[8]{0:T(128)}, u32[]{:S(2)}) %copy-start.5) | copy-done | bytes 56
  1.9 0.0 copy-done.2
  2.0 0.0 copy-done.3
  2.0 0.0 copy-done.1
  2.0 0.0 copy-done.4
  2.0 0.0 copy-start
  2.0 0.8 %copy-done = f32[64,256]{1,0:T(8,128)S(1)} copy-done((f32[64,256]{1,0:T(8,128)S(1)}, f32[64,256]{1,0:T(8,128)}, u32[]{:S(2)}) %copy-start) | copy-done | bytes 65560
  2.8 1.8 %shard_map.95 = (f32[6,8,8,256]{3,2,1,0:T(8,128)S(1)}, f32[8,8,256]{2,1,0:T(8,128)S(1)}, f32[6,2,8,256]{3,2,1,0:T(8,128)S(1)}, s32[37]{0:T(128)S(4)}, f32[8]{0:T...) custom-call(f32[6,64,256]{2,1,0:T(8,128)} %bitcast.state_ref, ...), custom_call_target="tpu_custom_call" | custom-call | bytes 1 | tf_op jit(solution)/shard_map/pallas_call | solution.py:540
  4.7 0.5 %collective-permute-start.5 = (f32[6,8,8,256]{3,2,1,0:T(8,128)S(1)}, f32[6,8,8,256]{3,2,1,0:T(8,128)S(1)}, u32[]{:S(2)}, u32[]{:S(2)}) collective-permute-start(f32[6,8,8,256]{3,2,1,0:T(8,128)S(1)} %get-tuple-element.29.rows_ref), channel_id=1, source_target_pairs={{0,4},{4,0},{8,12},{12,8},{1,5},{5,1},{9,13},{13,9},{2,6},{6,2},{1... | collective-permute-start | bytes 1179656 | tf_op jit(solution)/shard_map/ppermute | solution.py:521
  5.2 2.6 %collective-permute-start.4 = (f32[6,64,256]{2,1,0:T(8,128)}, f32[6,64,256]{2,1,0:T(8,128)S(1)}, u32[]{:S(2)}, u32[]{:S(2)}) collective-permute-start(f32[6,64,256]{2,1,0:T(8,128)} %bitcast.state_ref), channel_id=1, source_target_pairs={{0,8},{4,12},{8,0},{12,4},{1,9},{5,13},{9,1},{13,5},{2,10},{6,14},... | collective-permute-start | bytes 1179656 | tf_op jit(solution)/shard_map/ppermute | solution.py:521
  7.8 1.6 %collective-permute-start = (f32[48,256]{1,0:T(8,128)S(1)}, f32[48,256]{1,0:T(8,128)S(1)}, u32[]{:S(2)}, u32[]{:S(2)}) collective-permute-start(f32[48,256]{1,0:T(8,128)S(1)} %get-tuple-element.33), channel_id=1, source_target_pairs={{0,1},{1,2},{2,3},{3,0},{4,5},{5,6},{6,7},{7,4},{8,9},{9,10},{10,1... | collective-permute-start | bytes 147464 | tf_op jit(solution)/shard_map/ppermute | solution.py:525
  9.3 2.6 %collective-permute-start.1 = (f32[48,256]{1,0:T(8,128)S(1)}, f32[48,256]{1,0:T(8,128)S(1)}, u32[]{:S(2)}, u32[]{:S(2)}) collective-permute-start(f32[48,256]{1,0:T(8,128)S(1)} %get-tuple-element.34), channel_id=1, source_target_pairs={{0,2},{1,3},{2,0},{3,1},{4,6},{5,7},{6,4},{7,5},{8,10},{9,11},{10,... | collective-permute-start | bytes 147464 | tf_op jit(solution)/shard_map/ppermute | solution.py:525
  11.9 1.3 %collective-permute-start.2 = (f32[48,256]{1,0:T(8,128)S(1)}, f32[48,256]{1,0:T(8,128)S(1)}, u32[]{:S(2)}, u32[]{:S(2)}) collective-permute-start(f32[48,256]{1,0:T(8,128)S(1)} %get-tuple-element.35), channel_id=1, source_target_pairs={{0,3},{1,0},{2,1},{3,2},{4,7},{5,4},{6,5},{7,6},{8,11},{9,8},{10,9... | collective-permute-start | bytes 147464 | tf_op jit(solution)/shard_map/ppermute | solution.py:525
  13.3 0.4 %collective-permute-done.more_0_ = f32[48,256]{1,0:T(8,128)S(1)} collective-permute-done((f32[48,256]{1,0:T(8,128)S(1)}, f32[48,256]{1,0:T(8,128)S(1)}, u32[]{:S(2)}, u32[]{:S(2)}) %collective-permute-start) | collective-permute-done | bytes 49184 | tf_op jit(solution)/shard_map/ppermute | solution.py:525
  13.7 2.2 %collective-permute-done.1.more_1_ = f32[48,256]{1,0:T(8,128)S(1)} collective-permute-done((f32[48,256]{1,0:T(8,128)S(1)}, f32[48,256]{1,0:T(8,128)S(1)}, u32[]{:S(2)}, u32[]{:S(2)}) %collective-permute-start.1) | collective-permute-done | bytes 49184 | tf_op jit(solution)/shard_map/ppermute | solution.py:525
  15.8 0.4 collective-permute-done.2.more_2_
  16.2 0.3 shard_map.96.halo_ref
  16.5 0.0 collective-permute-done.5.sibling_ref
  16.5 0.3 shard_map.97
  16.9 0.8 %collective-permute-done.4.value_ref = f32[6,64,256]{2,1,0:T(8,128)S(1)} collective-permute-done((f32[6,64,256]{2,1,0:T(8,128)}, f32[6,64,256]{2,1,0:T(8,128)S(1)}, u32[]{:S(2)}, u32[]{:S(2)}) %collective-permute-start.4) | collective-permute-done | bytes 393248 | tf_op jit(solution)/shard_map/ppermute | solution.py:521
  17.7 0.0 collective-permute-start.6
  17.7 1.8 %collective-permute-start.3 = (f32[6,2,8,256]{3,2,1,0:T(8,128)S(1)}, f32[6,2,8,256]{3,2,1,0:T(8,128)S(1)}, u32[]{:S(2)}, u32[]{:S(2)}) collective-permute-start(f32[6,2,8,256]{3,2,1,0:T(8,128)S(1)} %shard_map.96.halo_ref), channel_id=1, source_target_pairs={{0,8},{4,12},{8,0},{12,4},{1,9},{5,13},{9,1},{13,5},{2,10},{6,14},... | collective-permute-start | bytes 294920 | tf_op jit(solution)/shard_map/ppermute | solution.py:521
  19.4 0.8 %shard_map.99 = (f32[6,8,8,256]{3,2,1,0:T(8,128)S(1)}, f32[8,8,256]{2,1,0:T(8,128)S(1)}) custom-call(f32[8]{0:T(128)S(4)} %get-tuple-element.28.weight_ref, f32[6,8,8,256]{3,2,1,0:T(8,128)S(1)} %get-tuple-element.29.rows_ref, f32[8,8,256]{2,1,0:T(8,128)S(1)} %get-tuple-element.30.vrows_ref, f32[6,2,8,256]{3,2,1,0:T(8,128)S(1)} %shard_map.96.halo_ref, ...), custom_call_target="tpu_custom_call" | custom-call | bytes 1 | tf_op jit(solution)/shard_map/pallas_call | solution.py:540
  20.2 2.7 %collective-permute-done.3.halo_ref.across_ref = f32[6,2,8,256]{3,2,1,0:T(8,128)S(1)} collective-permute-done((f32[6,2,8,256]{3,2,1,0:T(8,128)S(1)}, f32[6,2,8,256]{3,2,1,0:T(8,128)S(1)}, u32[]{:S(2)}, u32[]{:S(2)}) %collective-permute-start.3) | collective-permute-done | bytes 98336 | tf_op jit(solution)/shard_map/ppermute | solution.py:521
  22.9 0.8 %shard_map.100 = (f32[6,8,8,256]{3,2,1,0:T(8,128)S(1)}, f32[8,8,256]{2,1,0:T(8,128)S(1)}, f32[6,8,8,256]{3,2,1,0:T(8,128)S(1)}) custom-call(f32[8]{0:T(128)S(4)} %get-tuple-element.28.weight_ref, f32[6,8,8,256]{3,2,1,0:T(8,128)S(1)} %get-tuple-element.29.rows_ref, f32[8,8,256]{2,1,0:T(8,128)S(1)} %get-tuple-element.30.vrows_ref, ...), custom_call_target="tpu_custom_call" | custom-call | bytes 1 | tf_op jit(solution)/shard_map/pallas_call | solution.py:540
  23.7 0.0 collective-permute-done.6.far_ref
  23.7 0.2 shard_map.101
  24.0 0.1 collective-permute-start.11
  24.1 0.5 %collective-permute-start.7 = (f32[6,2,8,256]{3,2,1,0:T(8,128)S(1)}, f32[6,2,8,256]{3,2,1,0:T(8,128)S(1)}, u32[]{:S(2)}, u32[]{:S(2)}) collective-permute-start(f32[6,2,8,256]{3,2,1,0:T(8,128)S(1)} %collective-permute-done.3.halo_ref.across_ref), channel_id=1, source_target_pairs={{0,4},{4,0},{8,12},{12,8},{1,5},{5,1},{9,13},{13,9},{2,6},{6,2},{1... | collective-permute-start | bytes 294920 | tf_op jit(solution)/shard_map/ppermute | solution.py:521
  24.6 1.8 %collective-permute-start.8 = (f32[56,256]{1,0:T(8,128)S(1)}, f32[56,256]{1,0:T(8,128)S(1)}, u32[]{:S(2)}, u32[]{:S(2)}) collective-permute-start(f32[56,256]{1,0:T(8,128)S(1)} %get-tuple-element.43), channel_id=1, source_target_pairs={{0,1},{1,2},{2,3},{3,0},{4,5},{5,6},{6,7},{7,4},{8,9},{9,10},{10,1... | collective-permute-start | bytes 172040 | tf_op jit(solution)/shard_map/ppermute | solution.py:525
  26.4 2.6 %collective-permute-start.9 = (f32[56,256]{1,0:T(8,128)S(1)}, f32[56,256]{1,0:T(8,128)S(1)}, u32[]{:S(2)}, u32[]{:S(2)}) collective-permute-start(f32[56,256]{1,0:T(8,128)S(1)} %get-tuple-element.44), channel_id=1, source_target_pairs={{0,2},{1,3},{2,0},{3,1},{4,6},{5,7},{6,4},{7,5},{8,10},{9,11},{10,... | collective-permute-start | bytes 172040 | tf_op jit(solution)/shard_map/ppermute | solution.py:525
  29.0 1.3 %collective-permute-start.10 = (f32[56,256]{1,0:T(8,128)S(1)}, f32[56,256]{1,0:T(8,128)S(1)}, u32[]{:S(2)}, u32[]{:S(2)}) collective-permute-start(f32[56,256]{1,0:T(8,128)S(1)} %get-tuple-element.45), channel_id=1, source_target_pairs={{0,3},{1,0},{2,1},{3,2},{4,7},{5,4},{6,5},{7,6},{8,11},{9,8},{10,9... | collective-permute-start | bytes 172040 | tf_op jit(solution)/shard_map/ppermute | solution.py:525
  30.3 0.0 collective-permute-done.7.far_ref
  30.3 0.3 collective-permute-done.8.more_0_
  30.7 2.5 %collective-permute-done.9.more_1_ = f32[56,256]{1,0:T(8,128)S(1)} collective-permute-done((f32[56,256]{1,0:T(8,128)S(1)}, f32[56,256]{1,0:T(8,128)S(1)}, u32[]{:S(2)}, u32[]{:S(2)}) %collective-permute-start.9) | collective-permute-done | bytes 57376 | tf_op jit(solution)/shard_map/ppermute | solution.py:525
  33.2 0.4 %collective-permute-done.10.more_2_ = f32[56,256]{1,0:T(8,128)S(1)} collective-permute-done((f32[56,256]{1,0:T(8,128)S(1)}, f32[56,256]{1,0:T(8,128)S(1)}, u32[]{:S(2)}, u32[]{:S(2)}) %collective-permute-start.10) | collective-permute-done | bytes 57376 | tf_op jit(solution)/shard_map/ppermute | solution.py:525
  33.6 0.3 shard_map.102.halo_ref
  33.9 0.5 %shard_map.103 = (f32[6,8,8,256]{3,2,1,0:T(8,128)S(1)}, f32[8,8,256]{2,1,0:T(8,128)S(1)}) custom-call(f32[6,8,8,256]{3,2,1,0:T(8,128)S(1)} %get-tuple-element.42.rows_ref, f32[8,8,256]{2,1,0:T(8,128)S(1)} %get-tuple-element.30.vrows_ref, f32[6,8,8,256]{3,2,1,0:T(8,128)S(1)} %get-tuple-element.46.partial_ref, f32[8]{0:T(128)S(4)} %get-tuple-element.28.weight_ref), custom_call_target="tpu_custom_call" | custom-call | bytes 1 | tf_op jit(solution)/shard_map/pallas_call | solution.py:540
  34.4 0.0 collective-permute-done.11.received_ref
  34.4 1.4 %shard_map.104 = (f32[6,64,256]{2,1,0:T(8,128)}, f32[6,64,256]{2,1,0:T(8,128)}) custom-call(s32[37]{0:T(128)S(4)} %get-tuple-element.27.table_ref, f32[6,8,8,256]{3,2,1,0:T(8,128)S(1)} %get-tuple-element.42.rows_ref, f32[8,8,256]{2,1,0:T(8,128)S(1)} %get-tuple-element.30.vrows_ref, f32[6,2,8,256]{3,2,1,0:T(8,128)S(1)} %shard_map.102.halo_ref, ...), custom_call_target="tpu_custom_call" | custom-call | bytes 1 | tf_op jit(solution)/shard_map/pallas_call | solution.py:540
  (1 shorter events, 0.0 us)
Async XLA Ops:
  1.3 0.7 %copy-start.5 = (s32[8]{0:T(128)S(1)}, s32[8]{0:T(128)}, u32[]{:S(2)}) copy-start(s32[8]{0:T(128)} %place_ref.1) | copy-start | bytes 100
  1.3 0.7 %copy-start.2 = (s32[8,2]{0,1:T(2,128)S(1)}, s32[8,2]{0,1:T(2,128)}, u32[]{:S(2)}) copy-start(s32[8,2]{0,1:T(2,128)} %param.14) | copy-start | bytes 196
  1.3 0.7 %copy-start.3 = (s32[8,2]{0,1:T(2,128)S(1)}, s32[8,2]{0,1:T(2,128)}, u32[]{:S(2)}) copy-start(s32[8,2]{0,1:T(2,128)} %param.15) | copy-start | bytes 196
  1.3 0.7 %copy-start.1 = (s32[8,2]{0,1:T(2,128)S(1)}, s32[8,2]{0,1:T(2,128)}, u32[]{:S(2)}) copy-start(s32[8,2]{0,1:T(2,128)} %param.13) | copy-start | bytes 196
  1.3 0.7 %copy-start.4 = (s32[4]{0:T(128)S(1)}, s32[4]{0:T(128)}, u32[]{:S(2)}) copy-start(s32[4]{0:T(128)} %counts_ref.1) | copy-start | bytes 52
  2.0 0.8 %copy-start = (f32[64,256]{1,0:T(8,128)S(1)}, f32[64,256]{1,0:T(8,128)}, u32[]{:S(2)}) copy-start(f32[64,256]{1,0:T(8,128)} %volume_ref.1) | copy-start | bytes 196612
  4.7 11.8 %collective-permute-start.5 = (f32[6,8,8,256]{3,2,1,0:T(8,128)S(1)}, f32[6,8,8,256]{3,2,1,0:T(8,128)S(1)}, u32[]{:S(2)}, u32[]{:S(2)}) collective-permute-start(f32[6,8,8,256]{3,2,1,0:T(8,128)S(1)} %get-tuple-element.29.rows_ref), channel_id=1, source_target_pairs={{0,4},{4,0},{8,12},{12,8},{1,5},{5,1},{9,13},{13,9},{2,6},{6,2},{1... | collective-permute-start | bytes 1179656 | tf_op jit(solution)/shard_map/ppermute | solution.py:521
  5.2 12.5 %collective-permute-start.4 = (f32[6,64,256]{2,1,0:T(8,128)}, f32[6,64,256]{2,1,0:T(8,128)S(1)}, u32[]{:S(2)}, u32[]{:S(2)}) collective-permute-start(f32[6,64,256]{2,1,0:T(8,128)} %bitcast.state_ref), channel_id=1, source_target_pairs={{0,8},{4,12},{8,0},{12,4},{1,9},{5,13},{9,1},{13,5},{2,10},{6,14},... | collective-permute-start | bytes 1179656 | tf_op jit(solution)/shard_map/ppermute | solution.py:521
  7.8 5.9 %collective-permute-start = (f32[48,256]{1,0:T(8,128)S(1)}, f32[48,256]{1,0:T(8,128)S(1)}, u32[]{:S(2)}, u32[]{:S(2)}) collective-permute-start(f32[48,256]{1,0:T(8,128)S(1)} %get-tuple-element.33), channel_id=1, source_target_pairs={{0,1},{1,2},{2,3},{3,0},{4,5},{5,6},{6,7},{7,4},{8,9},{9,10},{10,1... | collective-permute-start | bytes 147464 | tf_op jit(solution)/shard_map/ppermute | solution.py:525
  9.3 6.5 %collective-permute-start.1 = (f32[48,256]{1,0:T(8,128)S(1)}, f32[48,256]{1,0:T(8,128)S(1)}, u32[]{:S(2)}, u32[]{:S(2)}) collective-permute-start(f32[48,256]{1,0:T(8,128)S(1)} %get-tuple-element.34), channel_id=1, source_target_pairs={{0,2},{1,3},{2,0},{3,1},{4,6},{5,7},{6,4},{7,5},{8,10},{9,11},{10,... | collective-permute-start | bytes 147464 | tf_op jit(solution)/shard_map/ppermute | solution.py:525
  11.9 4.3 %collective-permute-start.2 = (f32[48,256]{1,0:T(8,128)S(1)}, f32[48,256]{1,0:T(8,128)S(1)}, u32[]{:S(2)}, u32[]{:S(2)}) collective-permute-start(f32[48,256]{1,0:T(8,128)S(1)} %get-tuple-element.35), channel_id=1, source_target_pairs={{0,3},{1,0},{2,1},{3,2},{4,7},{5,4},{6,5},{7,6},{8,11},{9,8},{10,9... | collective-permute-start | bytes 147464 | tf_op jit(solution)/shard_map/ppermute | solution.py:525
  17.7 6.1 %collective-permute-start.6 = (f32[6,64,256]{2,1,0:T(8,128)S(1)}, f32[6,64,256]{2,1,0:T(8,128)S(1)}, u32[]{:S(2)}, u32[]{:S(2)}) collective-permute-start(f32[6,64,256]{2,1,0:T(8,128)S(1)} %shard_map.98.across_ref), channel_id=1, source_target_pairs={{0,4},{4,0},{8,12},{12,8},{1,5},{5,1},{9,13},{13,9},{2,6},{6,2},{1... | collective-permute-start | bytes 1179656 | tf_op jit(solution)/shard_map/ppermute | solution.py:521
  17.7 5.2 %collective-permute-start.3 = (f32[6,2,8,256]{3,2,1,0:T(8,128)S(1)}, f32[6,2,8,256]{3,2,1,0:T(8,128)S(1)}, u32[]{:S(2)}, u32[]{:S(2)}) collective-permute-start(f32[6,2,8,256]{3,2,1,0:T(8,128)S(1)} %shard_map.96.halo_ref), channel_id=1, source_target_pairs={{0,8},{4,12},{8,0},{12,4},{1,9},{5,13},{9,1},{13,5},{2,10},{6,14},... | collective-permute-start | bytes 294920 | tf_op jit(solution)/shard_map/ppermute | solution.py:521
  24.0 10.4 %collective-permute-start.11 = (f32[6,8,8,256]{3,2,1,0:T(8,128)S(1)}, f32[6,8,8,256]{3,2,1,0:T(8,128)S(1)}, u32[]{:S(2)}, u32[]{:S(2)}) collective-permute-start(f32[6,8,8,256]{3,2,1,0:T(8,128)S(1)} %get-tuple-element.49), channel_id=1, source_target_pairs={{0,4},{4,0},{8,12},{12,8},{1,5},{5,1},{9,13},{13,9},{2,6},{6,2},{1... | collective-permute-start | bytes 1179656 | tf_op jit(solution)/shard_map/ppermute | solution.py:521
  24.1 6.3 %collective-permute-start.7 = (f32[6,2,8,256]{3,2,1,0:T(8,128)S(1)}, f32[6,2,8,256]{3,2,1,0:T(8,128)S(1)}, u32[]{:S(2)}, u32[]{:S(2)}) collective-permute-start(f32[6,2,8,256]{3,2,1,0:T(8,128)S(1)} %collective-permute-done.3.halo_ref.across_ref), channel_id=1, source_target_pairs={{0,4},{4,0},{8,12},{12,8},{1,5},{5,1},{9,13},{13,9},{2,6},{6,2},{1... | collective-permute-start | bytes 294920 | tf_op jit(solution)/shard_map/ppermute | solution.py:521
  24.6 6.1 %collective-permute-start.8 = (f32[56,256]{1,0:T(8,128)S(1)}, f32[56,256]{1,0:T(8,128)S(1)}, u32[]{:S(2)}, u32[]{:S(2)}) collective-permute-start(f32[56,256]{1,0:T(8,128)S(1)} %get-tuple-element.43), channel_id=1, source_target_pairs={{0,1},{1,2},{2,3},{3,0},{4,5},{5,6},{6,7},{7,4},{8,9},{9,10},{10,1... | collective-permute-start | bytes 172040 | tf_op jit(solution)/shard_map/ppermute | solution.py:525
  26.4 6.8 %collective-permute-start.9 = (f32[56,256]{1,0:T(8,128)S(1)}, f32[56,256]{1,0:T(8,128)S(1)}, u32[]{:S(2)}, u32[]{:S(2)}) collective-permute-start(f32[56,256]{1,0:T(8,128)S(1)} %get-tuple-element.44), channel_id=1, source_target_pairs={{0,2},{1,3},{2,0},{3,1},{4,6},{5,7},{6,4},{7,5},{8,10},{9,11},{10,... | collective-permute-start | bytes 172040 | tf_op jit(solution)/shard_map/ppermute | solution.py:525
  29.0 4.6 %collective-permute-start.10 = (f32[56,256]{1,0:T(8,128)S(1)}, f32[56,256]{1,0:T(8,128)S(1)}, u32[]{:S(2)}, u32[]{:S(2)}) collective-permute-start(f32[56,256]{1,0:T(8,128)S(1)} %get-tuple-element.45), channel_id=1, source_target_pairs={{0,3},{1,0},{2,1},{3,2},{4,7},{5,4},{6,5},{7,6},{8,11},{9,8},{10,9... | collective-permute-start | bytes 172040 | tf_op jit(solution)/shard_map/ppermute | solution.py:525

commit v3 on v2

--- a/solution.py
+++ b/solution.py
@@ -25,6 +25,7 @@
 F32 = jnp.float32
 VMEM = pl.BlockSpec(memory_space=pltpu.VMEM)
 SMEM = pl.BlockSpec(memory_space=pltpu.SMEM)
+HBM = pl.BlockSpec(memory_space=pltpu.HBM)
 
 
 def spectral_weights(total):
@@ -36,6 +37,18 @@
         second = -sign / (2.0 * math.sin(angle) ** 2)
         weights.append(first - TIME_VISCOSITY * second)
     return weights
+
+
+def exchanges(total):
+    return [2, 3, 1] if total == 4 else list(range(1, total))
+
+
+def partner(device, k, total):
+    return device ^ k if total & (total - 1) == 0 else (device + k) % total
+
+
+def apart(device, source, total):
+    return device ^ source if total & (total - 1) == 0 else (device - source + total) % total
 
 
 def pair_cap(space_total, block_total):
@@ -173,7 +186,7 @@
                 rows_ref[c, r, :, pl.ds(128 * h, 128)] = half_ref[c, h, pl.ds(r, 8, stride=8), :]
 
 
-def put_coefficients(frequency_ref, weight_ref):
+def weight_kernel(frequency_ref, weight_ref):
     weights = spectral_weights(4)
     omega = frequency_ref[0]
     even = lax.axis_index("inst") % 2 == 0
@@ -194,24 +207,26 @@
 
 def pack_kernel(
     space_total, block_total, cap,
-    state_ref, volume_ref, frequency_ref, counts_ref, place_ref, links_ref, offset_ref, flip_ref,
-    rows_ref, vrows_ref, outer_ref, table_ref, weight_ref, index_ref, *more
+    state_ref, volume_ref, counts_in, place_in, links_in, offset_in, flip_in,
+    rows_ref, vrows_ref, outer_ref, table_ref, index_ref, *more
 ):
     sends = more[: space_total - 1]
-    half_ref, arrival, first_ref, inverse_ref = more[space_total - 1 :]
+    half_ref, arrival, first_ref, inverse_ref, *small = more[space_total - 1 :]
+    counts_ref, place_ref, links_ref, offset_ref, flip_ref = small
     width = state_ref.shape[2]
-    copies = []
+    moves = list(zip([counts_in, place_in, links_in, offset_in, flip_in], small))
     for h in range(2):
         lanes = pl.ds(128 * h, 128)
-        for n, (source, target) in enumerate(
-            [
-                (state_ref.at[:, :, lanes], half_ref.at[h, pl.ds(0, COMPS)]),
-                (volume_ref.at[:, lanes], half_ref.at[h, COMPS]),
-            ]
-        ):
-            copies.append(pltpu.make_async_copy(source, target, arrival.at[2 * h + n]))
-            copies[-1].start()
-    put_coefficients(frequency_ref, weight_ref)
+        moves.append((state_ref.at[:, :, lanes], half_ref.at[h, pl.ds(0, COMPS)]))
+        moves.append((volume_ref.at[:, lanes], half_ref.at[h, COMPS]))
+    copies = [
+        pltpu.make_async_copy(source, target, arrival.at[n])
+        for n, (source, target) in enumerate(moves)
+    ]
+    for copy in copies:
+        copy.start()
+    for copy in copies[: len(small)]:
+        copy.wait()
     me = lax.axis_index("space")
     total = jnp.int32(0)
     firsts = []
@@ -246,7 +261,7 @@
         slot, side = f // 2, f % 2
         block = block_in(me, slot)
         link, owner, source = source_of(block, side)
-        shift = lax.rem(me - owner + space_total, space_total)
+        shift = apart(me, owner, space_total)
         listed = 2 * counts_ref[owner] <= cap
         place = jnp.where(listed, jnp.minimum(source, cap - 1), min(f, cap - 1))
         outside = link < 0
@@ -261,12 +276,12 @@
     column = lax.broadcasted_iota(jnp.int32, (FACES, width), 1)
     index_ref[...] = (start + jnp.where(turned == 1, width - 1 - column, column)) % width
     for k in range(1, space_total):
-        target = lax.rem(me + k, space_total)
+        target = partner(me, k, space_total)
         for i in range(cap):
             _, owner, source = source_of(block_in(target, i // 2), i % 2)
             wanted = jnp.where(owner == me, source, 0)
             table_ref[3 * FACES + (k - 1) * cap + i] = jnp.where(few, i, wanted)
-    for copy in copies:
+    for copy in copies[len(small) :]:
         copy.wait()
     for c in range(COMPS + 1):
         for r in range(8):
@@ -295,8 +310,8 @@
 
 def permuted_halos(space_total, cap, table_ref, index_ref, outer_ref, received, pool_ref, raw_ref):
     comps = outer_ref.shape[0]
-    for k, part in enumerate(received):
-        pool_ref[pl.ds(k * POOLED * 2 * cap, comps * 2 * cap), :] = part[...]
+    for k, part in zip(exchanges(len(received) + 1), received):
+        pool_ref[pl.ds((k - 1) * POOLED * 2 * cap, comps * 2 * cap), :] = part[...]
     own_base = (space_total - 1) * POOLED * 2 * cap
     for c in range(comps):
         for l in range(2):
@@ -321,7 +336,7 @@
                 yield c, l, h, jnp.where(masks[h], a, b)
 
 
-def halo_kernel(space_total, cap, table_ref, index_ref, outer_ref, *more):
+def halo_kernel(space_total, cap, table_ref, index_ref, outer_ref, _, __, *more):
     received, (halo_ref, pool_ref, raw_ref) = more[: space_total - 1], more[space_total - 1 :]
     for c, l, h, halo in permuted_halos(
         space_total, cap, table_ref, index_ref, outer_ref, received, pool_ref, raw_ref
@@ -330,9 +345,11 @@
 
 
 def next_halo_kernel(
-    space_total, cap, table_ref, index_ref, weight_ref, outer_ref, across_ref, far_ref, *more
-):
-    received, (halo_ref, pool_ref, raw_ref) = more[: space_total - 1], more[space_total - 1 :]
+    space_total, cap, table_ref, index_ref, weight_ref, outer_ref, across_ref, _, *more
+):
+    received, halos = more[: space_total - 1], more[space_total - 1 : -4]
+    halo_ref, pool_ref, raw_ref, far_ref = more[-4:]
+    join_halos(halos, far_ref)
     omega, w_own, w_across, w_near, w_far = coefficients(weight_ref)
     gain = {}
     for c, l, h, halo in permuted_halos(
@@ -346,10 +363,30 @@
         halo_ref[c, l, :, lanes] = halo - gain[l, h] * lacking
 
 
+def pitchwise_kernel(weight_ref, rows_ref, vrows_ref, *more):
+    part_ref, rate_ref, near_ref, lower_ref = more[-4:]
+    pitchwise(lambda c, r: rows_ref[c, r], vrows_ref, weight_ref[0], part_ref, rate_ref, near_ref, lower_ref)
+
+
+def pitchwise(load, vrows_ref, omega, part_ref, rate_ref, near_ref, lower_ref):
+    pitchwise_shifts(load, near_ref)
+    for r in range(8):
+        q = [load(c, r) for c in range(COMPS)]
+        u, v, p = primitives(q)
+        upper, lower = pitchwise_faces(q, v, p, near_ref, r)
+        rate_ref[r] = own_instance_rate(jnp.abs(u) + jnp.abs(v), vrows_ref[r], omega)
+        for c in range(COMPS):
+            part_ref[c, r] = upper[c]
+            lower_ref[c, r] = lower[c]
+    for r in range(8):
+        for c in range(COMPS):
+            part_ref[c, r] = part_ref[c, r] - turn(lower_ref[c, r], 1)
+
+
 def outer_kernel(
-    cap, table_ref, weight_ref, rows_ref, vrows_ref, halo_ref, sibling_ref, outer_ref, *more
-):
-    sends, near_ref, lower_ref = more[:-2], more[-2], more[-1]
+    cap, table_ref, weight_ref, rows_ref, vrows_ref, part_ref, rate_ref, halo_ref, sibling_ref,
+    outer_ref, *sends
+):
     omega, w_own, w_across, w_near, w_far = coefficients(weight_ref)
     load = row_loader(lambda c, r: rows_ref[c, r], halo_ref)
     even = even_tiles(vrows_ref.shape[1:])
@@ -359,123 +396,109 @@
         k: [jnp.where(even, a, b) for a, b in zip(low[k - 2], high[k + 4])] for k in range(6)
     }
     rows = Rows(lambda k: picked[k])
-    for c in range(COMPS):
-        for l in range(2):
-            q = picked[l + 2][c]
-            near_ref[0, c, l] = turn(q, -1)
-            near_ref[1, c, l] = turn(q, -2)
-            near_ref[2, c, l] = turn(q, 1)
-    rates = []
     for l in range(2):
-        q = picked[l + 2]
-        u, v, p = rows.uvp(l + 2)
-        upper, lower = pitchwise_faces(q, v, p, near_ref, l)
         along = rows.along(l + 2)
         volume = jnp.where(even, vrows_ref[l], vrows_ref[l + 6])
-        rate = own_instance_rate(jnp.abs(u) + jnp.abs(v), volume, omega)
-        rates.append(rate)
+        rate = jnp.where(even, rate_ref[l], rate_ref[l + 6])
         outer_ref[COMPS, l] = rate * volume
         for c in range(COMPS):
+            q = picked[l + 2][c]
+            part = jnp.where(even, part_ref[c, l], part_ref[c, l + 6])
             sibling = jnp.where(even, sibling_ref[c, l], sibling_ref[c, l + 6])
-            spectral = w_own * q[c] + w_near * sibling
-            outer_ref[c, l] = q[c] - rate * (along[c] + upper[c] + volume * spectral)
-            lower_ref[c, l] = lower[c]
-    for l in range(2):
-        for c in range(COMPS):
-            outer_ref[c, l] = outer_ref[c, l] + rates[l] * turn(lower_ref[c, l], 1)
+            spectral = w_own * q + w_near * sibling
+            outer_ref[c, l] = q - rate * (along[c] + part + volume * spectral)
     pack_sends(cap, outer_ref, table_ref, sends)
 
 
-def sweep(load, halo_ref, vrows_ref, omega, term, next_ref, near_ref, lower_ref, rate_ref):
-    pitchwise_shifts(load, near_ref)
+def near_kernel(
+    weight_ref, vrows_ref,
+    rows_ref, part_ref, rate_ref, halo_ref,
+    sibling_ref, sibling_part_ref, sibling_rate_ref, sibling_halo_ref, _,
+    next_ref, sibling_next_ref, gain_ref, sibling_gain_ref
+):
+    omega, w_own, w_across, w_near, w_far = coefficients(weight_ref)
+    for one, other, weight, part, rate_of, halo, out, gain in (
+        (rows_ref, sibling_ref, w_near, part_ref, rate_ref, halo_ref, next_ref, gain_ref),
+        (sibling_ref, rows_ref, w_far, sibling_part_ref, sibling_rate_ref, sibling_halo_ref,
+         sibling_next_ref, sibling_gain_ref),
+    ):
+        rows = Rows(row_loader(lambda c, r: one[c, r], halo))
+        for r in range(8):
+            along, volume, rate = rows.along(r), vrows_ref[r], rate_of[r]
+            gain[r] = rate * volume
+            for c in range(COMPS):
+                spectral = w_own * one[c, r] + weight * other[c, r]
+                out[c, r] = one[c, r] - rate * (along[c] + part[c, r] + volume * spectral)
+
+
+def across_kernel(
+    weight_ref, vrows_ref, rows_ref, sibling_ref, own_ref, own_gain_ref, sibling_next_ref,
+    sibling_gain_ref, raw_ref, halo_ref,
+    next_ref, term_ref, across_ref, lacking_ref, gain_ref,
+    near_ref, lower_ref, half_ref, part_ref, rate_ref
+):
+    omega, w_own, w_across, w_near, w_far = coefficients(weight_ref)
+    rows_from(raw_ref, half_ref, across_ref)
+    load = lambda c, r: across_ref[c, r]
+    pitchwise(load, vrows_ref, omega, part_ref, rate_ref, near_ref, lower_ref)
     rows = Rows(row_loader(load, halo_ref))
     for r in range(8):
-        q = rows.q(r)
-        u, v, p = rows.uvp(r)
-        upper, lower = pitchwise_faces(q, v, p, near_ref, r)
-        along = rows.along(r)
-        volume = vrows_ref[r]
-        rate = own_instance_rate(jnp.abs(u) + jnp.abs(v), volume, omega)
-        rate_ref[r] = rate
+        along, volume, rate = rows.along(r), vrows_ref[r], rate_ref[r]
+        own_gain, sibling_gain, gain = own_gain_ref[r], sibling_gain_ref[r], rate * volume
+        gain_ref[r] = (
+            (w_own * w_far) * own_gain + (w_near * w_across) * sibling_gain + (w_across * w_near) * gain
+        )
+        lacking_ref[r] = w_far * own_gain
         for c in range(COMPS):
-            next_ref[c, r] = q[c] - rate * (along[c] + upper[c] + volume * term(c, r, q[c]))
-            lower_ref[c, r] = lower[c]
+            q = across_ref[c, r]
+            spectral = w_own * q + w_across * rows_ref[c, r] + w_far * sibling_ref[c, r]
+            new = q - rate * (along[c] + part_ref[c, r] + volume * spectral)
+            mine = own_ref[c, r] - (w_across * own_gain) * q
+            sibling = sibling_next_ref[c, r] - (w_near * sibling_gain) * q
+            next_ref[c, r] = mine
+            term_ref[c, r] = w_own * mine + w_near * sibling + w_across * new
+
+
+def far_pitchwise_kernel(
+    weight_ref, vrows_ref, raw_ref, rows_ref, part_ref, rate_ref, near_ref, lower_ref, half_ref
+):
+    rows_from(raw_ref, half_ref, rows_ref)
+    load = lambda c, r: rows_ref[c, r]
+    pitchwise(load, vrows_ref, weight_ref[0], part_ref, rate_ref, near_ref, lower_ref)
+
+
+def far_kernel(
+    weight_ref, vrows_ref, rows_ref, sibling_ref, across_ref, own_ref, partial_ref,
+    lacking_ref, lacking_term_ref, far_ref, part_ref, rate_ref, *more
+):
+    halos, (next_ref, term_ref, halo_ref) = more[:-3], more[-3:]
+    omega, w_own, w_across, w_near, w_far = coefficients(weight_ref)
+    join_halos(halos, halo_ref)
+    rows = Rows(row_loader(lambda c, r: far_ref[c, r], halo_ref))
     for r in range(8):
-        rate = rate_ref[r]
+        along, volume, rate = rows.along(r), vrows_ref[r], rate_ref[r]
+        lacking, lacking_term = lacking_ref[r], lacking_term_ref[r]
         for c in range(COMPS):
-            next_ref[c, r] = next_ref[c, r] + rate * turn(lower_ref[c, r], 1)
-
-
-def own_kernel(
-    weight_ref, rows_ref, vrows_ref, halo_ref, sibling_ref,
-    next_ref, gain_ref, near_ref, lower_ref
-):
-    omega, w_own, w_across, w_near, w_far = coefficients(weight_ref)
-    sweep(
-        lambda c, r: rows_ref[c, r], halo_ref, vrows_ref, omega,
-        lambda c, r, q: w_own * q + w_near * sibling_ref[c, r],
-        next_ref, near_ref, lower_ref, gain_ref,
-    )
-    for r in range(8):
-        gain_ref[r] = gain_ref[r] * vrows_ref[r]
-
-
-def across_kernel(
-    weight_ref, rows_ref, vrows_ref, halo_ref, across_ref, sibling_ref, own_ref, own_gain_ref,
-    next_ref, gain_ref, own_next_ref, near_ref, lower_ref, half_ref, state_ref
-):
-    omega, w_own, w_across, w_near, w_far = coefficients(weight_ref)
-    rows_from(across_ref, half_ref, state_ref)
-    sweep(
-        lambda c, r: state_ref[c, r], halo_ref, vrows_ref, omega,
-        lambda c, r, q: w_own * q + w_across * rows_ref[c, r] + w_far * sibling_ref[c, r],
-        next_ref, near_ref, lower_ref, gain_ref,
-    )
-    for r in range(8):
-        gain_ref[r] = gain_ref[r] * vrows_ref[r]
-        gain = own_gain_ref[r] * w_across
-        for c in range(COMPS):
-            own_next_ref[c, r] = own_ref[c, r] - gain * state_ref[c, r]
-
-
-def finish_kernel(
-    weight_ref, own_ref, own_gain_ref, across_ref, across_gain_ref, far_ref,
-    next_ref, partial_ref, send_ref, half_ref, state_ref
-):
-    omega, w_own, w_across, w_near, w_far = coefficients(weight_ref)
-    rows_from(far_ref, half_ref, state_ref)
-    for r in range(8):
-        own_gain, across_gain = own_gain_ref[r] * w_far, across_gain_ref[r] * w_near
-        for c in range(COMPS):
-            far = state_ref[c, r]
-            mine = own_ref[c, r] - own_gain * far
-            other = across_ref[c, r] - across_gain * far
-            next_ref[c, r] = mine
-            partial_ref[c, r] = w_own * mine + w_across * other
-            send_ref[c, r] = w_far * mine + w_near * other
-
-
-def pitchwise_kernel(
-    rows_ref, vrows_ref, partial_ref, weight_ref, sum_ref, rate_ref, near_ref, lower_ref
-):
-    load = lambda c, r: rows_ref[c, r]
-    pitchwise_shifts(load, near_ref)
-    for r in range(8):
-        q = [load(c, r) for c in range(COMPS)]
-        u, v, p = primitives(q)
-        upper, lower = pitchwise_faces(q, v, p, near_ref, r)
-        volume = vrows_ref[r]
-        rate_ref[r] = own_instance_rate(jnp.abs(u) + jnp.abs(v), volume, weight_ref[0])
-        for c in range(COMPS):
-            sum_ref[c, r] = upper[c] + volume * partial_ref[c, r]
-            lower_ref[c, r] = lower[c]
-    for r in range(8):
-        for c in range(COMPS):
-            sum_ref[c, r] = sum_ref[c, r] - turn(lower_ref[c, r], 1)
+            q = far_ref[c, r]
+            spectral = (
+                w_own * q + w_across * sibling_ref[c, r] + w_near * rows_ref[c, r]
+                + w_far * across_ref[c, r]
+            )
+            new = q - rate * (along[c] + part_ref[c, r] + volume * spectral)
+            next_ref[c, r] = own_ref[c, r] - lacking * q
+            term_ref[c, r] = partial_ref[c, r] - lacking_term * q + w_far * new
+
+
+def join_halos(parts, halo_ref):
+    size = COMPS // len(parts)
+    for n, part in enumerate(parts):
+        for c in range(size):
+            for l in range(2):
+                halo_ref[n * size + c, l] = part[c, l]
 
 
 def last_kernel(
-    space_total, cap, table_ref, rows_ref, vrows_ref, halo_ref, sum_ref, rate_ref, received_ref,
+    space_total, cap, table_ref, rows_ref, vrows_ref, halo_ref, part_ref, rate_ref, term_ref,
     new_ref, residual_ref, new_half_ref, residual_half_ref
 ):
     own = Rows(row_loader(lambda c, r: rows_ref[c, r], halo_ref))
@@ -487,7 +510,7 @@
         rate = rate_ref[r]
         inverse = 1.0 / volume
         for c in range(COMPS):
-            residual = sum_ref[c, r] + along[c] + volume * received_ref[c, r]
+            residual = part_ref[c, r] + along[c] + volume * term_ref[c, r]
             new = jnp.where(live, own.q(r)[c] - rate * residual, 0.0)
             scaled = jnp.where(live, residual * inverse, 0.0)
             for h in range(2):
@@ -500,12 +523,8 @@
             residual_ref[c, :, pl.ds(128 * h, 128)] = residual_half_ref[c, h]
 
 
-def after_kernel(value_ref, first_ref, out_ref):
+def after_kernel(value_ref, *more):
     pass
-
-
-def hold(x):
-    return pltpu.with_memory_space_constraint(x, pltpu.VMEM)
 
 
 def four_instances(
@@ -521,10 +540,13 @@
         return lax.ppermute(x, "inst", [(i, i ^ flip) for i in range(4)])
 
     def over_space(parts):
-        return [
-            lax.ppermute(x, "space", [(i, (i + k + 1) % space_total) for i in range(space_total)])
-            for k, x in enumerate(parts)
-        ]
+        arrived = {
+            k: lax.ppermute(
+                parts[k - 1], "space", [(i, partner(i, k, space_total)) for i in range(space_total)]
+            )
+            for k in exchanges(space_total)
+        }
+        return [arrived[k] for k in exchanges(space_total)]
 
     full = (comps, 8, 8, width)
     outer = (comps, 2, 8, width)
@@ -536,7 +558,9 @@
     shifts = [pltpu.VMEM((3,) + full, F32), pltpu.VMEM(full, F32)]
 
     def call(kernel, out, specs, args, scratch=(), micros=0.3, out_specs=None, aliases={}):
-        args = [hold(x) if spec is VMEM else x for spec, x in zip(specs, args)]
+        args = [
+            pltpu.with_memory_space_constraint(x, spec.memory_space) for spec, x in zip(specs, args)
+        ]
         return pl.pallas_call(
             kernel,
             out_shape=out,
@@ -544,110 +568,132 @@
             out_specs=out_specs or jax.tree.map(lambda _: VMEM, out),
             scratch_shapes=list(scratch),
             input_output_aliases=aliases,
-            compiler_params=pltpu.CompilerParams(vmem_limit_bytes=8 << 20),
+            compiler_params=pltpu.CompilerParams(vmem_limit_bytes=12 << 20),
             cost_estimate=pl.CostEstimate(
-                flops=0, bytes_accessed=1, transcendentals=0
+                flops=0, bytes_accessed=int(micros * 3.69e6), transcendentals=0
             ),
         )(*args)
 
-    in_smem = lambda x: pltpu.with_memory_space_constraint(x, pltpu.SMEM)
-    far_off = pl.BlockSpec(memory_space=pltpu.HBM)
     packed = call(
         functools.partial(pack_kernel, space_total, block_total, cap),
         [
             on_chip(full), on_chip(plane), on_chip(outer),
-            pltpu.SMEM((entries,), jnp.int32), pltpu.SMEM((8,), F32),
+            pltpu.SMEM((entries,), jnp.int32),
             on_chip((FACES, width), jnp.int32), *sends_shape(comps),
         ],
-        [far_off] * 2 + [SMEM] * 6,
-        (state, cell_volume, frequency, block_count, block_place, face_links.T, face_offset.T, face_flip.T),
+        [HBM] * 7,
+        (state, cell_volume, block_count, block_place, face_links.T, face_offset.T, face_flip.T),
         scratch=[
             pltpu.VMEM((2, comps + 1, row_count, 128), F32),
-            pltpu.SemaphoreType.DMA((4,)),
+            pltpu.SemaphoreType.DMA((9,)),
             pltpu.SMEM((space_total,), jnp.int32),
             pltpu.SMEM((block_total,), jnp.int32),
+            pltpu.SMEM((space_total,), jnp.int32),
+            pltpu.SMEM((block_total,), jnp.int32),
+            *[pltpu.SMEM((2, block_total), jnp.int32)] * 3,
         ],
         micros=2.0,
-        out_specs=[VMEM] * 3 + [SMEM] * 2 + [VMEM] * space_total,
-    )
-    rows, vrows, outer_rows, table, weights, index = packed[:6]
-    sends = packed[6:]
-    table, weights = in_smem(table), in_smem(weights)
+        out_specs=[VMEM] * 3 + [SMEM] + [VMEM] * space_total,
+    )
+    rows, vrows, outer_rows, table, index = packed[:5]
+    sends = packed[5:]
+    weights = pl.pallas_call(
+        weight_kernel, out_shape=pltpu.SMEM((8,), F32), in_specs=[SMEM], out_specs=SMEM
+    )(frequency)
     halves = [pltpu.VMEM((comps, 2, row_count, 128), F32), pltpu.VMEM(full, F32)]
     pool = [
         pltpu.VMEM(((space_total - 1) * POOLED * 2 * cap + POOLED * 2 * FACES, width), F32),
         pltpu.VMEM(pooled, F32),
     ]
 
+    def pitch(x, *first):
+        return call(
+            pitchwise_kernel,
+            [on_chip(full), on_chip(plane)],
+            [SMEM] + [VMEM] * (2 + len(first)),
+            (weights, x, vrows, *first),
+            scratch=shifts,
+            micros=0.5,
+        )
+
     across = over_inst(state, 2)
     sibling = over_inst(rows, 1)
     received = over_space(sends)
+    part, rate = pitch(rows)
+    sibling_part, sibling_rate = pitch(sibling, across)
     halo = call(
         functools.partial(halo_kernel, space_total, cap),
         on_chip(outer),
-        [SMEM] + [VMEM] * (1 + space_total),
-        (table, index, outer_rows, *received),
+        [SMEM] + [VMEM] * (3 + space_total),
+        (table, index, outer_rows, rate, sibling_rate, *received),
         scratch=pool,
     )
     across_halo = over_inst(halo, 2)
+    sibling_halo = over_inst(halo, 1)
     next_outer, *next_sends = call(
         functools.partial(outer_kernel, cap),
         [on_chip(pooled), *sends_shape(POOLED)],
-        [SMEM, SMEM] + [VMEM] * 4,
-        (table, weights, rows, vrows, halo, sibling),
-        scratch=[pltpu.VMEM((3,) + outer, F32), pltpu.VMEM(outer, F32)],
-        micros=0.4,
+        [SMEM, SMEM] + [VMEM] * 6,
+        (table, weights, rows, vrows, part, rate, halo, sibling),
+        micros=0.3,
     )
     next_received = over_space(next_sends)
-    far_halo = over_inst(across_halo, 1)
-    own, own_gain = call(
-        own_kernel,
-        [on_chip(full), on_chip(plane)],
-        [SMEM] + [VMEM] * 4,
-        (weights, rows, vrows, halo, sibling),
-        scratch=shifts,
-        micros=0.8,
-    )
-    across = call(
-        after_kernel, on_chip(state.shape), [VMEM] * 2, (across, next_outer), aliases={0: 0}, micros=0.05
-    )
-    far = over_inst(across, 1)
-    across_next, across_gain, own = call(
+    def after(x, *first):
+        return call(
+            after_kernel, on_chip(x.shape), [VMEM] * (1 + len(first)), (x, *first), aliases={0: 0}, micros=0.05
+        )
+
+    far = over_inst(after(across, next_outer), 1)
+    pieces = 2
+    size = comps // pieces
+    hx = across_halo
+    far_halo = [over_inst(hx[n * size : n * size + size], 1) for n in range(pieces)]
+    far_rows, far_part, far_rate = call(
+        far_pitchwise_kernel,
+        [on_chip(full)] * 2 + [on_chip(plane)],
+        [SMEM] + [VMEM] * 2,
+        (weights, vrows, far),
+        scratch=shifts + halves[:1],
+        micros=0.6,
+    )
+    own, sibling_next, own_gain, sibling_gain = call(
+        near_kernel,
+        [on_chip(full)] * 2 + [on_chip(plane)] * 2,
+        [SMEM] + [VMEM] * 10,
+        (weights, vrows, rows, part, rate, halo, sibling, sibling_part, sibling_rate, sibling_halo,
+         far_rate),
+        micros=0.7,
+    )
+    own, partial, across_rows, lacking, lacking_term = call(
         across_kernel,
-        [on_chip(full), on_chip(plane), on_chip(full)],
-        [SMEM] + [VMEM] * 7,
-        (weights, rows, vrows, across_halo, across, sibling, own, own_gain),
-        scratch=shifts + halves,
-        micros=0.9,
-    )
-    next_rows, partial, to_sibling = call(
-        finish_kernel,
-        [on_chip(full)] * 3,
-        [SMEM] + [VMEM] * 5,
-        (weights, own, own_gain, across_next, across_gain, far),
-        scratch=halves,
-    )
-    from_sibling = over_inst(to_sibling, 1)
-    total, rate = call(
-        pitchwise_kernel,
-        [on_chip(full), on_chip(plane)],
-        [VMEM] * 3 + [SMEM],
-        (next_rows, vrows, partial, weights),
-        scratch=shifts,
-        micros=0.6,
-    )
+        [on_chip(full)] * 3 + [on_chip(plane)] * 2,
+        [SMEM] + [VMEM] * 9,
+        (weights, vrows, rows, sibling, own, own_gain, sibling_next, sibling_gain, across, across_halo),
+        scratch=shifts + halves[:1] + [halves[1], pltpu.VMEM(plane, F32)],
+        micros=1.0,
+    )
+    next_rows, term = call(
+        far_kernel,
+        [on_chip(full)] * 2,
+        [SMEM] + [VMEM] * (11 + len(far_halo)),
+        (weights, vrows, rows, sibling, across_rows, own, partial, lacking, lacking_term,
+         far_rows, far_part, far_rate, *far_halo),
+        scratch=[pltpu.VMEM(outer, F32)],
+        micros=0.5,
+    )
+    next_part, next_rate = pitch(next_rows)
     next_halo = call(
         functools.partial(next_halo_kernel, space_total, cap),
         on_chip(outer),
-        [SMEM, VMEM, SMEM] + [VMEM] * (2 + space_total),
-        (table, index, weights, next_outer, across_halo, far_halo, *next_received),
-        scratch=pool,
+        [SMEM, VMEM, SMEM] + [VMEM] * (2 + space_total + len(far_halo)),
+        (table, index, weights, next_outer, across_halo, next_rate, *next_received, *far_halo),
+        scratch=pool + [pltpu.VMEM(outer, F32)],
     )
     new, residual = call(
         functools.partial(last_kernel, space_total, cap),
         [jax.ShapeDtypeStruct(state.shape, F32)] * 2,
         [SMEM] + [VMEM] * 6,
-        (table, next_rows, vrows, next_halo, total, rate, from_sibling),
+        (table, next_rows, vrows, next_halo, next_part, next_rate, term),
         scratch=[pltpu.VMEM((comps, 2, row_count, 128), F32)] * 2,
         micros=1.5,
     )

time: 36 us -> 27 us (0.75)
  waiting for transfers between devices: 9.68 us -> 3.01 us
  starting transfers between devices: 16.7 us -> 14.7 us
  local copies, waits for them, and re-layouts: 1.53 us -> 0.03 us
  Pallas kernels: 6.52 us -> 7.7 us
    ppermute x6, waiting for transfers between devices: 6.13 us -> 0.46 us  [over_space(): lax.ppermute(parts[k - 1], 'space', [(i, partner(i, k, space_total)) for...]
    ppermute x6, starting transfers between devices: 11.3 us -> 9.29 us  [over_space(): lax.ppermute(parts[k - 1], 'space', [(i, partner(i, k, space_total)) for...]
    unnamed x12 -> x1, local copies, waits for them, and re-layouts: 1.53 us -> 0.03 us
    pallas_call x10 -> x13, Pallas kernels: 6.52 us -> 7.68 us  [call(): pl.pallas_call(kernel, out_shape=out, in_specs=specs, out_specs=out_specs...]
    ppermute x6 -> x7, waiting for transfers between devices: 3.55 us -> 2.55 us  [over_inst(): return lax.ppermute(x, 'inst', [(i, i ^ flip) for i in range(4)])]
    ppermute x6 -> x7, starting transfers between devices: 5.41 us -> 5.39 us  [over_inst(): return lax.ppermute(x, 'inst', [(i, i ^ flip) for i in range(4)])]
  transfers between devices with their start and end apart: 12 -> 13, of which waited for: 8 -> 3; matrix products, arithmetic and copies ran while one was open for 0% -> 0% of each run, Pallas kernels for 9% -> 20%
where the time goes in v3:
time: 27 us; the launch traced here: 26.9 us
  starting transfers between devices  14.7 us (54%)
  Pallas kernels  7.7 us (29%)
  waiting for transfers between devices  3.01 us (11%)
  between operations  1.46 us (5%)
    ppermute x6, starting transfers between devices, over_space(): lax.ppermute(parts[k - 1], 'space', [(i, partner(i, k, space_total)) for...  9.29 us
    pallas_call x13, Pallas kernels, call(): pl.pallas_call(kernel, out_shape=out, in_specs=specs, out_specs=out_specs...  7.68 us
    ppermute x7, starting transfers between devices, over_inst(): return lax.ppermute(x, 'inst', [(i, i ^ flip) for i in range(4)])  5.39 us
    ppermute x7, waiting for transfers between devices, over_inst(): return lax.ppermute(x, 'inst', [(i, i ^ flip) for i in range(4)])  2.55 us
  transfers between devices with their start and end apart: 13, of which 3 were waited for; matrix products, arithmetic and copies ran while one was open for 0% of the time, Pallas kernels for 20%

profile of v3, /device:TPU:0, one launch (start us, length us, event | category | flops | bytes accessed | tf_op | source)
XLA Modules:
  0.0 26.9 jit_solution(13896972462670470636)
XLA Ops:
  0.6 3.0 %collective-permute-start.1 = (f32[6,64,256]{2,1,0:T(8,128)}, f32[6,64,256]{2,1,0:T(8,128)S(1)}, u32[]{:S(2)}, u32[]{:S(2)}) collective-permute-start(f32[6,64,256]{2,1,0:T(8,128)} %bitcast.6), channel_id=1, source_target_pairs={{0,8},{4,12},{8,0},{12,4},{1,9},{5,13},{9,1},{13,5},{2,10},{6,14},... | collective-permute-start | bytes 1179656 | tf_op jit(solution)/shard_map/ppermute | solution.py:540
  3.6 1.3 %shard_map.95 = (f32[6,8,8,256]{3,2,1,0:T(8,128)S(1)}, f32[8,8,256]{2,1,0:T(8,128)S(1)}, f32[6,2,8,256]{3,2,1,0:T(8,128)S(1)}, s32[37]{0:T(128)S(4)}, s32[8,256]...) custom-call(f32[6,64,256]{2,1,0:T(8,128)} %bitcast.7, ...), custom_call_target="tpu_custom_call" | custom-call | bytes 7380000 | tf_op jit(solution)/shard_map/pallas_call | solution.py:564
  4.9 0.1 collective-permute-start
  5.0 2.7 %collective-permute-start.2 = (f32[48,256]{1,0:T(8,128)S(1)}, f32[48,256]{1,0:T(8,128)S(1)}, u32[]{:S(2)}, u32[]{:S(2)}) collective-permute-start(f32[48,256]{1,0:T(8,128)S(1)} %get-tuple-element.44), channel_id=1, source_target_pairs={{0,2},{1,3},{2,0},{3,1},{4,6},{5,7},{6,4},{7,5},{8,10},{9,11},{10,... | collective-permute-start | bytes 147464 | tf_op jit(solution)/shard_map/ppermute | solution.py:544
  7.7 1.3 %collective-permute-start.3 = (f32[48,256]{1,0:T(8,128)S(1)}, f32[48,256]{1,0:T(8,128)S(1)}, u32[]{:S(2)}, u32[]{:S(2)}) collective-permute-start(f32[48,256]{1,0:T(8,128)S(1)} %get-tuple-element.45), channel_id=1, source_target_pairs={{0,3},{1,2},{2,1},{3,0},{4,7},{5,6},{6,5},{7,4},{8,11},{9,10},{10,... | collective-permute-start | bytes 147464 | tf_op jit(solution)/shard_map/ppermute | solution.py:544
  9.0 0.2 collective-permute-start.4
  9.9 0.5 %shard_map.97 = (f32[6,8,8,256]{3,2,1,0:T(8,128)S(1)}, f32[8,8,256]{2,1,0:T(8,128)S(1)}) custom-call(f32[8]{0:T(128)S(4)} %shard_map.96.weight_ref, f32[6,8,8,256]{3,2,1,0:T(8,128)S(1)} %get-tuple-element.38.rows_ref, f32[8,8,256]{2,1,0:T(8,128)S(1)} %get-tuple-element.37.vrows_ref), custom_call_target="tpu_custom_call" | custom-call | bytes 1845000 | tf_op jit(solution)/shard_map/pallas_call | solution.py:564
  10.4 2.5 %collective-permute-done.1.more_0_.raw_ref = f32[6,64,256]{2,1,0:T(8,128)S(1)} collective-permute-done((f32[6,64,256]{2,1,0:T(8,128)}, f32[6,64,256]{2,1,0:T(8,128)S(1)}, u32[]{:S(2)}, u32[]{:S(2)}) %collective-permute-start.1) | collective-permute-done | bytes 393248 | tf_op jit(solution)/shard_map/ppermute | solution.py:540
  13.0 0.0 collective-permute-done.rows_ref.sibling_ref
  13.0 0.5 %shard_map.98 = (f32[6,8,8,256]{3,2,1,0:T(8,128)S(1)}, f32[8,8,256]{2,1,0:T(8,128)S(1)}) custom-call(f32[8]{0:T(128)S(4)} %shard_map.96.weight_ref, f32[6,8,8,256]{3,2,1,0:T(8,128)S(1)} %collective-permute-done.rows_ref.sibling_ref, f32[8,8,256]{2,1,0:T(8,128)S(1)} %get-tuple-element.37.vrows_ref, f32[6,64,256]{2,1,0:T(8,128)S(1)} %collective-permute-done.1.more_0_.raw_ref), custom_call_target="tpu_custom_call" | custom-call | bytes 1845000 | tf_op jit(solution)/shard_map/pallas_call | solution.py:564
  13.5 0.0 collective-permute-done.2.more_0_
  13.5 0.3 %collective-permute-done.3.more_1_ = f32[48,256]{1,0:T(8,128)S(1)} collective-permute-done((f32[48,256]{1,0:T(8,128)S(1)}, f32[48,256]{1,0:T(8,128)S(1)}, u32[]{:S(2)}, u32[]{:S(2)}) %collective-permute-start.3) | collective-permute-done | bytes 49184 | tf_op jit(solution)/shard_map/ppermute | solution.py:544
  13.8 0.0 collective-permute-done.4.more_2_
  13.8 0.3 %shard_map.99.halo_ref = f32[6,2,8,256]{3,2,1,0:T(8,128)S(1)} custom-call(s32[37]{0:T(128)S(4)} %get-tuple-element.36.table_ref, s32[8,256]{1,0:T(8,128)S(1)} %get-tuple-element.41.index_ref, f32[6,2,8,256]{3,2,1,0:T(8,128)S(1)} %get-tuple-element.42.outer_ref, f32[8,8,256]{2,1,0:T(8,128)S(1)} %get-tuple-element.40._.rate_ref, ...), custom_call_target="tpu_custom_call" | custom-call | bytes 1107000 | tf_op jit(solution)/shard_map/pallas_call | solution.py:564
  14.1 0.2 shard_map.100
  14.4 0.1 collective-permute-start.6
  14.5 1.5 %collective-permute-start.7 = (f32[6,2,8,256]{3,2,1,0:T(8,128)S(1)}, f32[6,2,8,256]{3,2,1,0:T(8,128)S(1)}, u32[]{:S(2)}, u32[]{:S(2)}) collective-permute-start(f32[6,2,8,256]{3,2,1,0:T(8,128)S(1)} %shard_map.99.halo_ref), channel_id=1, source_target_pairs={{0,8},{4,12},{8,0},{12,4},{1,9},{5,13},{9,1},{13,5},{2,10},{6,14},... | collective-permute-start | bytes 294920 | tf_op jit(solution)/shard_map/ppermute | solution.py:540
  16.0 0.2 collective-permute-start.5
  16.1 2.6 %collective-permute-start.10 = (f32[56,256]{1,0:T(8,128)S(1)}, f32[56,256]{1,0:T(8,128)S(1)}, u32[]{:S(2)}, u32[]{:S(2)}) collective-permute-start(f32[56,256]{1,0:T(8,128)S(1)} %get-tuple-element.63), channel_id=1, source_target_pairs={{0,2},{1,3},{2,0},{3,1},{4,6},{5,7},{6,4},{7,5},{8,10},{9,11},{10,... | collective-permute-start | bytes 172040 | tf_op jit(solution)/shard_map/ppermute | solution.py:544
  18.7 1.3 %collective-permute-start.11 = (f32[56,256]{1,0:T(8,128)S(1)}, f32[56,256]{1,0:T(8,128)S(1)}, u32[]{:S(2)}, u32[]{:S(2)}) collective-permute-start(f32[56,256]{1,0:T(8,128)S(1)} %get-tuple-element.64), channel_id=1, source_target_pairs={{0,3},{1,2},{2,1},{3,0},{4,7},{5,6},{6,5},{7,4},{8,11},{9,10},{10,... | collective-permute-start | bytes 172040 | tf_op jit(solution)/shard_map/ppermute | solution.py:544
  20.1 0.0 collective-permute-done.7.halo_ref.across_ref
  20.1 1.1 %collective-permute-start.12 = (f32[56,256]{1,0:T(8,128)S(1)}, f32[56,256]{1,0:T(8,128)S(1)}, u32[]{:S(2)}, u32[]{:S(2)}) collective-permute-start(f32[56,256]{1,0:T(8,128)S(1)} %get-tuple-element.65), channel_id=1, source_target_pairs={{0,1},{1,0},{2,3},{3,2},{4,5},{5,4},{6,7},{7,6},{8,9},{9,8},{10,11... | collective-permute-start | bytes 172040 | tf_op jit(solution)/shard_map/ppermute | solution.py:544
  21.2 0.0 collective-permute-done.5.sibling_halo_ref
  21.2 0.1 collective-permute-start.8
  21.3 0.0 collective-permute-done.6.raw_ref
  21.3 0.5 %collective-permute-start.9 = (f32[3,2,8,256]{3,2,1,0:T(8,128)S(1)}, f32[3,2,8,256]{3,2,1,0:T(8,128)S(1)}, u32[]{:S(2)}, u32[]{:S(2)}) collective-permute-start(f32[3,2,8,256]{3,2,1,0:T(8,128)S(1)} %get-tuple-element.70), channel_id=1, source_target_pairs={{0,4},{4,0},{8,12},{12,8},{1,5},{5,1},{9,13},{13,9},{2,6},{6,2},{1... | collective-permute-start | bytes 147464 | tf_op jit(solution)/shard_map/ppermute | solution.py:540
  21.8 0.5 %shard_map.102 = (f32[6,8,8,256]{3,2,1,0:T(8,128)S(1)}, f32[6,8,8,256]{3,2,1,0:T(8,128)S(1)}, f32[8,8,256]{2,1,0:T(8,128)S(1)}) custom-call(f32[8]{0:T(128)S(4)} %shard_map.96.weight_ref, f32[8,8,256]{2,1,0:T(8,128)S(1)} %get-tuple-element.37.vrows_ref, f32[6,64,256]{2,1,0:T(8,128)S(1)} %collective-permute-done.6.raw_ref), custom_call_target="tpu_custom_call" | custom-call | bytes 2214000 | tf_op jit(solution)/shard_map/pallas_call | solution.py:564
  22.3 0.7 %shard_map.103 = (f32[6,8,8,256]{3,2,1,0:T(8,128)S(1)}, f32[6,8,8,256]{3,2,1,0:T(8,128)S(1)}, f32[8,8,256]{2,1,0:T(8,128)S(1)}, f32[8,8,256]{2,1,0:T(8,128)S(1)}) custom-call(f32[8]{0:T(128)S(4)} %shard_map.96.weight_ref, f32[8,8,256]{2,1,0:T(8,128)S(1)} %get-tuple-element.37.vrows_ref, f32[6,8,8,256]{3,2,1,0:T(8,128)S(1)} %get-tuple-element.38.rows_ref, ...), custom_call_target="tpu_custom_call" | custom-call | bytes 2583000 | tf_op jit(solution)/shard_map/pallas_call | solution.py:564
  23.0 1.0 %shard_map.104 = (f32[6,8,8,256]{3,2,1,0:T(8,128)S(1)}, f32[6,8,8,256]{3,2,1,0:T(8,128)S(1)}, f32[6,8,8,256]{3,2,1,0:T(8,128)S(1)}, f32[8,8,256]{2,1,0:T(8,128)S(1)}, f32[8,8,256]{2,1,0:T(8,128)S(1)}) custom-call(f32[8]{0:T(128)S(4)} %shard_map.96.weight_ref, f32[8,8,256]{2,1,0:T(8,128)S(1)} %get-tuple-element.37.vrows_ref, ...), custom_call_target="tpu_custom_call" | custom-call | bytes 3690000 | tf_op jit(solution)/shard_map/pallas_call | solution.py:564
  24.0 0.0 collective-permute-done.8.more_0_.more_3_
  24.0 0.0 collective-permute-done.9.more_1_.more_4_
  24.0 0.5 %shard_map.105 = (f32[6,8,8,256]{3,2,1,0:T(8,128)S(1)}, f32[6,8,8,256]{3,2,1,0:T(8,128)S(1)}) custom-call(f32[8]{0:T(128)S(4)} %shard_map.96.weight_ref, f32[8,8,256]{2,1,0:T(8,128)S(1)} %get-tuple-element.37.vrows_ref, f32[6,8,8,256]{3,2,1,0:T(8,128)S(1)} %get-tuple-element.38.rows_ref, f32[6,8,8,256]{3,2,1,0:T(8,128)S(1)} %collective-permute-done.rows_ref.sibling_ref, ...), custom_call_target="tpu_custom_call" | custom-call | bytes 1845000 | tf_op jit(solution)/shard_map/pallas_call | solution.py:564
  24.5 0.5 %shard_map.106 = (f32[6,8,8,256]{3,2,1,0:T(8,128)S(1)}, f32[8,8,256]{2,1,0:T(8,128)S(1)}) custom-call(f32[8]{0:T(128)S(4)} %shard_map.96.weight_ref, f32[6,8,8,256]{3,2,1,0:T(8,128)S(1)} %get-tuple-element.61.rows_ref, f32[8,8,256]{2,1,0:T(8,128)S(1)} %get-tuple-element.37.vrows_ref), custom_call_target="tpu_custom_call" | custom-call | bytes 1845000 | tf_op jit(solution)/shard_map/pallas_call | solution.py:564
  25.0 0.0 collective-permute-done.10.more_0_
  25.0 0.1 collective-permute-done.11.more_1_
  25.1 0.0 collective-permute-done.12.more_2_
  25.1 0.3 %shard_map.107.halo_ref = f32[6,2,8,256]{3,2,1,0:T(8,128)S(1)} custom-call(s32[37]{0:T(128)S(4)} %get-tuple-element.36.table_ref, s32[8,256]{1,0:T(8,128)S(1)} %get-tuple-element.41.index_ref, f32[8]{0:T(128)S(4)} %shard_map.96.weight_ref, f32[7,2,8,256]{3,2,1,0:T(8,128)S(1)} %get-tuple-element.48.more_0_.outer_ref, ...), custom_call_target="tpu_custom_call" | custom-call | bytes 1107000 | tf_op jit(solution)/shard_map/pallas_call | solution.py:564
  25.5 1.4 %shard_map.108 = (f32[6,64,256]{2,1,0:T(8,128)}, f32[6,64,256]{2,1,0:T(8,128)}) custom-call(s32[37]{0:T(128)S(4)} %get-tuple-element.36.table_ref, f32[6,8,8,256]{3,2,1,0:T(8,128)S(1)} %get-tuple-element.61.rows_ref, f32[8,8,256]{2,1,0:T(8,128)S(1)} %get-tuple-element.37.vrows_ref, f32[6,2,8,256]{3,2,1,0:T(8,128)S(1)} %shard_map.107.halo_ref, ...), custom_call_target="tpu_custom_call" | custom-call | bytes 5535000 | tf_op jit(solution)/shard_map/pallas_call | solution.py:564
  (4 shorter events, 0.1 us)
Async XLA Ops:
  0.6 12.3 %collective-permute-start.1 = (f32[6,64,256]{2,1,0:T(8,128)}, f32[6,64,256]{2,1,0:T(8,128)S(1)}, u32[]{:S(2)}, u32[]{:S(2)}) collective-permute-start(f32[6,64,256]{2,1,0:T(8,128)} %bitcast.6), channel_id=1, source_target_pairs={{0,8},{4,12},{8,0},{12,4},{1,9},{5,13},{9,1},{13,5},{2,10},{6,14},... | collective-permute-start | bytes 1179656 | tf_op jit(solution)/shard_map/ppermute | solution.py:540
  4.9 8.1 %collective-permute-start = (f32[6,8,8,256]{3,2,1,0:T(8,128)S(1)}, f32[6,8,8,256]{3,2,1,0:T(8,128)S(1)}, u32[]{:S(2)}, u32[]{:S(2)}) collective-permute-start(f32[6,8,8,256]{3,2,1,0:T(8,128)S(1)} %get-tuple-element.38.rows_ref), channel_id=1, source_target_pairs={{0,4},{4,0},{8,12},{12,8},{1,5},{5,1},{9,13},{13,9},{2,6},{6,2},{1... | collective-permute-start | bytes 1179656 | tf_op jit(solution)/shard_map/ppermute | solution.py:540
  5.0 8.5 %collective-permute-start.2 = (f32[48,256]{1,0:T(8,128)S(1)}, f32[48,256]{1,0:T(8,128)S(1)}, u32[]{:S(2)}, u32[]{:S(2)}) collective-permute-start(f32[48,256]{1,0:T(8,128)S(1)} %get-tuple-element.44), channel_id=1, source_target_pairs={{0,2},{1,3},{2,0},{3,1},{4,6},{5,7},{6,4},{7,5},{8,10},{9,11},{10,... | collective-permute-start | bytes 147464 | tf_op jit(solution)/shard_map/ppermute | solution.py:544
  7.7 6.2 %collective-permute-start.3 = (f32[48,256]{1,0:T(8,128)S(1)}, f32[48,256]{1,0:T(8,128)S(1)}, u32[]{:S(2)}, u32[]{:S(2)}) collective-permute-start(f32[48,256]{1,0:T(8,128)S(1)} %get-tuple-element.45), channel_id=1, source_target_pairs={{0,3},{1,2},{2,1},{3,0},{4,7},{5,6},{6,5},{7,4},{8,11},{9,10},{10,... | collective-permute-start | bytes 147464 | tf_op jit(solution)/shard_map/ppermute | solution.py:544
  9.0 4.8 %collective-permute-start.4 = (f32[48,256]{1,0:T(8,128)S(1)}, f32[48,256]{1,0:T(8,128)S(1)}, u32[]{:S(2)}, u32[]{:S(2)}) collective-permute-start(f32[48,256]{1,0:T(8,128)S(1)} %get-tuple-element.46), channel_id=1, source_target_pairs={{0,1},{1,0},{2,3},{3,2},{4,5},{5,4},{6,7},{7,6},{8,9},{9,8},{10,11... | collective-permute-start | bytes 147464 | tf_op jit(solution)/shard_map/ppermute | solution.py:544
  14.4 6.9 %collective-permute-start.6 = (f32[6,64,256]{2,1,0:T(8,128)S(1)}, f32[6,64,256]{2,1,0:T(8,128)S(1)}, u32[]{:S(2)}, u32[]{:S(2)}) collective-permute-start(f32[6,64,256]{2,1,0:T(8,128)S(1)} %shard_map.101), channel_id=1, source_target_pairs={{0,4},{4,0},{8,12},{12,8},{1,5},{5,1},{9,13},{13,9},{2,6},{6,2},{1... | collective-permute-start | bytes 1179656 | tf_op jit(solution)/shard_map/ppermute | solution.py:540
  14.5 5.6 %collective-permute-start.7 = (f32[6,2,8,256]{3,2,1,0:T(8,128)S(1)}, f32[6,2,8,256]{3,2,1,0:T(8,128)S(1)}, u32[]{:S(2)}, u32[]{:S(2)}) collective-permute-start(f32[6,2,8,256]{3,2,1,0:T(8,128)S(1)} %shard_map.99.halo_ref), channel_id=1, source_target_pairs={{0,8},{4,12},{8,0},{12,4},{1,9},{5,13},{9,1},{13,5},{2,10},{6,14},... | collective-permute-start | bytes 294920 | tf_op jit(solution)/shard_map/ppermute | solution.py:540
  16.0 5.2 %collective-permute-start.5 = (f32[6,2,8,256]{3,2,1,0:T(8,128)S(1)}, f32[6,2,8,256]{3,2,1,0:T(8,128)S(1)}, u32[]{:S(2)}, u32[]{:S(2)}) collective-permute-start(f32[6,2,8,256]{3,2,1,0:T(8,128)S(1)} %shard_map.99.halo_ref), channel_id=1, source_target_pairs={{0,4},{4,0},{8,12},{12,8},{1,5},{5,1},{9,13},{13,9},{2,6},{6,2},{1... | collective-permute-start | bytes 294920 | tf_op jit(solution)/shard_map/ppermute | solution.py:540
  16.1 8.8 %collective-permute-start.10 = (f32[56,256]{1,0:T(8,128)S(1)}, f32[56,256]{1,0:T(8,128)S(1)}, u32[]{:S(2)}, u32[]{:S(2)}) collective-permute-start(f32[56,256]{1,0:T(8,128)S(1)} %get-tuple-element.63), channel_id=1, source_target_pairs={{0,2},{1,3},{2,0},{3,1},{4,6},{5,7},{6,4},{7,5},{8,10},{9,11},{10,... | collective-permute-start | bytes 172040 | tf_op jit(solution)/shard_map/ppermute | solution.py:544
  18.7 6.4 %collective-permute-start.11 = (f32[56,256]{1,0:T(8,128)S(1)}, f32[56,256]{1,0:T(8,128)S(1)}, u32[]{:S(2)}, u32[]{:S(2)}) collective-permute-start(f32[56,256]{1,0:T(8,128)S(1)} %get-tuple-element.64), channel_id=1, source_target_pairs={{0,3},{1,2},{2,1},{3,0},{4,7},{5,6},{6,5},{7,4},{8,11},{9,10},{10,... | collective-permute-start | bytes 172040 | tf_op jit(solution)/shard_map/ppermute | solution.py:544
  20.1 5.1 %collective-permute-start.12 = (f32[56,256]{1,0:T(8,128)S(1)}, f32[56,256]{1,0:T(8,128)S(1)}, u32[]{:S(2)}, u32[]{:S(2)}) collective-permute-start(f32[56,256]{1,0:T(8,128)S(1)} %get-tuple-element.65), channel_id=1, source_target_pairs={{0,1},{1,0},{2,3},{3,2},{4,5},{5,4},{6,7},{7,6},{8,9},{9,8},{10,11... | collective-permute-start | bytes 172040 | tf_op jit(solution)/shard_map/ppermute | solution.py:544
  21.2 2.8 %collective-permute-start.8 = (f32[3,2,8,256]{3,2,1,0:T(8,128)S(1)}, f32[3,2,8,256]{3,2,1,0:T(8,128)S(1)}, u32[]{:S(2)}, u32[]{:S(2)}) collective-permute-start(f32[3,2,8,256]{3,2,1,0:T(8,128)S(1)} %get-tuple-element.71), channel_id=1, source_target_pairs={{0,4},{4,0},{8,12},{12,8},{1,5},{5,1},{9,13},{13,9},{2,6},{6,2},{1... | collective-permute-start | bytes 147464 | tf_op jit(solution)/shard_map/ppermute | solution.py:540
  21.3 2.7 %collective-permute-start.9 = (f32[3,2,8,256]{3,2,1,0:T(8,128)S(1)}, f32[3,2,8,256]{3,2,1,0:T(8,128)S(1)}, u32[]{:S(2)}, u32[]{:S(2)}) collective-permute-start(f32[3,2,8,256]{3,2,1,0:T(8,128)S(1)} %get-tuple-element.70), channel_id=1, source_target_pairs={{0,4},{4,0},{8,12},{12,8},{1,5},{5,1},{9,13},{13,9},{2,6},{6,2},{1... | collective-permute-start | bytes 147464 | tf_op jit(solution)/shard_map/ppermute | solution.py:540

commit v4 on v3

--- a/solution.py
+++ b/solution.py
@@ -66,8 +66,12 @@
     return u, v, p
 
 
-def flux_along_i(q, u, p):
-    return [q[1], q[1] * u + p, q[2] * u, q[3] * u, (q[4] + p) * u, q[5] * u]
+def flux_along_i(q, u, p, c):
+    if c == 0:
+        return q[1]
+    if c == 1:
+        return q[1] * u + p
+    return ((q[4] + p) if c == 4 else q[c]) * u
 
 
 def flux_along_j(q, v, p):
@@ -116,7 +120,8 @@
 class Rows:
     def __init__(self, load):
         self.load = load
-        self.state, self.prim, self.flux, self.steps, self.faces = {}, {}, {}, {}, {}
+        self.state, self.prim, self.flux = {}, {}, {}
+        self.steps, self.radii, self.faces = {}, {}, {}
 
     def q(self, r):
         if r not in self.state:
@@ -128,31 +133,37 @@
             self.prim[r] = primitives(self.q(r))
         return self.prim[r]
 
-    def f(self, r):
-        if r not in self.flux:
+    def f(self, c, r):
+        if (c, r) not in self.flux:
             u, _, p = self.uvp(r)
-            self.flux[r] = flux_along_i(self.q(r), u, p)
-        return self.flux[r]
-
-    def step(self, r):
-        if r not in self.steps:
-            self.steps[r] = [b - a for a, b in zip(self.q(r), self.q(r + 1))]
-        return self.steps[r]
-
-    def face(self, r):
-        if r not in self.faces:
-            radius = 0.5 * (jnp.abs(self.uvp(r)[0]) + jnp.abs(self.uvp(r + 1)[0])) + SOUND_SPEED
-            out = []
-            for c in range(COMPS):
-                damping = DIFF_ONE * self.step(r)[c] - FOURTH_DISSIPATION * (
-                    self.step(r + 1)[c] + self.step(r - 1)[c]
-                )
-                out.append(0.5 * (self.f(r)[c] + self.f(r + 1)[c]) - radius * damping)
-            self.faces[r] = out
-        return self.faces[r]
+            self.flux[c, r] = flux_along_i(self.q(r), u, p, c)
+        return self.flux[c, r]
+
+    def step(self, c, r):
+        if (c, r) not in self.steps:
+            self.steps[c, r] = self.q(r + 1)[c] - self.q(r)[c]
+        return self.steps[c, r]
+
+    def radius(self, r):
+        if r not in self.radii:
+            speeds = jnp.abs(self.uvp(r)[0]) + jnp.abs(self.uvp(r + 1)[0])
+            self.radii[r] = 0.5 * speeds + SOUND_SPEED
+        return self.radii[r]
+
+    def face(self, c, r):
+        if (c, r) not in self.faces:
+            damping = DIFF_ONE * self.step(c, r) - FOURTH_DISSIPATION * (
+                self.step(c, r + 1) + self.step(c, r - 1)
+            )
+            average = 0.5 * (self.f(c, r) + self.f(c, r + 1))
+            self.faces[c, r] = average - self.radius(r) * damping
+        return self.faces[c, r]
+
+    def along_one(self, c, r):
+        return self.face(c, r) - self.face(c, r - 1)
 
     def along(self, r):
-        return [b - a for a, b in zip(self.face(r - 1), self.face(r))]
+        return [self.along_one(c, r) for c in range(COMPS)]
 
 
 def even_tiles(shape):
@@ -368,6 +379,15 @@
     pitchwise(lambda c, r: rows_ref[c, r], vrows_ref, weight_ref[0], part_ref, rate_ref, near_ref, lower_ref)
 
 
+def sibling_pitchwise_kernel(
+    weight_ref, vrows_ref, first_ref, second_ref, rows_ref, part_ref, rate_ref, near_ref, lower_ref
+):
+    for c in range(COMPS):
+        rows_ref[c] = first_ref[c] if c < 3 else second_ref[c - 3]
+    load = lambda c, r: rows_ref[c, r]
+    pitchwise(load, vrows_ref, weight_ref[0], part_ref, rate_ref, near_ref, lower_ref)
+
+
 def pitchwise(load, vrows_ref, omega, part_ref, rate_ref, near_ref, lower_ref):
     pitchwise_shifts(load, near_ref)
     for r in range(8):
@@ -499,28 +519,34 @@
 
 def last_kernel(
     space_total, cap, table_ref, rows_ref, vrows_ref, halo_ref, part_ref, rate_ref, term_ref,
-    new_ref, residual_ref, new_half_ref, residual_half_ref
+    new_ref, residual_ref, new_half_ref, residual_half_ref, inverse_ref, left
 ):
     own = Rows(row_loader(lambda c, r: rows_ref[c, r], halo_ref))
     live_slots = table_ref[3 * FACES + (space_total - 1) * cap]
     live = (lax.broadcasted_iota(jnp.int32, vrows_ref.shape[1:], 0) // 2) < live_slots
     for r in range(8):
-        volume = vrows_ref[r]
-        along = own.along(r)
-        rate = rate_ref[r]
-        inverse = 1.0 / volume
-        for c in range(COMPS):
-            residual = part_ref[c, r] + along[c] + volume * term_ref[c, r]
-            new = jnp.where(live, own.q(r)[c] - rate * residual, 0.0)
-            scaled = jnp.where(live, residual * inverse, 0.0)
+        inverse_ref[r] = 1.0 / vrows_ref[r]
+    copies = []
+    for c in range(COMPS):
+        for r in range(8):
+            residual = part_ref[c, r] + own.along_one(c, r) + vrows_ref[r] * term_ref[c, r]
+            new = jnp.where(live, own.q(r)[c] - rate_ref[r] * residual, 0.0)
+            scaled = jnp.where(live, residual * inverse_ref[r], 0.0)
             for h in range(2):
                 lanes = slice(128 * h, 128 * h + 128)
                 new_half_ref[c, h, pl.ds(r, 8, stride=8), :] = new[:, lanes]
                 residual_half_ref[c, h, pl.ds(r, 8, stride=8), :] = scaled[:, lanes]
-    for c in range(COMPS):
-        for h in range(2):
-            new_ref[c, :, pl.ds(128 * h, 128)] = new_half_ref[c, h]
-            residual_ref[c, :, pl.ds(128 * h, 128)] = residual_half_ref[c, h]
+        for n, (half_ref, out_ref) in enumerate(
+            [(new_half_ref, new_ref), (residual_half_ref, residual_ref)]
+        ):
+            for h in range(2):
+                copy = pltpu.make_async_copy(
+                    half_ref.at[c, h], out_ref.at[c, :, pl.ds(128 * h, 128)], left.at[len(copies)]
+                )
+                copy.start()
+                copies.append(copy)
+    for copy in copies:
+        copy.wait()
 
 
 def after_kernel(value_ref, *more):
@@ -617,10 +643,17 @@
         )
 
     across = over_inst(state, 2)
-    sibling = over_inst(rows, 1)
+    sibling_halves = [over_inst(rows[n * 3 : n * 3 + 3], 1) for n in range(2)]
     received = over_space(sends)
     part, rate = pitch(rows)
-    sibling_part, sibling_rate = pitch(sibling, across)
+    sibling, sibling_part, sibling_rate = call(
+        sibling_pitchwise_kernel,
+        [on_chip(full)] * 2 + [on_chip(plane)],
+        [SMEM] + [VMEM] * 3,
+        (weights, vrows, *sibling_halves),
+        scratch=shifts,
+        micros=0.5,
+    )
     halo = call(
         functools.partial(halo_kernel, space_total, cap),
         on_chip(outer),
@@ -694,8 +727,10 @@
         [jax.ShapeDtypeStruct(state.shape, F32)] * 2,
         [SMEM] + [VMEM] * 6,
         (table, next_rows, vrows, next_halo, next_part, next_rate, term),
-        scratch=[pltpu.VMEM((comps, 2, row_count, 128), F32)] * 2,
+        scratch=[pltpu.VMEM((comps, 2, row_count, 128), F32)] * 2
+        + [pltpu.VMEM(plane, F32), pltpu.SemaphoreType.DMA((4 * comps,))],
         micros=1.5,
+        out_specs=[HBM] * 2,
     )
     return new[None], residual[None]
 

time: 27 us -> 26.5 us (0.981)
  starting transfers between devices: 14.7 us -> 12.8 us
  waiting for transfers between devices: 3.01 us -> 4.41 us
    ppermute x6, waiting for transfers between devices: 0.46 us -> 3.4 us  [over_space(): lax.ppermute(parts[k - 1], 'space', [(i, partner(i, k, space_total)) for...]
    ppermute x7 -> x8, waiting for transfers between devices: 2.55 us -> 1.01 us  [over_inst(): return lax.ppermute(x, 'inst', [(i, i ^ flip) for i in range(4)])]
    ppermute x6, starting transfers between devices: 9.29 us -> 7.84 us  [over_space(): lax.ppermute(parts[k - 1], 'space', [(i, partner(i, k, space_total)) for...]
    ppermute x7 -> x8, starting transfers between devices: 5.39 us -> 4.97 us  [over_inst(): return lax.ppermute(x, 'inst', [(i, i ^ flip) for i in range(4)])]
  transfers between devices with their start and end apart: 13 -> 14, of which waited for: 3 -> 4; matrix products, arithmetic and copies ran while one was open for 0% -> 0% of each run, Pallas kernels for 20% -> 23%
where the time goes in v4:
time: 26.5 us; the launch traced here: 26.3 us
  starting transfers between devices  12.8 us (48%)
  Pallas kernels  7.56 us (29%)
  waiting for transfers between devices  4.41 us (17%)
  between operations  1.48 us (6%)
    ppermute x6, starting transfers between devices, over_space(): lax.ppermute(parts[k - 1], 'space', [(i, partner(i, k, space_total)) for...  7.84 us
    pallas_call x13, Pallas kernels, call(): pl.pallas_call(kernel, out_shape=out, in_specs=specs, out_specs=out_specs...  7.54 us
    ppermute x8, starting transfers between devices, over_inst(): return lax.ppermute(x, 'inst', [(i, i ^ flip) for i in range(4)])  4.97 us
    ppermute x6, waiting for transfers between devices, over_space(): lax.ppermute(parts[k - 1], 'space', [(i, partner(i, k, space_total)) for...  3.4 us
    ppermute x8, waiting for transfers between devices, over_inst(): return lax.ppermute(x, 'inst', [(i, i ^ flip) for i in range(4)])  1.01 us
  transfers between devices with their start and end apart: 14, of which 4 were waited for; matrix products, arithmetic and copies ran while one was open for 0% of the time, Pallas kernels for 23%

profile of v4, /device:TPU:0, one launch (start us, length us, event | category | flops | bytes accessed | tf_op | source)
XLA Modules:
  0.0 26.3 jit_solution(17597519979496891980)
XLA Ops:
  0.6 3.0 %collective-permute-start.6 = (f32[6,64,256]{2,1,0:T(8,128)}, f32[6,64,256]{2,1,0:T(8,128)S(1)}, u32[]{:S(2)}, u32[]{:S(2)}) collective-permute-start(f32[6,64,256]{2,1,0:T(8,128)} %bitcast.6), channel_id=1, source_target_pairs={{0,8},{4,12},{8,0},{12,4},{1,9},{5,13},{9,1},{13,5},{2,10},{6,14},... | collective-permute-start | bytes 1179656 | tf_op jit(solution)/shard_map/ppermute | solution.py:566
  3.6 1.3 %shard_map.95 = (f32[6,8,8,256]{3,2,1,0:T(8,128)S(1)}, f32[8,8,256]{2,1,0:T(8,128)S(1)}, f32[6,2,8,256]{3,2,1,0:T(8,128)S(1)}, s32[37]{0:T(128)S(4)}, s32[8,256]...) custom-call(f32[6,64,256]{2,1,0:T(8,128)} %bitcast.7, ...), custom_call_target="tpu_custom_call" | custom-call | bytes 7380000 | tf_op jit(solution)/shard_map/pallas_call | solution.py:590
  5.0 0.1 collective-permute-start
  5.0 0.5 %collective-permute-start.1 = (f32[3,8,8,256]{3,2,1,0:T(8,128)S(1)}, f32[3,8,8,256]{3,2,1,0:T(8,128)S(1)}, u32[]{:S(2)}, u32[]{:S(2)}) collective-permute-start(f32[3,8,8,256]{3,2,1,0:T(8,128)S(1)} %get-tuple-element.72), channel_id=1, source_target_pairs={{0,4},{4,0},{8,12},{12,8},{1,5},{5,1},{9,13},{13,9},{2,6},{6,2},{1... | collective-permute-start | bytes 589832 | tf_op jit(solution)/shard_map/ppermute | solution.py:566
  5.5 2.6 %collective-permute-start.2 = (f32[48,256]{1,0:T(8,128)S(1)}, f32[48,256]{1,0:T(8,128)S(1)}, u32[]{:S(2)}, u32[]{:S(2)}) collective-permute-start(f32[48,256]{1,0:T(8,128)S(1)} %get-tuple-element.46), channel_id=1, source_target_pairs={{0,2},{1,3},{2,0},{3,1},{4,6},{5,7},{6,4},{7,5},{8,10},{9,11},{10,... | collective-permute-start | bytes 147464 | tf_op jit(solution)/shard_map/ppermute | solution.py:570
  8.1 1.3 %collective-permute-start.3 = (f32[48,256]{1,0:T(8,128)S(1)}, f32[48,256]{1,0:T(8,128)S(1)}, u32[]{:S(2)}, u32[]{:S(2)}) collective-permute-start(f32[48,256]{1,0:T(8,128)S(1)} %get-tuple-element.47), channel_id=1, source_target_pairs={{0,3},{1,2},{2,1},{3,0},{4,7},{5,6},{6,5},{7,4},{8,11},{9,10},{10,... | collective-permute-start | bytes 147464 | tf_op jit(solution)/shard_map/ppermute | solution.py:570
  9.5 0.0 collective-permute-done.first_ref
  9.5 0.2 collective-permute-start.4
  10.4 0.5 %shard_map.98 = (f32[6,8,8,256]{3,2,1,0:T(8,128)S(1)}, f32[8,8,256]{2,1,0:T(8,128)S(1)}) custom-call(f32[8]{0:T(128)S(4)} %shard_map.96.weight_ref, f32[6,8,8,256]{3,2,1,0:T(8,128)S(1)} %get-tuple-element.39.rows_ref, f32[8,8,256]{2,1,0:T(8,128)S(1)} %get-tuple-element.38.vrows_ref), custom_call_target="tpu_custom_call" | custom-call | bytes 1845000 | tf_op jit(solution)/shard_map/pallas_call | solution.py:590
  10.9 0.0 collective-permute-done.1.second_ref
  10.9 0.5 %shard_map.97 = (f32[6,8,8,256]{3,2,1,0:T(8,128)S(1)}, f32[6,8,8,256]{3,2,1,0:T(8,128)S(1)}, f32[8,8,256]{2,1,0:T(8,128)S(1)}) custom-call(f32[8]{0:T(128)S(4)} %shard_map.96.weight_ref, f32[8,8,256]{2,1,0:T(8,128)S(1)} %get-tuple-element.38.vrows_ref, f32[3,8,8,256]{3,2,1,0:T(8,128)S(1)} %collective-permute-done.first_ref, ...), custom_call_target="tpu_custom_call" | custom-call | bytes 1845000 | tf_op jit(solution)/shard_map/pallas_call | solution.py:590
  11.4 0.2 collective-permute-done.2.more_0_
  11.6 2.5 %collective-permute-done.3.more_1_ = f32[48,256]{1,0:T(8,128)S(1)} collective-permute-done((f32[48,256]{1,0:T(8,128)S(1)}, f32[48,256]{1,0:T(8,128)S(1)}, u32[]{:S(2)}, u32[]{:S(2)}) %collective-permute-start.3) | collective-permute-done | bytes 49184 | tf_op jit(solution)/shard_map/ppermute | solution.py:570
  14.1 0.0 collective-permute-done.4.more_2_
  14.1 0.3 %shard_map.99.halo_ref = f32[6,2,8,256]{3,2,1,0:T(8,128)S(1)} custom-call(s32[37]{0:T(128)S(4)} %get-tuple-element.37.table_ref, s32[8,256]{1,0:T(8,128)S(1)} %get-tuple-element.43.index_ref, f32[6,2,8,256]{3,2,1,0:T(8,128)S(1)} %get-tuple-element.44.outer_ref, f32[8,8,256]{2,1,0:T(8,128)S(1)} %get-tuple-element.42._.rate_ref, ...), custom_call_target="tpu_custom_call" | custom-call | bytes 1107000 | tf_op jit(solution)/shard_map/pallas_call | solution.py:590
  14.4 0.2 shard_map.100
  14.6 0.0 collective-permute-done.6.raw_ref
  14.7 0.1 collective-permute-start.7
  14.8 0.6 %collective-permute-start.8 = (f32[6,2,8,256]{3,2,1,0:T(8,128)S(1)}, f32[6,2,8,256]{3,2,1,0:T(8,128)S(1)}, u32[]{:S(2)}, u32[]{:S(2)}) collective-permute-start(f32[6,2,8,256]{3,2,1,0:T(8,128)S(1)} %shard_map.99.halo_ref), channel_id=1, source_target_pairs={{0,8},{4,12},{8,0},{12,4},{1,9},{5,13},{9,1},{13,5},{2,10},{6,14},... | collective-permute-start | bytes 294920 | tf_op jit(solution)/shard_map/ppermute | solution.py:566
  15.4 0.2 collective-permute-start.5
  15.5 2.1 %collective-permute-start.11 = (f32[56,256]{1,0:T(8,128)S(1)}, f32[56,256]{1,0:T(8,128)S(1)}, u32[]{:S(2)}, u32[]{:S(2)}) collective-permute-start(f32[56,256]{1,0:T(8,128)S(1)} %get-tuple-element.65), channel_id=1, source_target_pairs={{0,2},{1,3},{2,0},{3,1},{4,6},{5,7},{6,4},{7,5},{8,10},{9,11},{10,... | collective-permute-start | bytes 172040 | tf_op jit(solution)/shard_map/ppermute | solution.py:570
  17.6 1.3 %collective-permute-start.12 = (f32[56,256]{1,0:T(8,128)S(1)}, f32[56,256]{1,0:T(8,128)S(1)}, u32[]{:S(2)}, u32[]{:S(2)}) collective-permute-start(f32[56,256]{1,0:T(8,128)S(1)} %get-tuple-element.66), channel_id=1, source_target_pairs={{0,3},{1,2},{2,1},{3,0},{4,7},{5,6},{6,5},{7,4},{8,11},{9,10},{10,... | collective-permute-start | bytes 172040 | tf_op jit(solution)/shard_map/ppermute | solution.py:570
  19.0 1.0 %collective-permute-done.8.halo_ref.across_ref = f32[6,2,8,256]{3,2,1,0:T(8,128)S(1)} collective-permute-done((f32[6,2,8,256]{3,2,1,0:T(8,128)S(1)}, f32[6,2,8,256]{3,2,1,0:T(8,128)S(1)}, u32[]{:S(2)}, u32[]{:S(2)}) %collective-permute-start.8) | collective-permute-done | bytes 98336 | tf_op jit(solution)/shard_map/ppermute | solution.py:566
  20.0 0.2 collective-permute-start.13
  20.2 0.0 collective-permute-done.5.sibling_halo_ref
  20.2 0.1 collective-permute-start.10
  20.3 0.0 collective-permute-done.7.raw_ref
  20.3 0.5 %collective-permute-start.9 = (f32[3,2,8,256]{3,2,1,0:T(8,128)S(1)}, f32[3,2,8,256]{3,2,1,0:T(8,128)S(1)}, u32[]{:S(2)}, u32[]{:S(2)}) collective-permute-start(f32[3,2,8,256]{3,2,1,0:T(8,128)S(1)} %get-tuple-element.75), channel_id=1, source_target_pairs={{0,4},{4,0},{8,12},{12,8},{1,5},{5,1},{9,13},{13,9},{2,6},{6,2},{1... | collective-permute-start | bytes 147464 | tf_op jit(solution)/shard_map/ppermute | solution.py:566
  20.8 0.5 %shard_map.102 = (f32[6,8,8,256]{3,2,1,0:T(8,128)S(1)}, f32[6,8,8,256]{3,2,1,0:T(8,128)S(1)}, f32[8,8,256]{2,1,0:T(8,128)S(1)}) custom-call(f32[8]{0:T(128)S(4)} %shard_map.96.weight_ref, f32[8,8,256]{2,1,0:T(8,128)S(1)} %get-tuple-element.38.vrows_ref, f32[6,64,256]{2,1,0:T(8,128)S(1)} %collective-permute-done.7.raw_ref), custom_call_target="tpu_custom_call" | custom-call | bytes 2214000 | tf_op jit(solution)/shard_map/pallas_call | solution.py:590
  21.3 0.7 %shard_map.103 = (f32[6,8,8,256]{3,2,1,0:T(8,128)S(1)}, f32[6,8,8,256]{3,2,1,0:T(8,128)S(1)}, f32[8,8,256]{2,1,0:T(8,128)S(1)}, f32[8,8,256]{2,1,0:T(8,128)S(1)}) custom-call(f32[8]{0:T(128)S(4)} %shard_map.96.weight_ref, f32[8,8,256]{2,1,0:T(8,128)S(1)} %get-tuple-element.38.vrows_ref, f32[6,8,8,256]{3,2,1,0:T(8,128)S(1)} %get-tuple-element.39.rows_ref, ...), custom_call_target="tpu_custom_call" | custom-call | bytes 2583000 | tf_op jit(solution)/shard_map/pallas_call | solution.py:590
  22.0 1.0 %shard_map.104 = (f32[6,8,8,256]{3,2,1,0:T(8,128)S(1)}, f32[6,8,8,256]{3,2,1,0:T(8,128)S(1)}, f32[6,8,8,256]{3,2,1,0:T(8,128)S(1)}, f32[8,8,256]{2,1,0:T(8,128)S(1)}, f32[8,8,256]{2,1,0:T(8,128)S(1)}) custom-call(f32[8]{0:T(128)S(4)} %shard_map.96.weight_ref, f32[8,8,256]{2,1,0:T(8,128)S(1)} %get-tuple-element.38.vrows_ref, ...), custom_call_target="tpu_custom_call" | custom-call | bytes 3690000 | tf_op jit(solution)/shard_map/pallas_call | solution.py:590
  23.0 0.0 collective-permute-done.10.more_1_.more_4_
  23.0 0.0 collective-permute-done.9.more_0_.more_3_
  23.0 0.5 %shard_map.105 = (f32[6,8,8,256]{3,2,1,0:T(8,128)S(1)}, f32[6,8,8,256]{3,2,1,0:T(8,128)S(1)}) custom-call(f32[8]{0:T(128)S(4)} %shard_map.96.weight_ref, f32[8,8,256]{2,1,0:T(8,128)S(1)} %get-tuple-element.38.vrows_ref, f32[6,8,8,256]{3,2,1,0:T(8,128)S(1)} %get-tuple-element.39.rows_ref, f32[6,8,8,256]{3,2,1,0:T(8,128)S(1)} %get-tuple-element.40.sibling_ref, ...), custom_call_target="tpu_custom_call" | custom-call | bytes 1845000 | tf_op jit(solution)/shard_map/pallas_call | solution.py:590
  23.5 0.5 %shard_map.106 = (f32[6,8,8,256]{3,2,1,0:T(8,128)S(1)}, f32[8,8,256]{2,1,0:T(8,128)S(1)}) custom-call(f32[8]{0:T(128)S(4)} %shard_map.96.weight_ref, f32[6,8,8,256]{3,2,1,0:T(8,128)S(1)} %get-tuple-element.63.rows_ref, f32[8,8,256]{2,1,0:T(8,128)S(1)} %get-tuple-element.38.vrows_ref), custom_call_target="tpu_custom_call" | custom-call | bytes 1845000 | tf_op jit(solution)/shard_map/pallas_call | solution.py:590
  24.0 0.0 collective-permute-done.11.more_0_
  24.0 0.0 collective-permute-done.12.more_1_
  24.0 0.7 %collective-permute-done.13.more_2_ = f32[56,256]{1,0:T(8,128)S(1)} collective-permute-done((f32[56,256]{1,0:T(8,128)S(1)}, f32[56,256]{1,0:T(8,128)S(1)}, u32[]{:S(2)}, u32[]{:S(2)}) %collective-permute-start.13) | collective-permute-done | bytes 57376 | tf_op jit(solution)/shard_map/ppermute | solution.py:570
  24.7 0.3 %shard_map.107.halo_ref = f32[6,2,8,256]{3,2,1,0:T(8,128)S(1)} custom-call(s32[37]{0:T(128)S(4)} %get-tuple-element.37.table_ref, s32[8,256]{1,0:T(8,128)S(1)} %get-tuple-element.43.index_ref, f32[8]{0:T(128)S(4)} %shard_map.96.weight_ref, f32[7,2,8,256]{3,2,1,0:T(8,128)S(1)} %get-tuple-element.50.more_0_.outer_ref, ...), custom_call_target="tpu_custom_call" | custom-call | bytes 1107000 | tf_op jit(solution)/shard_map/pallas_call | solution.py:590
  25.1 1.3 %shard_map.108 = (f32[6,64,256]{2,1,0:T(8,128)}, f32[6,64,256]{2,1,0:T(8,128)}) custom-call(s32[37]{0:T(128)S(4)} %get-tuple-element.37.table_ref, f32[6,8,8,256]{3,2,1,0:T(8,128)S(1)} %get-tuple-element.63.rows_ref, f32[8,8,256]{2,1,0:T(8,128)S(1)} %get-tuple-element.38.vrows_ref, f32[6,2,8,256]{3,2,1,0:T(8,128)S(1)} %shard_map.107.halo_ref, ...), custom_call_target="tpu_custom_call" | custom-call | bytes 5535000 | tf_op jit(solution)/shard_map/pallas_call | solution.py:590
  (5 shorter events, 0.1 us)
Async XLA Ops:
  0.6 14.0 %collective-permute-start.6 = (f32[6,64,256]{2,1,0:T(8,128)}, f32[6,64,256]{2,1,0:T(8,128)S(1)}, u32[]{:S(2)}, u32[]{:S(2)}) collective-permute-start(f32[6,64,256]{2,1,0:T(8,128)} %bitcast.6), channel_id=1, source_target_pairs={{0,8},{4,12},{8,0},{12,4},{1,9},{5,13},{9,1},{13,5},{2,10},{6,14},... | collective-permute-start | bytes 1179656 | tf_op jit(solution)/shard_map/ppermute | solution.py:566
  5.0 4.5 %collective-permute-start = (f32[3,8,8,256]{3,2,1,0:T(8,128)S(1)}, f32[3,8,8,256]{3,2,1,0:T(8,128)S(1)}, u32[]{:S(2)}, u32[]{:S(2)}) collective-permute-start(f32[3,8,8,256]{3,2,1,0:T(8,128)S(1)} %get-tuple-element.73), channel_id=1, source_target_pairs={{0,4},{4,0},{8,12},{12,8},{1,5},{5,1},{9,13},{13,9},{2,6},{6,2},{1... | collective-permute-start | bytes 589832 | tf_op jit(solution)/shard_map/ppermute | solution.py:566
  5.0 5.9 %collective-permute-start.1 = (f32[3,8,8,256]{3,2,1,0:T(8,128)S(1)}, f32[3,8,8,256]{3,2,1,0:T(8,128)S(1)}, u32[]{:S(2)}, u32[]{:S(2)}) collective-permute-start(f32[3,8,8,256]{3,2,1,0:T(8,128)S(1)} %get-tuple-element.72), channel_id=1, source_target_pairs={{0,4},{4,0},{8,12},{12,8},{1,5},{5,1},{9,13},{13,9},{2,6},{6,2},{1... | collective-permute-start | bytes 589832 | tf_op jit(solution)/shard_map/ppermute | solution.py:566
  5.5 6.0 %collective-permute-start.2 = (f32[48,256]{1,0:T(8,128)S(1)}, f32[48,256]{1,0:T(8,128)S(1)}, u32[]{:S(2)}, u32[]{:S(2)}) collective-permute-start(f32[48,256]{1,0:T(8,128)S(1)} %get-tuple-element.46), channel_id=1, source_target_pairs={{0,2},{1,3},{2,0},{3,1},{4,6},{5,7},{6,4},{7,5},{8,10},{9,11},{10,... | collective-permute-start | bytes 147464 | tf_op jit(solution)/shard_map/ppermute | solution.py:570
  8.1 6.0 %collective-permute-start.3 = (f32[48,256]{1,0:T(8,128)S(1)}, f32[48,256]{1,0:T(8,128)S(1)}, u32[]{:S(2)}, u32[]{:S(2)}) collective-permute-start(f32[48,256]{1,0:T(8,128)S(1)} %get-tuple-element.47), channel_id=1, source_target_pairs={{0,3},{1,2},{2,1},{3,0},{4,7},{5,6},{6,5},{7,4},{8,11},{9,10},{10,... | collective-permute-start | bytes 147464 | tf_op jit(solution)/shard_map/ppermute | solution.py:570
  9.5 4.6 %collective-permute-start.4 = (f32[48,256]{1,0:T(8,128)S(1)}, f32[48,256]{1,0:T(8,128)S(1)}, u32[]{:S(2)}, u32[]{:S(2)}) collective-permute-start(f32[48,256]{1,0:T(8,128)S(1)} %get-tuple-element.48), channel_id=1, source_target_pairs={{0,1},{1,0},{2,3},{3,2},{4,5},{5,4},{6,7},{7,6},{8,9},{9,8},{10,11... | collective-permute-start | bytes 147464 | tf_op jit(solution)/shard_map/ppermute | solution.py:570
  14.7 5.6 %collective-permute-start.7 = (f32[6,64,256]{2,1,0:T(8,128)S(1)}, f32[6,64,256]{2,1,0:T(8,128)S(1)}, u32[]{:S(2)}, u32[]{:S(2)}) collective-permute-start(f32[6,64,256]{2,1,0:T(8,128)S(1)} %shard_map.101), channel_id=1, source_target_pairs={{0,4},{4,0},{8,12},{12,8},{1,5},{5,1},{9,13},{13,9},{2,6},{6,2},{1... | collective-permute-start | bytes 1179656 | tf_op jit(solution)/shard_map/ppermute | solution.py:566
  14.8 5.2 %collective-permute-start.8 = (f32[6,2,8,256]{3,2,1,0:T(8,128)S(1)}, f32[6,2,8,256]{3,2,1,0:T(8,128)S(1)}, u32[]{:S(2)}, u32[]{:S(2)}) collective-permute-start(f32[6,2,8,256]{3,2,1,0:T(8,128)S(1)} %shard_map.99.halo_ref), channel_id=1, source_target_pairs={{0,8},{4,12},{8,0},{12,4},{1,9},{5,13},{9,1},{13,5},{2,10},{6,14},... | collective-permute-start | bytes 294920 | tf_op jit(solution)/shard_map/ppermute | solution.py:566
  15.4 4.8 %collective-permute-start.5 = (f32[6,2,8,256]{3,2,1,0:T(8,128)S(1)}, f32[6,2,8,256]{3,2,1,0:T(8,128)S(1)}, u32[]{:S(2)}, u32[]{:S(2)}) collective-permute-start(f32[6,2,8,256]{3,2,1,0:T(8,128)S(1)} %shard_map.99.halo_ref), channel_id=1, source_target_pairs={{0,4},{4,0},{8,12},{12,8},{1,5},{5,1},{9,13},{13,9},{2,6},{6,2},{1... | collective-permute-start | bytes 294920 | tf_op jit(solution)/shard_map/ppermute | solution.py:566
  15.5 8.5 %collective-permute-start.11 = (f32[56,256]{1,0:T(8,128)S(1)}, f32[56,256]{1,0:T(8,128)S(1)}, u32[]{:S(2)}, u32[]{:S(2)}) collective-permute-start(f32[56,256]{1,0:T(8,128)S(1)} %get-tuple-element.65), channel_id=1, source_target_pairs={{0,2},{1,3},{2,0},{3,1},{4,6},{5,7},{6,4},{7,5},{8,10},{9,11},{10,... | collective-permute-start | bytes 172040 | tf_op jit(solution)/shard_map/ppermute | solution.py:570
  17.6 6.4 %collective-permute-start.12 = (f32[56,256]{1,0:T(8,128)S(1)}, f32[56,256]{1,0:T(8,128)S(1)}, u32[]{:S(2)}, u32[]{:S(2)}) collective-permute-start(f32[56,256]{1,0:T(8,128)S(1)} %get-tuple-element.66), channel_id=1, source_target_pairs={{0,3},{1,2},{2,1},{3,0},{4,7},{5,6},{6,5},{7,4},{8,11},{9,10},{10,... | collective-permute-start | bytes 172040 | tf_op jit(solution)/shard_map/ppermute | solution.py:570
  20.0 4.8 %collective-permute-start.13 = (f32[56,256]{1,0:T(8,128)S(1)}, f32[56,256]{1,0:T(8,128)S(1)}, u32[]{:S(2)}, u32[]{:S(2)}) collective-permute-start(f32[56,256]{1,0:T(8,128)S(1)} %get-tuple-element.67), channel_id=1, source_target_pairs={{0,1},{1,0},{2,3},{3,2},{4,5},{5,4},{6,7},{7,6},{8,9},{9,8},{10,11... | collective-permute-start | bytes 172040 | tf_op jit(solution)/shard_map/ppermute | solution.py:570
  20.2 2.8 %collective-permute-start.10 = (f32[3,2,8,256]{3,2,1,0:T(8,128)S(1)}, f32[3,2,8,256]{3,2,1,0:T(8,128)S(1)}, u32[]{:S(2)}, u32[]{:S(2)}) collective-permute-start(f32[3,2,8,256]{3,2,1,0:T(8,128)S(1)} %get-tuple-element.74), channel_id=1, source_target_pairs={{0,4},{4,0},{8,12},{12,8},{1,5},{5,1},{9,13},{13,9},{2,6},{6,2},{1... | collective-permute-start | bytes 147464 | tf_op jit(solution)/shard_map/ppermute | solution.py:566
  20.3 2.7 %collective-permute-start.9 = (f32[3,2,8,256]{3,2,1,0:T(8,128)S(1)}, f32[3,2,8,256]{3,2,1,0:T(8,128)S(1)}, u32[]{:S(2)}, u32[]{:S(2)}) collective-permute-start(f32[3,2,8,256]{3,2,1,0:T(8,128)S(1)} %get-tuple-element.75), channel_id=1, source_target_pairs={{0,4},{4,0},{8,12},{12,8},{1,5},{5,1},{9,13},{13,9},{2,6},{6,2},{1... | collective-permute-start | bytes 147464 | tf_op jit(solution)/shard_map/ppermute | solution.py:566

commit v5 on v4

--- a/solution.py
+++ b/solution.py
@@ -216,29 +216,17 @@
     return COURANT / (speeds + 2.0 * SOUND_SPEED + volume * (omega * (0.5 * 4)))
 
 
-def pack_kernel(
-    space_total, block_total, cap,
-    state_ref, volume_ref, counts_in, place_in, links_in, offset_in, flip_in,
-    rows_ref, vrows_ref, outer_ref, table_ref, index_ref, *more
-):
-    sends = more[: space_total - 1]
-    half_ref, arrival, first_ref, inverse_ref, *small = more[space_total - 1 :]
-    counts_ref, place_ref, links_ref, offset_ref, flip_ref = small
-    width = state_ref.shape[2]
-    moves = list(zip([counts_in, place_in, links_in, offset_in, flip_in], small))
-    for h in range(2):
-        lanes = pl.ds(128 * h, 128)
-        moves.append((state_ref.at[:, :, lanes], half_ref.at[h, pl.ds(0, COMPS)]))
-        moves.append((volume_ref.at[:, lanes], half_ref.at[h, COMPS]))
+def get_tables(space_total, block_total, sources, targets, arrival, more=()):
+    moves = list(zip(sources, targets)) + list(more)
     copies = [
         pltpu.make_async_copy(source, target, arrival.at[n])
         for n, (source, target) in enumerate(moves)
     ]
     for copy in copies:
         copy.start()
-    for copy in copies[: len(small)]:
+    for copy in copies[: len(sources)]:
         copy.wait()
-    me = lax.axis_index("space")
+    counts_ref, place_ref, links_ref, first_ref, inverse_ref = targets[:3] + targets[-2:]
     total = jnp.int32(0)
     firsts = []
     for d in range(space_total):
@@ -262,9 +250,69 @@
             first = jnp.where(past, firsts[d], first)
         return link, owner, 2 * (place - first) + (1 - side)
 
+    return block_in, source_of, copies[len(sources) :]
+
+
+def pack_kernel(
+    space_total, block_total, cap,
+    state_ref, volume_ref, counts_in, place_in, links_in,
+    half_ref, volume_half_ref, outer_ref, table_ref, *more
+):
+    sends = more[: space_total - 1]
+    arrival, *small = more[space_total - 1 :]
+    moves = []
+    for c in range(COMPS + 1):
+        for h in range(2):
+            lanes = pl.ds(128 * h, 128)
+            if c < COMPS:
+                moves.append((state_ref.at[c, :, lanes], half_ref.at[h, c]))
+            else:
+                moves.append((volume_ref.at[:, lanes], volume_half_ref.at[h]))
+    block_in, source_of, copies = get_tables(
+        space_total, block_total, (counts_in, place_in, links_in), small, arrival, moves
+    )
+    me = lax.axis_index("space")
+    few = 2 * small[0][me] <= cap
+    for k in range(1, space_total):
+        target = partner(me, k, space_total)
+        for i in range(cap):
+            _, owner, source = source_of(block_in(target, i // 2), i % 2)
+            wanted = jnp.where(owner == me, source, 0)
+            table_ref[(k - 1) * cap + i] = jnp.where(few, i, wanted)
+    even = even_tiles((8, 128))
+    for c in range(COMPS):
+        copies[2 * c].wait()
+        copies[2 * c + 1].wait()
+        for l in range(2):
+            for h in range(2):
+                low = half_ref[h, c, pl.ds(l, 8, stride=8), :]
+                high = half_ref[h, c, pl.ds(6 + l, 8, stride=8), :]
+                outer_ref[c, l, :, pl.ds(128 * h, 128)] = jnp.where(even, low, high)
+        pack_sends(cap, outer_ref, table_ref, sends, (c,))
+    for copy in copies[2 * COMPS :]:
+        copy.wait()
+
+
+def rows_kernel(
+    space_total, block_total, cap,
+    half_ref, volume_half_ref, counts_in, place_in, links_in, offset_in, flip_in,
+    rows_ref, vrows_ref, table_ref, index_ref, arrival, *small
+):
+    block_in, source_of, _ = get_tables(
+        space_total, block_total, (counts_in, place_in, links_in, offset_in, flip_in), small, arrival
+    )
+    counts_ref, _, _, offset_ref, flip_ref = small[:5]
+    width = index_ref.shape[1]
+    for h in range(2):
+        for r in range(8):
+            rows = pl.ds(r, 8, stride=8)
+            lanes = pl.ds(128 * h, 128)
+            vrows_ref[r, :, lanes] = volume_half_ref[h, rows, :]
+            for c in range(COMPS):
+                rows_ref[c, r, :, lanes] = half_ref[h, c, rows, :]
+    me = lax.axis_index("space")
     own_base = (space_total - 1) * POOLED * 2 * cap
-    few = 2 * counts_ref[me] <= cap
-    table_ref[3 * FACES + (space_total - 1) * cap] = counts_ref[me]
+    table_ref[3 * FACES] = counts_ref[me]
     tile = lax.broadcasted_iota(jnp.int32, (FACES, width), 0)
     start = jnp.zeros((FACES, width), jnp.int32)
     turned = jnp.zeros((FACES, width), jnp.int32)
@@ -286,35 +334,13 @@
         turned = jnp.where(tile == f, jnp.where(outside, 0, flip_ref[side, block]), turned)
     column = lax.broadcasted_iota(jnp.int32, (FACES, width), 1)
     index_ref[...] = (start + jnp.where(turned == 1, width - 1 - column, column)) % width
-    for k in range(1, space_total):
-        target = partner(me, k, space_total)
-        for i in range(cap):
-            _, owner, source = source_of(block_in(target, i // 2), i % 2)
-            wanted = jnp.where(owner == me, source, 0)
-            table_ref[3 * FACES + (k - 1) * cap + i] = jnp.where(few, i, wanted)
-    for copy in copies[len(small) :]:
-        copy.wait()
-    for c in range(COMPS + 1):
-        for r in range(8):
-            for h in range(2):
-                row = half_ref[h, c, pl.ds(r, 8, stride=8), :]
-                if c < COMPS:
-                    rows_ref[c, r, :, pl.ds(128 * h, 128)] = row
-                else:
-                    vrows_ref[r, :, pl.ds(128 * h, 128)] = row
-    even = even_tiles((8, width))
-    for c in range(COMPS):
-        for l in range(2):
-            low, high = rows_ref[c, l], rows_ref[c, 6 + l]
-            outer_ref[c, l] = jnp.where(even, low, high)
-    pack_sends(cap, outer_ref, table_ref, sends)
-
-
-def pack_sends(cap, outer_ref, table_ref, sends):
+
+
+def pack_sends(cap, outer_ref, table_ref, sends, comps):
     for k, send_ref in enumerate(sends):
         for i in range(cap):
-            f = table_ref[3 * FACES + k * cap + i]
-            for c in range(outer_ref.shape[0]):
+            f = table_ref[k * cap + i]
+            for c in comps:
                 for l in range(2):
                     send_ref[pl.ds((2 * c + l) * cap + i, 1), :] = outer_ref[c, l, pl.ds(f, 1), :]
 
@@ -379,11 +405,10 @@
     pitchwise(lambda c, r: rows_ref[c, r], vrows_ref, weight_ref[0], part_ref, rate_ref, near_ref, lower_ref)
 
 
-def sibling_pitchwise_kernel(
-    weight_ref, vrows_ref, first_ref, second_ref, rows_ref, part_ref, rate_ref, near_ref, lower_ref
-):
-    for c in range(COMPS):
-        rows_ref[c] = first_ref[c] if c < 3 else second_ref[c - 3]
+def cells_pitchwise_kernel(
+    weight_ref, vrows_ref, raw_ref, rows_ref, part_ref, rate_ref, near_ref, lower_ref, half_ref
+):
+    rows_from(raw_ref, half_ref, rows_ref)
     load = lambda c, r: rows_ref[c, r]
     pitchwise(load, vrows_ref, weight_ref[0], part_ref, rate_ref, near_ref, lower_ref)
 
@@ -427,28 +452,49 @@
             sibling = jnp.where(even, sibling_ref[c, l], sibling_ref[c, l + 6])
             spectral = w_own * q + w_near * sibling
             outer_ref[c, l] = q - rate * (along[c] + part + volume * spectral)
-    pack_sends(cap, outer_ref, table_ref, sends)
-
-
-def near_kernel(
-    weight_ref, vrows_ref,
-    rows_ref, part_ref, rate_ref, halo_ref,
-    sibling_ref, sibling_part_ref, sibling_rate_ref, sibling_halo_ref, _,
-    next_ref, sibling_next_ref, gain_ref, sibling_gain_ref
-):
+    pack_sends(cap, outer_ref, table_ref, sends, range(POOLED))
+
+
+def near_rows(weight_ref, vrows_ref, of, rows):
     omega, w_own, w_across, w_near, w_far = coefficients(weight_ref)
-    for one, other, weight, part, rate_of, halo, out, gain in (
-        (rows_ref, sibling_ref, w_near, part_ref, rate_ref, halo_ref, next_ref, gain_ref),
-        (sibling_ref, rows_ref, w_far, sibling_part_ref, sibling_rate_ref, sibling_halo_ref,
-         sibling_next_ref, sibling_gain_ref),
+    for weight, (one, part, rate_of, halo, out, gain), other in (
+        (w_near, of[0], of[1][0]), (w_far, of[1], of[0][0])
     ):
-        rows = Rows(row_loader(lambda c, r: one[c, r], halo))
-        for r in range(8):
-            along, volume, rate = rows.along(r), vrows_ref[r], rate_of[r]
-            gain[r] = rate * volume
+        load = lambda c, r: one[c, r]
+        if halo is None:
+            line = Rows(lambda r: [one[c, r] for c in range(COMPS)])
+        else:
+            line = Rows(row_loader(load, halo))
+        for r in rows:
+            along, volume, rate = line.along(r), vrows_ref[r], rate_of[r]
             for c in range(COMPS):
                 spectral = w_own * one[c, r] + weight * other[c, r]
                 out[c, r] = one[c, r] - rate * (along[c] + part[c, r] + volume * spectral)
+        if halo is None:
+            for r in range(8):
+                gain[r] = rate_of[r] * vrows_ref[r]
+
+
+def near_inner_kernel(
+    weight_ref, vrows_ref, rows_ref, part_ref, rate_ref,
+    sibling_ref, sibling_part_ref, sibling_rate_ref,
+    next_ref, sibling_next_ref, gain_ref, sibling_gain_ref
+):
+    near_rows(weight_ref, vrows_ref, (
+        (rows_ref, part_ref, rate_ref, None, next_ref, gain_ref),
+        (sibling_ref, sibling_part_ref, sibling_rate_ref, None, sibling_next_ref, sibling_gain_ref),
+    ), range(2, 6))
+
+
+def near_outer_kernel(
+    weight_ref, vrows_ref, rows_ref, part_ref, rate_ref, halo_ref,
+    sibling_ref, sibling_part_ref, sibling_rate_ref, sibling_halo_ref, _, __, ___,
+    next_ref, sibling_next_ref
+):
+    near_rows(weight_ref, vrows_ref, (
+        (rows_ref, part_ref, rate_ref, halo_ref, next_ref, None),
+        (sibling_ref, sibling_part_ref, sibling_rate_ref, sibling_halo_ref, sibling_next_ref, None),
+    ), (0, 1, 6, 7))
 
 
 def across_kernel(
@@ -479,14 +525,6 @@
             term_ref[c, r] = w_own * mine + w_near * sibling + w_across * new
 
 
-def far_pitchwise_kernel(
-    weight_ref, vrows_ref, raw_ref, rows_ref, part_ref, rate_ref, near_ref, lower_ref, half_ref
-):
-    rows_from(raw_ref, half_ref, rows_ref)
-    load = lambda c, r: rows_ref[c, r]
-    pitchwise(load, vrows_ref, weight_ref[0], part_ref, rate_ref, near_ref, lower_ref)
-
-
 def far_kernel(
     weight_ref, vrows_ref, rows_ref, sibling_ref, across_ref, own_ref, partial_ref,
     lacking_ref, lacking_term_ref, far_ref, part_ref, rate_ref, *more
@@ -522,7 +560,7 @@
     new_ref, residual_ref, new_half_ref, residual_half_ref, inverse_ref, left
 ):
     own = Rows(row_loader(lambda c, r: rows_ref[c, r], halo_ref))
-    live_slots = table_ref[3 * FACES + (space_total - 1) * cap]
+    live_slots = table_ref[3 * FACES]
     live = (lax.broadcasted_iota(jnp.int32, vrows_ref.shape[1:], 0) // 2) < live_slots
     for r in range(8):
         inverse_ref[r] = 1.0 / vrows_ref[r]
@@ -578,7 +616,6 @@
     outer = (comps, 2, 8, width)
     plane = (8, 8, width)
     pooled = (POOLED, 2, 8, width)
-    entries = 3 * FACES + (space_total - 1) * cap + 1
     on_chip = lambda shape, dtype=F32: pltpu.VMEM(shape, dtype)
     sends_shape = lambda n: [on_chip((n * 2 * cap, width)) for _ in range(space_total - 1)]
     shifts = [pltpu.VMEM((3,) + full, F32), pltpu.VMEM(full, F32)]
@@ -600,29 +637,31 @@
             ),
         )(*args)
 
-    packed = call(
+    tables = (block_count, block_place, face_links.T, face_offset.T, face_flip.T)
+    in_smem = lambda *shape: pltpu.SMEM(shape, jnp.int32)
+    small = [in_smem(space_total), in_smem(block_total)] + [in_smem(2, block_total)] * 3
+    derived = [in_smem(space_total), in_smem(block_total)]
+    half, volume_half, outer_rows, send_table, *sends = call(
         functools.partial(pack_kernel, space_total, block_total, cap),
         [
-            on_chip(full), on_chip(plane), on_chip(outer),
-            pltpu.SMEM((entries,), jnp.int32),
-            on_chip((FACES, width), jnp.int32), *sends_shape(comps),
+            on_chip((2, comps, row_count, 128)), on_chip((2, row_count, 128)), on_chip(outer),
+            in_smem((space_total - 1) * cap), *sends_shape(comps),
         ],
-        [HBM] * 7,
-        (state, cell_volume, block_count, block_place, face_links.T, face_offset.T, face_flip.T),
-        scratch=[
-            pltpu.VMEM((2, comps + 1, row_count, 128), F32),
-            pltpu.SemaphoreType.DMA((9,)),
-            pltpu.SMEM((space_total,), jnp.int32),
-            pltpu.SMEM((block_total,), jnp.int32),
-            pltpu.SMEM((space_total,), jnp.int32),
-            pltpu.SMEM((block_total,), jnp.int32),
-            *[pltpu.SMEM((2, block_total), jnp.int32)] * 3,
-        ],
-        micros=2.0,
-        out_specs=[VMEM] * 3 + [SMEM] + [VMEM] * space_total,
-    )
-    rows, vrows, outer_rows, table, index = packed[:5]
-    sends = packed[5:]
+        [HBM] * 5,
+        (state, cell_volume, *tables[:3]),
+        scratch=[pltpu.SemaphoreType.DMA((5 + 2 * comps,)), *small[:3], *derived],
+        micros=1.0,
+        out_specs=[VMEM] * 3 + [SMEM] + [VMEM] * (space_total - 1),
+    )
+    rows, vrows, table, index = call(
+        functools.partial(rows_kernel, space_total, block_total, cap),
+        [on_chip(full), on_chip(plane), in_smem(3 * FACES + 1), on_chip((FACES, width), jnp.int32)],
+        [VMEM] * 2 + [HBM] * 5,
+        (half, volume_half, *tables),
+        scratch=[pltpu.SemaphoreType.DMA((5,)), *small, *derived],
+        micros=1.0,
+        out_specs=[VMEM] * 2 + [SMEM, VMEM],
+    )
     weights = pl.pallas_call(
         weight_kernel, out_shape=pltpu.SMEM((8,), F32), in_specs=[SMEM], out_specs=SMEM
     )(frequency)
@@ -643,22 +682,29 @@
         )
 
     across = over_inst(state, 2)
-    sibling_halves = [over_inst(rows[n * 3 : n * 3 + 3], 1) for n in range(2)]
+    sibling_raw = over_inst(state, 1)
     received = over_space(sends)
     part, rate = pitch(rows)
     sibling, sibling_part, sibling_rate = call(
-        sibling_pitchwise_kernel,
+        cells_pitchwise_kernel,
         [on_chip(full)] * 2 + [on_chip(plane)],
-        [SMEM] + [VMEM] * 3,
-        (weights, vrows, *sibling_halves),
-        scratch=shifts,
+        [SMEM] + [VMEM] * 2,
+        (weights, vrows, sibling_raw),
+        scratch=shifts + halves[:1],
         micros=0.5,
+    )
+    own, sibling_next, own_gain, sibling_gain = call(
+        near_inner_kernel,
+        [on_chip(full)] * 2 + [on_chip(plane)] * 2,
+        [SMEM] + [VMEM] * 7,
+        (weights, vrows, rows, part, rate, sibling, sibling_part, sibling_rate),
+        micros=0.3,
     )
     halo = call(
         functools.partial(halo_kernel, space_total, cap),
         on_chip(outer),
         [SMEM] + [VMEM] * (3 + space_total),
-        (table, index, outer_rows, rate, sibling_rate, *received),
+        (table, index, outer_rows, own_gain, sibling_gain, *received),
         scratch=pool,
     )
     across_halo = over_inst(halo, 2)
@@ -667,7 +713,7 @@
         functools.partial(outer_kernel, cap),
         [on_chip(pooled), *sends_shape(POOLED)],
         [SMEM, SMEM] + [VMEM] * 6,
-        (table, weights, rows, vrows, part, rate, halo, sibling),
+        (send_table, weights, rows, vrows, part, rate, halo, sibling),
         micros=0.3,
     )
     next_received = over_space(next_sends)
@@ -682,20 +728,21 @@
     hx = across_halo
     far_halo = [over_inst(hx[n * size : n * size + size], 1) for n in range(pieces)]
     far_rows, far_part, far_rate = call(
-        far_pitchwise_kernel,
+        cells_pitchwise_kernel,
         [on_chip(full)] * 2 + [on_chip(plane)],
         [SMEM] + [VMEM] * 2,
         (weights, vrows, far),
         scratch=shifts + halves[:1],
         micros=0.6,
     )
-    own, sibling_next, own_gain, sibling_gain = call(
-        near_kernel,
-        [on_chip(full)] * 2 + [on_chip(plane)] * 2,
-        [SMEM] + [VMEM] * 10,
+    own, sibling_next = call(
+        near_outer_kernel,
+        [on_chip(full)] * 2,
+        [SMEM] + [VMEM] * 12,
         (weights, vrows, rows, part, rate, halo, sibling, sibling_part, sibling_rate, sibling_halo,
-         far_rate),
-        micros=0.7,
+         far_rate, own, sibling_next),
+        micros=0.4,
+        aliases={11: 0, 12: 1},
     )
     own, partial, across_rows, lacking, lacking_term = call(
         across_kernel,

time: 26.5 us -> 26.5 us (level)
  waiting for transfers between devices: 4.41 us -> 1.66 us
  starting transfers between devices: 12.8 us -> 14.5 us
  Pallas kernels: 7.56 us -> 8.63 us
    ppermute x6, waiting for transfers between devices: 3.4 us -> 1.64 us  [over_space(): lax.ppermute(parts[k - 1], 'space', [(i, partner(i, k, space_total)) for...]
    ppermute x6, starting transfers between devices: 7.84 us -> 9.29 us  [over_space(): lax.ppermute(parts[k - 1], 'space', [(i, partner(i, k, space_total)) for...]
    pallas_call x13 -> x15, Pallas kernels: 7.54 us -> 8.62 us  [call(): pl.pallas_call(kernel, out_shape=out, in_specs=specs, out_specs=out_specs...]
    ppermute x8 -> x7, waiting for transfers between devices: 1.01 us -> 0.02 us  [over_inst(): return lax.ppermute(x, 'inst', [(i, i ^ flip) for i in range(4)])]
    ppermute x8 -> x7, starting transfers between devices: 4.97 us -> 5.25 us  [over_inst(): return lax.ppermute(x, 'inst', [(i, i ^ flip) for i in range(4)])]
  transfers between devices with their start and end apart: 14 -> 13, of which waited for: 4 -> 2; matrix products, arithmetic and copies ran while one was open for 0% -> 0% of each run, Pallas kernels for 23% -> 27%
where the time goes in v5:
time: 26.5 us; the launch traced here: 26.3 us
  starting transfers between devices  14.5 us (55%)
  Pallas kernels  8.63 us (33%)
  waiting for transfers between devices  1.66 us (6%)
  between operations  1.47 us (6%)
    ppermute x6, starting transfers between devices, over_space(): lax.ppermute(parts[k - 1], 'space', [(i, partner(i, k, space_total)) for...  9.29 us
    pallas_call x15, Pallas kernels, call(): pl.pallas_call(kernel, out_shape=out, in_specs=specs, out_specs=out_specs...  8.62 us
    ppermute x7, starting transfers between devices, over_inst(): return lax.ppermute(x, 'inst', [(i, i ^ flip) for i in range(4)])  5.25 us
    ppermute x6, waiting for transfers between devices, over_space(): lax.ppermute(parts[k - 1], 'space', [(i, partner(i, k, space_total)) for...  1.64 us
  transfers between devices with their start and end apart: 13, of which 2 were waited for; matrix products, arithmetic and copies ran while one was open for 0% of the time, Pallas kernels for 27%

profile of v5, /device:TPU:0, one launch (start us, length us, event | category | flops | bytes accessed | tf_op | source)
XLA Modules:
  0.0 26.3 jit_solution(5554500199559855283)
XLA Ops:
  0.6 0.5 %collective-permute-start = (f32[6,64,256]{2,1,0:T(8,128)}, f32[6,64,256]{2,1,0:T(8,128)S(1)}, u32[]{:S(2)}, u32[]{:S(2)}) collective-permute-start(f32[6,64,256]{2,1,0:T(8,128)} %bitcast.6), channel_id=1, source_target_pairs={{0,4},{4,0},{8,12},{12,8},{1,5},{5,1},{9,13},{13,9},{2,6},{6,2},{1... | collective-permute-start | bytes 1179656 | tf_op jit(solution)/shard_map/ppermute | solution.py:604
  1.1 2.6 %collective-permute-start.5 = (f32[6,64,256]{2,1,0:T(8,128)}, f32[6,64,256]{2,1,0:T(8,128)S(1)}, u32[]{:S(2)}, u32[]{:S(2)}) collective-permute-start(f32[6,64,256]{2,1,0:T(8,128)} %bitcast.7), channel_id=1, source_target_pairs={{0,8},{4,12},{8,0},{12,4},{1,9},{5,13},{9,1},{13,5},{2,10},{6,14},... | collective-permute-start | bytes 1179656 | tf_op jit(solution)/shard_map/ppermute | solution.py:604
  3.7 1.2 %shard_map.95 = (f32[2,6,64,128]{3,2,1,0:T(8,128)S(1)}, f32[2,64,128]{2,1,0:T(8,128)S(1)}, f32[6,2,8,256]{3,2,1,0:T(8,128)S(1)}, s32[12]{0:T(128)S(4)}, f32[48,2...) custom-call(f32[6,64,256]{2,1,0:T(8,128)} %bitcast.8, f32[64,256]{1,0:T(8,128)} %volume_ref.1, ...), custom_call_target="tpu_custom_call" | custom-call | bytes 3690000 | tf_op jit(solution)/shard_map/pallas_call | solution.py:627
  4.9 2.7 %collective-permute-start.1 = (f32[48,256]{1,0:T(8,128)S(1)}, f32[48,256]{1,0:T(8,128)S(1)}, u32[]{:S(2)}, u32[]{:S(2)}) collective-permute-start(f32[48,256]{1,0:T(8,128)S(1)} %get-tuple-element.56), channel_id=1, source_target_pairs={{0,2},{1,3},{2,0},{3,1},{4,6},{5,7},{6,4},{7,5},{8,10},{9,11},{10,... | collective-permute-start | bytes 147464 | tf_op jit(solution)/shard_map/ppermute | solution.py:608
  7.6 1.3 %collective-permute-start.2 = (f32[48,256]{1,0:T(8,128)S(1)}, f32[48,256]{1,0:T(8,128)S(1)}, u32[]{:S(2)}, u32[]{:S(2)}) collective-permute-start(f32[48,256]{1,0:T(8,128)S(1)} %get-tuple-element.57), channel_id=1, source_target_pairs={{0,3},{1,2},{2,1},{3,0},{4,7},{5,6},{6,5},{7,4},{8,11},{9,10},{10,... | collective-permute-start | bytes 147464 | tf_op jit(solution)/shard_map/ppermute | solution.py:608
  8.9 0.2 collective-permute-start.3
  9.8 1.0 %shard_map.96 = (f32[6,8,8,256]{3,2,1,0:T(8,128)S(1)}, f32[8,8,256]{2,1,0:T(8,128)S(1)}, s32[25]{0:T(128)S(4)}, s32[8,256]{1,0:T(8,128)S(1)}) custom-call(f32[2,6,64,128]{3,2,1,0:T(8,128)S(1)} %get-tuple-element.42.half_ref, f32[2,64,128]{2,1,0:T(8,128)S(1)} %get-tuple-element.43.volume_half_ref, s32[4]{0:T(128)} %counts_in.3, s32[8]{0:T(128)} %place_in.3, ...), custom_call_target="tpu_custom_call" | custom-call | bytes 3690000 | tf_op jit(solution)/shard_map/pallas_call | solution.py:627
  10.8 0.5 %shard_map.99 = (f32[6,8,8,256]{3,2,1,0:T(8,128)S(1)}, f32[8,8,256]{2,1,0:T(8,128)S(1)}) custom-call(f32[8]{0:T(128)S(4)} %shard_map.97.weight_ref, f32[6,8,8,256]{3,2,1,0:T(8,128)S(1)} %get-tuple-element.46.rows_ref, f32[8,8,256]{2,1,0:T(8,128)S(1)} %get-tuple-element.45.vrows_ref), custom_call_target="tpu_custom_call" | custom-call | bytes 1845000 | tf_op jit(solution)/shard_map/pallas_call | solution.py:627
  11.4 0.0 collective-permute-done.raw_ref
  11.4 0.5 %shard_map.98 = (f32[6,8,8,256]{3,2,1,0:T(8,128)S(1)}, f32[6,8,8,256]{3,2,1,0:T(8,128)S(1)}, f32[8,8,256]{2,1,0:T(8,128)S(1)}) custom-call(f32[8]{0:T(128)S(4)} %shard_map.97.weight_ref, f32[8,8,256]{2,1,0:T(8,128)S(1)} %get-tuple-element.45.vrows_ref, f32[6,64,256]{2,1,0:T(8,128)S(1)} %collective-permute-done.raw_ref), custom_call_target="tpu_custom_call" | custom-call | bytes 1845000 | tf_op jit(solution)/shard_map/pallas_call | solution.py:627
  11.9 0.4 %shard_map.100 = (f32[6,8,8,256]{3,2,1,0:T(8,128)S(1)}, f32[6,8,8,256]{3,2,1,0:T(8,128)S(1)}, f32[8,8,256]{2,1,0:T(8,128)S(1)}, f32[8,8,256]{2,1,0:T(8,128)S(1)}) custom-call(f32[8]{0:T(128)S(4)} %shard_map.97.weight_ref, f32[8,8,256]{2,1,0:T(8,128)S(1)} %get-tuple-element.45.vrows_ref, f32[6,8,8,256]{3,2,1,0:T(8,128)S(1)} %get-tuple-element.46.rows_ref, ...), custom_call_target="tpu_custom_call" | custom-call | bytes 1107000 | tf_op jit(solution)/shard_map/pallas_call | solution.py:627
  12.3 0.0 collective-permute-done.1.more_0_
  12.3 1.3 %collective-permute-done.2.more_1_ = f32[48,256]{1,0:T(8,128)S(1)} collective-permute-done((f32[48,256]{1,0:T(8,128)S(1)}, f32[48,256]{1,0:T(8,128)S(1)}, u32[]{:S(2)}, u32[]{:S(2)}) %collective-permute-start.2) | collective-permute-done | bytes 49184 | tf_op jit(solution)/shard_map/ppermute | solution.py:608
  13.5 0.0 collective-permute-done.3.more_2_
  13.5 0.3 %shard_map.101.halo_ref = f32[6,2,8,256]{3,2,1,0:T(8,128)S(1)} custom-call(s32[25]{0:T(128)S(4)} %get-tuple-element.44.table_ref, s32[8,256]{1,0:T(8,128)S(1)} %get-tuple-element.50.index_ref, f32[6,2,8,256]{3,2,1,0:T(8,128)S(1)} %get-tuple-element.51.outer_ref, f32[8,8,256]{2,1,0:T(8,128)S(1)} %get-tuple-element.54._.own_gain_ref, ...), custom_call_target="tpu_custom_call" | custom-call | bytes 1107000 | tf_op jit(solution)/shard_map/pallas_call | solution.py:627
  13.8 0.2 shard_map.102
  14.1 0.0 collective-permute-done.5.raw_ref
  14.1 0.1 collective-permute-start.6
  14.2 1.4 %collective-permute-start.7 = (f32[6,2,8,256]{3,2,1,0:T(8,128)S(1)}, f32[6,2,8,256]{3,2,1,0:T(8,128)S(1)}, u32[]{:S(2)}, u32[]{:S(2)}) collective-permute-start(f32[6,2,8,256]{3,2,1,0:T(8,128)S(1)} %shard_map.101.halo_ref), channel_id=1, source_target_pairs={{0,8},{4,12},{8,0},{12,4},{1,9},{5,13},{9,1},{13,5},{2,10},{6,14},... | collective-permute-start | bytes 294920 | tf_op jit(solution)/shard_map/ppermute | solution.py:604
  15.6 0.2 collective-permute-start.4
  15.7 2.6 %collective-permute-start.10 = (f32[56,256]{1,0:T(8,128)S(1)}, f32[56,256]{1,0:T(8,128)S(1)}, u32[]{:S(2)}, u32[]{:S(2)}) collective-permute-start(f32[56,256]{1,0:T(8,128)S(1)} %get-tuple-element.75), channel_id=1, source_target_pairs={{0,2},{1,3},{2,0},{3,1},{4,6},{5,7},{6,4},{7,5},{8,10},{9,11},{10,... | collective-permute-start | bytes 172040 | tf_op jit(solution)/shard_map/ppermute | solution.py:608
  18.3 1.3 %collective-permute-start.11 = (f32[56,256]{1,0:T(8,128)S(1)}, f32[56,256]{1,0:T(8,128)S(1)}, u32[]{:S(2)}, u32[]{:S(2)}) collective-permute-start(f32[56,256]{1,0:T(8,128)S(1)} %get-tuple-element.76), channel_id=1, source_target_pairs={{0,3},{1,2},{2,1},{3,0},{4,7},{5,6},{6,5},{7,4},{8,11},{9,10},{10,... | collective-permute-start | bytes 172040 | tf_op jit(solution)/shard_map/ppermute | solution.py:608
  19.7 0.0 collective-permute-done.7.halo_ref.across_ref
  19.7 1.1 %collective-permute-start.12 = (f32[56,256]{1,0:T(8,128)S(1)}, f32[56,256]{1,0:T(8,128)S(1)}, u32[]{:S(2)}, u32[]{:S(2)}) collective-permute-start(f32[56,256]{1,0:T(8,128)S(1)} %get-tuple-element.77), channel_id=1, source_target_pairs={{0,1},{1,0},{2,3},{3,2},{4,5},{5,4},{6,7},{7,6},{8,9},{9,8},{10,11... | collective-permute-start | bytes 172040 | tf_op jit(solution)/shard_map/ppermute | solution.py:608
  20.8 0.0 collective-permute-done.4.sibling_halo_ref
  20.8 0.1 collective-permute-start.8
  20.9 0.0 collective-permute-done.6.raw_ref
  20.9 0.5 %collective-permute-start.9 = (f32[3,2,8,256]{3,2,1,0:T(8,128)S(1)}, f32[3,2,8,256]{3,2,1,0:T(8,128)S(1)}, u32[]{:S(2)}, u32[]{:S(2)}) collective-permute-start(f32[3,2,8,256]{3,2,1,0:T(8,128)S(1)} %get-tuple-element.82), channel_id=1, source_target_pairs={{0,4},{4,0},{8,12},{12,8},{1,5},{5,1},{9,13},{13,9},{2,6},{6,2},{1... | collective-permute-start | bytes 147464 | tf_op jit(solution)/shard_map/ppermute | solution.py:604
  21.4 0.5 %shard_map.104 = (f32[6,8,8,256]{3,2,1,0:T(8,128)S(1)}, f32[6,8,8,256]{3,2,1,0:T(8,128)S(1)}, f32[8,8,256]{2,1,0:T(8,128)S(1)}) custom-call(f32[8]{0:T(128)S(4)} %shard_map.97.weight_ref, f32[8,8,256]{2,1,0:T(8,128)S(1)} %get-tuple-element.45.vrows_ref, f32[6,64,256]{2,1,0:T(8,128)S(1)} %collective-permute-done.6.raw_ref), custom_call_target="tpu_custom_call" | custom-call | bytes 2214000 | tf_op jit(solution)/shard_map/pallas_call | solution.py:627
  21.9 0.4 %shard_map.105 = (f32[6,8,8,256]{3,2,1,0:T(8,128)S(1)}, f32[6,8,8,256]{3,2,1,0:T(8,128)S(1)}) custom-call(f32[8]{0:T(128)S(4)} %shard_map.97.weight_ref, f32[8,8,256]{2,1,0:T(8,128)S(1)} %get-tuple-element.45.vrows_ref, f32[6,8,8,256]{3,2,1,0:T(8,128)S(1)} %get-tuple-element.46.rows_ref, ...), custom_call_target="tpu_custom_call", output_to_operand_aliasing={{0}: (11, {}), {1}: (12, {})} | custom-call | bytes 1476000 | tf_op jit(solution)/shard_map/pallas_call | solution.py:627
  22.4 1.0 %shard_map.106 = (f32[6,8,8,256]{3,2,1,0:T(8,128)S(1)}, f32[6,8,8,256]{3,2,1,0:T(8,128)S(1)}, f32[6,8,8,256]{3,2,1,0:T(8,128)S(1)}, f32[8,8,256]{2,1,0:T(8,128)S(1)}, f32[8,8,256]{2,1,0:T(8,128)S(1)}) custom-call(f32[8]{0:T(128)S(4)} %shard_map.97.weight_ref, f32[8,8,256]{2,1,0:T(8,128)S(1)} %get-tuple-element.45.vrows_ref, ...), custom_call_target="tpu_custom_call" | custom-call | bytes 3690000 | tf_op jit(solution)/shard_map/pallas_call | solution.py:627
  23.4 0.0 collective-permute-done.8.more_0_.more_3_
  23.4 0.0 collective-permute-done.9.more_1_.more_4_
  23.4 0.5 %shard_map.107 = (f32[6,8,8,256]{3,2,1,0:T(8,128)S(1)}, f32[6,8,8,256]{3,2,1,0:T(8,128)S(1)}) custom-call(f32[8]{0:T(128)S(4)} %shard_map.97.weight_ref, f32[8,8,256]{2,1,0:T(8,128)S(1)} %get-tuple-element.45.vrows_ref, f32[6,8,8,256]{3,2,1,0:T(8,128)S(1)} %get-tuple-element.46.rows_ref, f32[6,8,8,256]{3,2,1,0:T(8,128)S(1)} %get-tuple-element.47.sibling_ref, ...), custom_call_target="tpu_custom_call" | custom-call | bytes 1845000 | tf_op jit(solution)/shard_map/pallas_call | solution.py:627
  23.9 0.5 %shard_map.108 = (f32[6,8,8,256]{3,2,1,0:T(8,128)S(1)}, f32[8,8,256]{2,1,0:T(8,128)S(1)}) custom-call(f32[8]{0:T(128)S(4)} %shard_map.97.weight_ref, f32[6,8,8,256]{3,2,1,0:T(8,128)S(1)} %get-tuple-element.73.rows_ref, f32[8,8,256]{2,1,0:T(8,128)S(1)} %get-tuple-element.45.vrows_ref), custom_call_target="tpu_custom_call" | custom-call | bytes 1845000 | tf_op jit(solution)/shard_map/pallas_call | solution.py:627
  24.4 0.0 collective-permute-done.10.more_0_
  24.4 0.4 %collective-permute-done.11.more_1_ = f32[56,256]{1,0:T(8,128)S(1)} collective-permute-done((f32[56,256]{1,0:T(8,128)S(1)}, f32[56,256]{1,0:T(8,128)S(1)}, u32[]{:S(2)}, u32[]{:S(2)}) %collective-permute-start.11) | collective-permute-done | bytes 57376 | tf_op jit(solution)/shard_map/ppermute | solution.py:608
  24.7 0.0 collective-permute-done.12.more_2_
  24.7 0.3 %shard_map.109.halo_ref = f32[6,2,8,256]{3,2,1,0:T(8,128)S(1)} custom-call(s32[25]{0:T(128)S(4)} %get-tuple-element.44.table_ref, s32[8,256]{1,0:T(8,128)S(1)} %get-tuple-element.50.index_ref, f32[8]{0:T(128)S(4)} %shard_map.97.weight_ref, f32[7,2,8,256]{3,2,1,0:T(8,128)S(1)} %get-tuple-element.60.more_0_.outer_ref, ...), custom_call_target="tpu_custom_call" | custom-call | bytes 1107000 | tf_op jit(solution)/shard_map/pallas_call | solution.py:627
  25.1 1.3 %shard_map.110 = (f32[6,64,256]{2,1,0:T(8,128)}, f32[6,64,256]{2,1,0:T(8,128)}) custom-call(s32[25]{0:T(128)S(4)} %get-tuple-element.44.table_ref, f32[6,8,8,256]{3,2,1,0:T(8,128)S(1)} %get-tuple-element.73.rows_ref, f32[8,8,256]{2,1,0:T(8,128)S(1)} %get-tuple-element.45.vrows_ref, f32[6,2,8,256]{3,2,1,0:T(8,128)S(1)} %shard_map.109.halo_ref, ...), custom_call_target="tpu_custom_call" | custom-call | bytes 5535000 | tf_op jit(solution)/shard_map/pallas_call | solution.py:627
  (4 shorter events, 0.1 us)
Async XLA Ops:
  0.6 10.7 %collective-permute-start = (f32[6,64,256]{2,1,0:T(8,128)}, f32[6,64,256]{2,1,0:T(8,128)S(1)}, u32[]{:S(2)}, u32[]{:S(2)}) collective-permute-start(f32[6,64,256]{2,1,0:T(8,128)} %bitcast.6), channel_id=1, source_target_pairs={{0,4},{4,0},{8,12},{12,8},{1,5},{5,1},{9,13},{13,9},{2,6},{6,2},{1... | collective-permute-start | bytes 1179656 | tf_op jit(solution)/shard_map/ppermute | solution.py:604
  1.1 12.9 %collective-permute-start.5 = (f32[6,64,256]{2,1,0:T(8,128)}, f32[6,64,256]{2,1,0:T(8,128)S(1)}, u32[]{:S(2)}, u32[]{:S(2)}) collective-permute-start(f32[6,64,256]{2,1,0:T(8,128)} %bitcast.7), channel_id=1, source_target_pairs={{0,8},{4,12},{8,0},{12,4},{1,9},{5,13},{9,1},{13,5},{2,10},{6,14},... | collective-permute-start | bytes 1179656 | tf_op jit(solution)/shard_map/ppermute | solution.py:604
  4.9 7.4 %collective-permute-start.1 = (f32[48,256]{1,0:T(8,128)S(1)}, f32[48,256]{1,0:T(8,128)S(1)}, u32[]{:S(2)}, u32[]{:S(2)}) collective-permute-start(f32[48,256]{1,0:T(8,128)S(1)} %get-tuple-element.56), channel_id=1, source_target_pairs={{0,2},{1,3},{2,0},{3,1},{4,6},{5,7},{6,4},{7,5},{8,10},{9,11},{10,... | collective-permute-start | bytes 147464 | tf_op jit(solution)/shard_map/ppermute | solution.py:608
  7.6 6.0 %collective-permute-start.2 = (f32[48,256]{1,0:T(8,128)S(1)}, f32[48,256]{1,0:T(8,128)S(1)}, u32[]{:S(2)}, u32[]{:S(2)}) collective-permute-start(f32[48,256]{1,0:T(8,128)S(1)} %get-tuple-element.57), channel_id=1, source_target_pairs={{0,3},{1,2},{2,1},{3,0},{4,7},{5,6},{6,5},{7,4},{8,11},{9,10},{10,... | collective-permute-start | bytes 147464 | tf_op jit(solution)/shard_map/ppermute | solution.py:608
  8.9 4.6 %collective-permute-start.3 = (f32[48,256]{1,0:T(8,128)S(1)}, f32[48,256]{1,0:T(8,128)S(1)}, u32[]{:S(2)}, u32[]{:S(2)}) collective-permute-start(f32[48,256]{1,0:T(8,128)S(1)} %get-tuple-element.58), channel_id=1, source_target_pairs={{0,1},{1,0},{2,3},{3,2},{4,5},{5,4},{6,7},{7,6},{8,9},{9,8},{10,11... | collective-permute-start | bytes 147464 | tf_op jit(solution)/shard_map/ppermute | solution.py:608
  14.1 6.8 %collective-permute-start.6 = (f32[6,64,256]{2,1,0:T(8,128)S(1)}, f32[6,64,256]{2,1,0:T(8,128)S(1)}, u32[]{:S(2)}, u32[]{:S(2)}) collective-permute-start(f32[6,64,256]{2,1,0:T(8,128)S(1)} %shard_map.103), channel_id=1, source_target_pairs={{0,4},{4,0},{8,12},{12,8},{1,5},{5,1},{9,13},{13,9},{2,6},{6,2},{1... | collective-permute-start | bytes 1179656 | tf_op jit(solution)/shard_map/ppermute | solution.py:604
  14.2 5.5 %collective-permute-start.7 = (f32[6,2,8,256]{3,2,1,0:T(8,128)S(1)}, f32[6,2,8,256]{3,2,1,0:T(8,128)S(1)}, u32[]{:S(2)}, u32[]{:S(2)}) collective-permute-start(f32[6,2,8,256]{3,2,1,0:T(8,128)S(1)} %shard_map.101.halo_ref), channel_id=1, source_target_pairs={{0,8},{4,12},{8,0},{12,4},{1,9},{5,13},{9,1},{13,5},{2,10},{6,14},... | collective-permute-start | bytes 294920 | tf_op jit(solution)/shard_map/ppermute | solution.py:604
  15.6 5.2 %collective-permute-start.4 = (f32[6,2,8,256]{3,2,1,0:T(8,128)S(1)}, f32[6,2,8,256]{3,2,1,0:T(8,128)S(1)}, u32[]{:S(2)}, u32[]{:S(2)}) collective-permute-start(f32[6,2,8,256]{3,2,1,0:T(8,128)S(1)} %shard_map.101.halo_ref), channel_id=1, source_target_pairs={{0,4},{4,0},{8,12},{12,8},{1,5},{5,1},{9,13},{13,9},{2,6},{6,2},{1... | collective-permute-start | bytes 294920 | tf_op jit(solution)/shard_map/ppermute | solution.py:604
  15.7 8.6 %collective-permute-start.10 = (f32[56,256]{1,0:T(8,128)S(1)}, f32[56,256]{1,0:T(8,128)S(1)}, u32[]{:S(2)}, u32[]{:S(2)}) collective-permute-start(f32[56,256]{1,0:T(8,128)S(1)} %get-tuple-element.75), channel_id=1, source_target_pairs={{0,2},{1,3},{2,0},{3,1},{4,6},{5,7},{6,4},{7,5},{8,10},{9,11},{10,... | collective-permute-start | bytes 172040 | tf_op jit(solution)/shard_map/ppermute | solution.py:608
  18.3 6.4 %collective-permute-start.11 = (f32[56,256]{1,0:T(8,128)S(1)}, f32[56,256]{1,0:T(8,128)S(1)}, u32[]{:S(2)}, u32[]{:S(2)}) collective-permute-start(f32[56,256]{1,0:T(8,128)S(1)} %get-tuple-element.76), channel_id=1, source_target_pairs={{0,3},{1,2},{2,1},{3,0},{4,7},{5,6},{6,5},{7,4},{8,11},{9,10},{10,... | collective-permute-start | bytes 172040 | tf_op jit(solution)/shard_map/ppermute | solution.py:608
  19.7 5.1 %collective-permute-start.12 = (f32[56,256]{1,0:T(8,128)S(1)}, f32[56,256]{1,0:T(8,128)S(1)}, u32[]{:S(2)}, u32[]{:S(2)}) collective-permute-start(f32[56,256]{1,0:T(8,128)S(1)} %get-tuple-element.77), channel_id=1, source_target_pairs={{0,1},{1,0},{2,3},{3,2},{4,5},{5,4},{6,7},{7,6},{8,9},{9,8},{10,11... | collective-permute-start | bytes 172040 | tf_op jit(solution)/shard_map/ppermute | solution.py:608
  20.8 2.5 %collective-permute-start.8 = (f32[3,2,8,256]{3,2,1,0:T(8,128)S(1)}, f32[3,2,8,256]{3,2,1,0:T(8,128)S(1)}, u32[]{:S(2)}, u32[]{:S(2)}) collective-permute-start(f32[3,2,8,256]{3,2,1,0:T(8,128)S(1)} %get-tuple-element.83), channel_id=1, source_target_pairs={{0,4},{4,0},{8,12},{12,8},{1,5},{5,1},{9,13},{13,9},{2,6},{6,2},{1... | collective-permute-start | bytes 147464 | tf_op jit(solution)/shard_map/ppermute | solution.py:604
  20.9 2.5 %collective-permute-start.9 = (f32[3,2,8,256]{3,2,1,0:T(8,128)S(1)}, f32[3,2,8,256]{3,2,1,0:T(8,128)S(1)}, u32[]{:S(2)}, u32[]{:S(2)}) collective-permute-start(f32[3,2,8,256]{3,2,1,0:T(8,128)S(1)} %get-tuple-element.82), channel_id=1, source_target_pairs={{0,4},{4,0},{8,12},{12,8},{1,5},{5,1},{9,13},{13,9},{2,6},{6,2},{1... | collective-permute-start | bytes 147464 | tf_op jit(solution)/shard_map/ppermute | solution.py:604

commit v6 on v5

--- a/solution.py
+++ b/solution.py
@@ -405,6 +405,17 @@
     pitchwise(lambda c, r: rows_ref[c, r], vrows_ref, weight_ref[0], part_ref, rate_ref, near_ref, lower_ref)
 
 
+def halves_pitchwise_kernel(
+    weight_ref, vrows_ref, low_ref, high_ref, rows_ref, part_ref, rate_ref, near_ref, lower_ref
+):
+    for h, half_ref in enumerate((low_ref, high_ref)):
+        for c in range(COMPS):
+            for r in range(8):
+                rows_ref[c, r, :, pl.ds(128 * h, 128)] = half_ref[c, pl.ds(r, 8, stride=8), :]
+    load = lambda c, r: rows_ref[c, r]
+    pitchwise(load, vrows_ref, weight_ref[0], part_ref, rate_ref, near_ref, lower_ref)
+
+
 def cells_pitchwise_kernel(
     weight_ref, vrows_ref, raw_ref, rows_ref, part_ref, rate_ref, near_ref, lower_ref, half_ref
 ):
@@ -548,11 +559,9 @@
 
 
 def join_halos(parts, halo_ref):
-    size = COMPS // len(parts)
-    for n, part in enumerate(parts):
-        for c in range(size):
-            for l in range(2):
-                halo_ref[n * size + c, l] = part[c, l]
+    tiles = [part[pl.ds(row, 8), :] for part in parts for row in range(0, part.shape[0], 8)]
+    for n, tile in enumerate(tiles):
+        halo_ref[n // 2, n % 2] = tile
 
 
 def last_kernel(
@@ -682,15 +691,15 @@
         )
 
     across = over_inst(state, 2)
-    sibling_raw = over_inst(state, 1)
+    sibling_halves = [over_inst(half[h], 1) for h in range(2)]
     received = over_space(sends)
     part, rate = pitch(rows)
     sibling, sibling_part, sibling_rate = call(
-        cells_pitchwise_kernel,
+        halves_pitchwise_kernel,
         [on_chip(full)] * 2 + [on_chip(plane)],
-        [SMEM] + [VMEM] * 2,
-        (weights, vrows, sibling_raw),
-        scratch=shifts + halves[:1],
+        [SMEM] + [VMEM] * 3,
+        (weights, vrows, *sibling_halves),
+        scratch=shifts,
         micros=0.5,
     )
     own, sibling_next, own_gain, sibling_gain = call(
@@ -723,10 +732,8 @@
         )
 
     far = over_inst(after(across, next_outer), 1)
-    pieces = 2
-    size = comps // pieces
-    hx = across_halo
-    far_halo = [over_inst(hx[n * size : n * size + size], 1) for n in range(pieces)]
+    stacked = across_halo.reshape(comps * 2 * 8, width)
+    far_halo = [over_inst(x, 1) for x in (stacked[:48], stacked[48:])]
     far_rows, far_part, far_rate = call(
         cells_pitchwise_kernel,
         [on_chip(full)] * 2 + [on_chip(plane)],

time: 26.5 us -> 26.4 us (level)
  starting transfers between devices: 14.5 us -> 13.2 us
  waiting for transfers between devices: 1.66 us -> 2.82 us
    ppermute x6, starting transfers between devices: 9.29 us -> 8.25 us  [over_space(): lax.ppermute(parts[k - 1], 'space', [(i, partner(i, k, space_total)) for...]
    ppermute x7 -> x8, waiting for transfers between devices: 0.02 us -> 0.92 us  [over_inst(): return lax.ppermute(x, 'inst', [(i, i ^ flip) for i in range(4)])]
    ppermute x7 -> x8, starting transfers between devices: 5.25 us -> 4.97 us  [over_inst(): return lax.ppermute(x, 'inst', [(i, i ^ flip) for i in range(4)])]
  transfers between devices with their start and end apart: 13 -> 14, of which waited for: 2 -> 3; matrix products, arithmetic and copies ran while one was open for 0% -> 0% of each run, Pallas kernels for 27% -> 27%
where the time goes in v6:
time: 26.4 us; the launch traced here: 26.2 us
  starting transfers between devices  13.2 us (50%)
  Pallas kernels  8.61 us (33%)
  waiting for transfers between devices  2.82 us (11%)
  between operations  1.49 us (6%)
    pallas_call x15, Pallas kernels, call(): pl.pallas_call(kernel, out_shape=out, in_specs=specs, out_specs=out_specs...  8.59 us
    ppermute x6, starting transfers between devices, over_space(): lax.ppermute(parts[k - 1], 'space', [(i, partner(i, k, space_total)) for...  8.25 us
    ppermute x8, starting transfers between devices, over_inst(): return lax.ppermute(x, 'inst', [(i, i ^ flip) for i in range(4)])  4.97 us
    ppermute x6, waiting for transfers between devices, over_space(): lax.ppermute(parts[k - 1], 'space', [(i, partner(i, k, space_total)) for...  1.9 us
    ppermute x8, waiting for transfers between devices, over_inst(): return lax.ppermute(x, 'inst', [(i, i ^ flip) for i in range(4)])  0.92 us
  transfers between devices with their start and end apart: 14, of which 3 were waited for; matrix products, arithmetic and copies ran while one was open for 0% of the time, Pallas kernels for 27%

profile of v6, /device:TPU:0, one launch (start us, length us, event | category | flops | bytes accessed | tf_op | source)
XLA Modules:
  0.0 26.2 jit_solution(15971907435015934146)
XLA Ops:
  0.6 3.0 %collective-permute-start.6 = (f32[6,64,256]{2,1,0:T(8,128)}, f32[6,64,256]{2,1,0:T(8,128)S(1)}, u32[]{:S(2)}, u32[]{:S(2)}) collective-permute-start(f32[6,64,256]{2,1,0:T(8,128)} %bitcast.12), channel_id=1, source_target_pairs={{0,8},{4,12},{8,0},{12,4},{1,9},{5,13},{9,1},{13,5},{2,10},{6,14},... | collective-permute-start | bytes 1179656 | tf_op jit(solution)/shard_map/ppermute | solution.py:613
  3.6 1.2 %shard_map.95 = (f32[2,6,64,128]{3,2,1,0:T(8,128)S(1)}, f32[2,64,128]{2,1,0:T(8,128)S(1)}, f32[6,2,8,256]{3,2,1,0:T(8,128)S(1)}, s32[12]{0:T(128)S(4)}, f32[48,2...) custom-call(f32[6,64,256]{2,1,0:T(8,128)} %bitcast.13, f32[64,256]{1,0:T(8,128)} %volume_ref.1, ...), custom_call_target="tpu_custom_call" | custom-call | bytes 3690000 | tf_op jit(solution)/shard_map/pallas_call | solution.py:636
  4.9 0.1 collective-permute-start
  5.0 0.5 %collective-permute-start.1 = (f32[6,64,128]{2,1,0:T(8,128)S(1)}, f32[6,64,128]{2,1,0:T(8,128)S(1)}, u32[]{:S(2)}, u32[]{:S(2)}) collective-permute-start(f32[6,64,128]{2,1,0:T(8,128)S(1)} %get-tuple-element.82), channel_id=1, source_target_pairs={{0,4},{4,0},{8,12},{12,8},{1,5},{5,1},{9,13},{13,9},{2,6},{6,2},{1... | collective-permute-start | bytes 589832 | tf_op jit(solution)/shard_map/ppermute | solution.py:613
  5.4 2.6 %collective-permute-start.2 = (f32[48,256]{1,0:T(8,128)S(1)}, f32[48,256]{1,0:T(8,128)S(1)}, u32[]{:S(2)}, u32[]{:S(2)}) collective-permute-start(f32[48,256]{1,0:T(8,128)S(1)} %get-tuple-element.56), channel_id=1, source_target_pairs={{0,2},{1,3},{2,0},{3,1},{4,6},{5,7},{6,4},{7,5},{8,10},{9,11},{10,... | collective-permute-start | bytes 147464 | tf_op jit(solution)/shard_map/ppermute | solution.py:617
  8.0 1.3 %collective-permute-start.3 = (f32[48,256]{1,0:T(8,128)S(1)}, f32[48,256]{1,0:T(8,128)S(1)}, u32[]{:S(2)}, u32[]{:S(2)}) collective-permute-start(f32[48,256]{1,0:T(8,128)S(1)} %get-tuple-element.57), channel_id=1, source_target_pairs={{0,3},{1,2},{2,1},{3,0},{4,7},{5,6},{6,5},{7,4},{8,11},{9,10},{10,... | collective-permute-start | bytes 147464 | tf_op jit(solution)/shard_map/ppermute | solution.py:617
  9.4 0.0 collective-permute-done.low_ref
  9.4 0.2 collective-permute-start.4
  10.3 1.0 %shard_map.96 = (f32[6,8,8,256]{3,2,1,0:T(8,128)S(1)}, f32[8,8,256]{2,1,0:T(8,128)S(1)}, s32[25]{0:T(128)S(4)}, s32[8,256]{1,0:T(8,128)S(1)}) custom-call(f32[2,6,64,128]{3,2,1,0:T(8,128)S(1)} %get-tuple-element.42.half_ref, f32[2,64,128]{2,1,0:T(8,128)S(1)} %get-tuple-element.43.volume_half_ref, s32[4]{0:T(128)} %counts_in.3, s32[8]{0:T(128)} %place_in.3, ...), custom_call_target="tpu_custom_call" | custom-call | bytes 3690000 | tf_op jit(solution)/shard_map/pallas_call | solution.py:636
  11.3 0.5 %shard_map.99 = (f32[6,8,8,256]{3,2,1,0:T(8,128)S(1)}, f32[8,8,256]{2,1,0:T(8,128)S(1)}) custom-call(f32[8]{0:T(128)S(4)} %shard_map.97.weight_ref, f32[6,8,8,256]{3,2,1,0:T(8,128)S(1)} %get-tuple-element.46.rows_ref, f32[8,8,256]{2,1,0:T(8,128)S(1)} %get-tuple-element.45.vrows_ref), custom_call_target="tpu_custom_call" | custom-call | bytes 1845000 | tf_op jit(solution)/shard_map/pallas_call | solution.py:636
  11.8 0.0 collective-permute-done.1.high_ref
  11.8 0.5 %shard_map.98 = (f32[6,8,8,256]{3,2,1,0:T(8,128)S(1)}, f32[6,8,8,256]{3,2,1,0:T(8,128)S(1)}, f32[8,8,256]{2,1,0:T(8,128)S(1)}) custom-call(f32[8]{0:T(128)S(4)} %shard_map.97.weight_ref, f32[8,8,256]{2,1,0:T(8,128)S(1)} %get-tuple-element.45.vrows_ref, f32[6,64,128]{2,1,0:T(8,128)S(1)} %collective-permute-done.low_ref, ...), custom_call_target="tpu_custom_call" | custom-call | bytes 1845000 | tf_op jit(solution)/shard_map/pallas_call | solution.py:636
  12.4 0.4 %shard_map.100 = (f32[6,8,8,256]{3,2,1,0:T(8,128)S(1)}, f32[6,8,8,256]{3,2,1,0:T(8,128)S(1)}, f32[8,8,256]{2,1,0:T(8,128)S(1)}, f32[8,8,256]{2,1,0:T(8,128)S(1)}) custom-call(f32[8]{0:T(128)S(4)} %shard_map.97.weight_ref, f32[8,8,256]{2,1,0:T(8,128)S(1)} %get-tuple-element.45.vrows_ref, f32[6,8,8,256]{3,2,1,0:T(8,128)S(1)} %get-tuple-element.46.rows_ref, ...), custom_call_target="tpu_custom_call" | custom-call | bytes 1107000 | tf_op jit(solution)/shard_map/pallas_call | solution.py:636
  12.7 0.0 collective-permute-done.2.more_0_
  12.7 1.3 %collective-permute-done.3.more_1_ = f32[48,256]{1,0:T(8,128)S(1)} collective-permute-done((f32[48,256]{1,0:T(8,128)S(1)}, f32[48,256]{1,0:T(8,128)S(1)}, u32[]{:S(2)}, u32[]{:S(2)}) %collective-permute-start.3) | collective-permute-done | bytes 49184 | tf_op jit(solution)/shard_map/ppermute | solution.py:617
  14.0 0.0 collective-permute-done.4.more_2_
  14.0 0.3 %shard_map.101.halo_ref = f32[6,2,8,256]{3,2,1,0:T(8,128)S(1)} custom-call(s32[25]{0:T(128)S(4)} %get-tuple-element.44.table_ref, s32[8,256]{1,0:T(8,128)S(1)} %get-tuple-element.50.index_ref, f32[6,2,8,256]{3,2,1,0:T(8,128)S(1)} %get-tuple-element.51.outer_ref, f32[8,8,256]{2,1,0:T(8,128)S(1)} %get-tuple-element.54._.own_gain_ref, ...), custom_call_target="tpu_custom_call" | custom-call | bytes 1107000 | tf_op jit(solution)/shard_map/pallas_call | solution.py:636
  14.3 0.2 shard_map.102
  14.5 0.0 collective-permute-done.6.raw_ref
  14.6 0.1 collective-permute-start.7
  14.7 0.6 %collective-permute-start.8 = (f32[6,2,8,256]{3,2,1,0:T(8,128)S(1)}, f32[6,2,8,256]{3,2,1,0:T(8,128)S(1)}, u32[]{:S(2)}, u32[]{:S(2)}) collective-permute-start(f32[6,2,8,256]{3,2,1,0:T(8,128)S(1)} %shard_map.101.halo_ref), channel_id=1, source_target_pairs={{0,8},{4,12},{8,0},{12,4},{1,9},{5,13},{9,1},{13,5},{2,10},{6,14},... | collective-permute-start | bytes 294920 | tf_op jit(solution)/shard_map/ppermute | solution.py:613
  15.3 0.2 collective-permute-start.5
  15.4 2.2 %collective-permute-start.11 = (f32[56,256]{1,0:T(8,128)S(1)}, f32[56,256]{1,0:T(8,128)S(1)}, u32[]{:S(2)}, u32[]{:S(2)}) collective-permute-start(f32[56,256]{1,0:T(8,128)S(1)} %get-tuple-element.75), channel_id=1, source_target_pairs={{0,2},{1,3},{2,0},{3,1},{4,6},{5,7},{6,4},{7,5},{8,10},{9,11},{10,... | collective-permute-start | bytes 172040 | tf_op jit(solution)/shard_map/ppermute | solution.py:617
  17.6 1.3 %collective-permute-start.12 = (f32[56,256]{1,0:T(8,128)S(1)}, f32[56,256]{1,0:T(8,128)S(1)}, u32[]{:S(2)}, u32[]{:S(2)}) collective-permute-start(f32[56,256]{1,0:T(8,128)S(1)} %get-tuple-element.76), channel_id=1, source_target_pairs={{0,3},{1,2},{2,1},{3,0},{4,7},{5,6},{6,5},{7,4},{8,11},{9,10},{10,... | collective-permute-start | bytes 172040 | tf_op jit(solution)/shard_map/ppermute | solution.py:617
  19.0 0.9 %collective-permute-done.8.halo_ref.across_ref = f32[6,2,8,256]{3,2,1,0:T(8,128)S(1)} collective-permute-done((f32[6,2,8,256]{3,2,1,0:T(8,128)S(1)}, f32[6,2,8,256]{3,2,1,0:T(8,128)S(1)}, u32[]{:S(2)}, u32[]{:S(2)}) %collective-permute-start.8) | collective-permute-done | bytes 98336 | tf_op jit(solution)/shard_map/ppermute | solution.py:613
  19.9 0.5 %collective-permute-start.13 = (f32[56,256]{1,0:T(8,128)S(1)}, f32[56,256]{1,0:T(8,128)S(1)}, u32[]{:S(2)}, u32[]{:S(2)}) collective-permute-start(f32[56,256]{1,0:T(8,128)S(1)} %get-tuple-element.77), channel_id=1, source_target_pairs={{0,1},{1,0},{2,3},{3,2},{4,5},{5,4},{6,7},{7,6},{8,9},{9,8},{10,11... | collective-permute-start | bytes 172040 | tf_op jit(solution)/shard_map/ppermute | solution.py:617
  20.4 0.0 collective-permute-done.5.sibling_halo_ref
  20.4 0.1 collective-permute-start.10
  20.5 0.0 collective-permute-done.7.raw_ref
  20.5 0.5 %collective-permute-start.9 = (f32[48,256]{1,0:T(8,128)S(1)}, f32[48,256]{1,0:T(8,128)S(1)}, u32[]{:S(2)}, u32[]{:S(2)}) collective-permute-start(f32[48,256]{1,0:T(8,128)S(1)} %bitcast.14), channel_id=1, source_target_pairs={{0,4},{4,0},{8,12},{12,8},{1,5},{5,1},{9,13},{13,9},{2,6},{6,2},{1... | collective-permute-start | bytes 147464 | tf_op jit(solution)/shard_map/ppermute | solution.py:613
  21.0 0.5 %shard_map.104 = (f32[6,8,8,256]{3,2,1,0:T(8,128)S(1)}, f32[6,8,8,256]{3,2,1,0:T(8,128)S(1)}, f32[8,8,256]{2,1,0:T(8,128)S(1)}) custom-call(f32[8]{0:T(128)S(4)} %shard_map.97.weight_ref, f32[8,8,256]{2,1,0:T(8,128)S(1)} %get-tuple-element.45.vrows_ref, f32[6,64,256]{2,1,0:T(8,128)S(1)} %collective-permute-done.7.raw_ref), custom_call_target="tpu_custom_call" | custom-call | bytes 2214000 | tf_op jit(solution)/shard_map/pallas_call | solution.py:636
  21.6 0.4 %shard_map.105 = (f32[6,8,8,256]{3,2,1,0:T(8,128)S(1)}, f32[6,8,8,256]{3,2,1,0:T(8,128)S(1)}) custom-call(f32[8]{0:T(128)S(4)} %shard_map.97.weight_ref, f32[8,8,256]{2,1,0:T(8,128)S(1)} %get-tuple-element.45.vrows_ref, f32[6,8,8,256]{3,2,1,0:T(8,128)S(1)} %get-tuple-element.46.rows_ref, ...), custom_call_target="tpu_custom_call", output_to_operand_aliasing={{0}: (11, {}), {1}: (12, {})} | custom-call | bytes 1476000 | tf_op jit(solution)/shard_map/pallas_call | solution.py:636
  22.0 1.0 %shard_map.106 = (f32[6,8,8,256]{3,2,1,0:T(8,128)S(1)}, f32[6,8,8,256]{3,2,1,0:T(8,128)S(1)}, f32[6,8,8,256]{3,2,1,0:T(8,128)S(1)}, f32[8,8,256]{2,1,0:T(8,128)S(1)}, f32[8,8,256]{2,1,0:T(8,128)S(1)}) custom-call(f32[8]{0:T(128)S(4)} %shard_map.97.weight_ref, f32[8,8,256]{2,1,0:T(8,128)S(1)} %get-tuple-element.45.vrows_ref, ...), custom_call_target="tpu_custom_call" | custom-call | bytes 3690000 | tf_op jit(solution)/shard_map/pallas_call | solution.py:636
  23.0 0.0 collective-permute-done.10.more_1_.more_4_
  23.0 0.0 collective-permute-done.9.more_0_.more_3_
  23.0 0.5 %shard_map.107 = (f32[6,8,8,256]{3,2,1,0:T(8,128)S(1)}, f32[6,8,8,256]{3,2,1,0:T(8,128)S(1)}) custom-call(f32[8]{0:T(128)S(4)} %shard_map.97.weight_ref, f32[8,8,256]{2,1,0:T(8,128)S(1)} %get-tuple-element.45.vrows_ref, f32[6,8,8,256]{3,2,1,0:T(8,128)S(1)} %get-tuple-element.46.rows_ref, f32[6,8,8,256]{3,2,1,0:T(8,128)S(1)} %get-tuple-element.47.sibling_ref, ...), custom_call_target="tpu_custom_call" | custom-call | bytes 1845000 | tf_op jit(solution)/shard_map/pallas_call | solution.py:636
  23.5 0.5 %shard_map.108 = (f32[6,8,8,256]{3,2,1,0:T(8,128)S(1)}, f32[8,8,256]{2,1,0:T(8,128)S(1)}) custom-call(f32[8]{0:T(128)S(4)} %shard_map.97.weight_ref, f32[6,8,8,256]{3,2,1,0:T(8,128)S(1)} %get-tuple-element.73.rows_ref, f32[8,8,256]{2,1,0:T(8,128)S(1)} %get-tuple-element.45.vrows_ref), custom_call_target="tpu_custom_call" | custom-call | bytes 1845000 | tf_op jit(solution)/shard_map/pallas_call | solution.py:636
  24.0 0.0 collective-permute-done.11.more_0_
  24.0 0.0 collective-permute-done.12.more_1_
  24.0 0.6 %collective-permute-done.13.more_2_ = f32[56,256]{1,0:T(8,128)S(1)} collective-permute-done((f32[56,256]{1,0:T(8,128)S(1)}, f32[56,256]{1,0:T(8,128)S(1)}, u32[]{:S(2)}, u32[]{:S(2)}) %collective-permute-start.13) | collective-permute-done | bytes 57376 | tf_op jit(solution)/shard_map/ppermute | solution.py:617
  24.6 0.3 %shard_map.109.halo_ref = f32[6,2,8,256]{3,2,1,0:T(8,128)S(1)} custom-call(s32[25]{0:T(128)S(4)} %get-tuple-element.44.table_ref, s32[8,256]{1,0:T(8,128)S(1)} %get-tuple-element.50.index_ref, f32[8]{0:T(128)S(4)} %shard_map.97.weight_ref, f32[7,2,8,256]{3,2,1,0:T(8,128)S(1)} %get-tuple-element.60.more_0_.outer_ref, ...), custom_call_target="tpu_custom_call" | custom-call | bytes 1107000 | tf_op jit(solution)/shard_map/pallas_call | solution.py:636
  24.9 1.3 %shard_map.110 = (f32[6,64,256]{2,1,0:T(8,128)}, f32[6,64,256]{2,1,0:T(8,128)}) custom-call(s32[25]{0:T(128)S(4)} %get-tuple-element.44.table_ref, f32[6,8,8,256]{3,2,1,0:T(8,128)S(1)} %get-tuple-element.73.rows_ref, f32[8,8,256]{2,1,0:T(8,128)S(1)} %get-tuple-element.45.vrows_ref, f32[6,2,8,256]{3,2,1,0:T(8,128)S(1)} %shard_map.109.halo_ref, ...), custom_call_target="tpu_custom_call" | custom-call | bytes 5535000 | tf_op jit(solution)/shard_map/pallas_call | solution.py:636
  (5 shorter events, 0.1 us)
Async XLA Ops:
  0.6 13.9 %collective-permute-start.6 = (f32[6,64,256]{2,1,0:T(8,128)}, f32[6,64,256]{2,1,0:T(8,128)S(1)}, u32[]{:S(2)}, u32[]{:S(2)}) collective-permute-start(f32[6,64,256]{2,1,0:T(8,128)} %bitcast.12), channel_id=1, source_target_pairs={{0,8},{4,12},{8,0},{12,4},{1,9},{5,13},{9,1},{13,5},{2,10},{6,14},... | collective-permute-start | bytes 1179656 | tf_op jit(solution)/shard_map/ppermute | solution.py:613
  4.9 4.5 %collective-permute-start = (f32[6,64,128]{2,1,0:T(8,128)S(1)}, f32[6,64,128]{2,1,0:T(8,128)S(1)}, u32[]{:S(2)}, u32[]{:S(2)}) collective-permute-start(f32[6,64,128]{2,1,0:T(8,128)S(1)} %get-tuple-element.83), channel_id=1, source_target_pairs={{0,4},{4,0},{8,12},{12,8},{1,5},{5,1},{9,13},{13,9},{2,6},{6,2},{1... | collective-permute-start | bytes 589832 | tf_op jit(solution)/shard_map/ppermute | solution.py:613
  5.0 6.9 %collective-permute-start.1 = (f32[6,64,128]{2,1,0:T(8,128)S(1)}, f32[6,64,128]{2,1,0:T(8,128)S(1)}, u32[]{:S(2)}, u32[]{:S(2)}) collective-permute-start(f32[6,64,128]{2,1,0:T(8,128)S(1)} %get-tuple-element.82), channel_id=1, source_target_pairs={{0,4},{4,0},{8,12},{12,8},{1,5},{5,1},{9,13},{13,9},{2,6},{6,2},{1... | collective-permute-start | bytes 589832 | tf_op jit(solution)/shard_map/ppermute | solution.py:613
  5.4 7.3 %collective-permute-start.2 = (f32[48,256]{1,0:T(8,128)S(1)}, f32[48,256]{1,0:T(8,128)S(1)}, u32[]{:S(2)}, u32[]{:S(2)}) collective-permute-start(f32[48,256]{1,0:T(8,128)S(1)} %get-tuple-element.56), channel_id=1, source_target_pairs={{0,2},{1,3},{2,0},{3,1},{4,6},{5,7},{6,4},{7,5},{8,10},{9,11},{10,... | collective-permute-start | bytes 147464 | tf_op jit(solution)/shard_map/ppermute | solution.py:617
  8.0 6.0 %collective-permute-start.3 = (f32[48,256]{1,0:T(8,128)S(1)}, f32[48,256]{1,0:T(8,128)S(1)}, u32[]{:S(2)}, u32[]{:S(2)}) collective-permute-start(f32[48,256]{1,0:T(8,128)S(1)} %get-tuple-element.57), channel_id=1, source_target_pairs={{0,3},{1,2},{2,1},{3,0},{4,7},{5,6},{6,5},{7,4},{8,11},{9,10},{10,... | collective-permute-start | bytes 147464 | tf_op jit(solution)/shard_map/ppermute | solution.py:617
  9.4 4.6 %collective-permute-start.4 = (f32[48,256]{1,0:T(8,128)S(1)}, f32[48,256]{1,0:T(8,128)S(1)}, u32[]{:S(2)}, u32[]{:S(2)}) collective-permute-start(f32[48,256]{1,0:T(8,128)S(1)} %get-tuple-element.58), channel_id=1, source_target_pairs={{0,1},{1,0},{2,3},{3,2},{4,5},{5,4},{6,7},{7,6},{8,9},{9,8},{10,11... | collective-permute-start | bytes 147464 | tf_op jit(solution)/shard_map/ppermute | solution.py:617
  14.6 5.9 %collective-permute-start.7 = (f32[6,64,256]{2,1,0:T(8,128)S(1)}, f32[6,64,256]{2,1,0:T(8,128)S(1)}, u32[]{:S(2)}, u32[]{:S(2)}) collective-permute-start(f32[6,64,256]{2,1,0:T(8,128)S(1)} %shard_map.103), channel_id=1, source_target_pairs={{0,4},{4,0},{8,12},{12,8},{1,5},{5,1},{9,13},{13,9},{2,6},{6,2},{1... | collective-permute-start | bytes 1179656 | tf_op jit(solution)/shard_map/ppermute | solution.py:613
  14.7 5.2 %collective-permute-start.8 = (f32[6,2,8,256]{3,2,1,0:T(8,128)S(1)}, f32[6,2,8,256]{3,2,1,0:T(8,128)S(1)}, u32[]{:S(2)}, u32[]{:S(2)}) collective-permute-start(f32[6,2,8,256]{3,2,1,0:T(8,128)S(1)} %shard_map.101.halo_ref), channel_id=1, source_target_pairs={{0,8},{4,12},{8,0},{12,4},{1,9},{5,13},{9,1},{13,5},{2,10},{6,14},... | collective-permute-start | bytes 294920 | tf_op jit(solution)/shard_map/ppermute | solution.py:613
  15.3 5.2 %collective-permute-start.5 = (f32[6,2,8,256]{3,2,1,0:T(8,128)S(1)}, f32[6,2,8,256]{3,2,1,0:T(8,128)S(1)}, u32[]{:S(2)}, u32[]{:S(2)}) collective-permute-start(f32[6,2,8,256]{3,2,1,0:T(8,128)S(1)} %shard_map.101.halo_ref), channel_id=1, source_target_pairs={{0,4},{4,0},{8,12},{12,8},{1,5},{5,1},{9,13},{13,9},{2,6},{6,2},{1... | collective-permute-start | bytes 294920 | tf_op jit(solution)/shard_map/ppermute | solution.py:613
  15.4 8.5 %collective-permute-start.11 = (f32[56,256]{1,0:T(8,128)S(1)}, f32[56,256]{1,0:T(8,128)S(1)}, u32[]{:S(2)}, u32[]{:S(2)}) collective-permute-start(f32[56,256]{1,0:T(8,128)S(1)} %get-tuple-element.75), channel_id=1, source_target_pairs={{0,2},{1,3},{2,0},{3,1},{4,6},{5,7},{6,4},{7,5},{8,10},{9,11},{10,... | collective-permute-start | bytes 172040 | tf_op jit(solution)/shard_map/ppermute | solution.py:617
  17.6 6.4 %collective-permute-start.12 = (f32[56,256]{1,0:T(8,128)S(1)}, f32[56,256]{1,0:T(8,128)S(1)}, u32[]{:S(2)}, u32[]{:S(2)}) collective-permute-start(f32[56,256]{1,0:T(8,128)S(1)} %get-tuple-element.76), channel_id=1, source_target_pairs={{0,3},{1,2},{2,1},{3,0},{4,7},{5,6},{6,5},{7,4},{8,11},{9,10},{10,... | collective-permute-start | bytes 172040 | tf_op jit(solution)/shard_map/ppermute | solution.py:617
  19.9 4.7 %collective-permute-start.13 = (f32[56,256]{1,0:T(8,128)S(1)}, f32[56,256]{1,0:T(8,128)S(1)}, u32[]{:S(2)}, u32[]{:S(2)}) collective-permute-start(f32[56,256]{1,0:T(8,128)S(1)} %get-tuple-element.77), channel_id=1, source_target_pairs={{0,1},{1,0},{2,3},{3,2},{4,5},{5,4},{6,7},{7,6},{8,9},{9,8},{10,11... | collective-permute-start | bytes 172040 | tf_op jit(solution)/shard_map/ppermute | solution.py:617
  20.4 2.5 %collective-permute-start.10 = (f32[48,256]{1,0:T(8,128)S(1)}, f32[48,256]{1,0:T(8,128)S(1)}, u32[]{:S(2)}, u32[]{:S(2)}) collective-permute-start(f32[48,256]{1,0:T(8,128)S(1)} %bitcast.15), channel_id=1, source_target_pairs={{0,4},{4,0},{8,12},{12,8},{1,5},{5,1},{9,13},{13,9},{2,6},{6,2},{1... | collective-permute-start | bytes 147464 | tf_op jit(solution)/shard_map/ppermute | solution.py:613
  20.5 2.5 %collective-permute-start.9 = (f32[48,256]{1,0:T(8,128)S(1)}, f32[48,256]{1,0:T(8,128)S(1)}, u32[]{:S(2)}, u32[]{:S(2)}) collective-permute-start(f32[48,256]{1,0:T(8,128)S(1)} %bitcast.14), channel_id=1, source_target_pairs={{0,4},{4,0},{8,12},{12,8},{1,5},{5,1},{9,13},{13,9},{2,6},{6,2},{1... | collective-permute-start | bytes 147464 | tf_op jit(solution)/shard_map/ppermute | solution.py:613

commit v7 on v6

--- a/solution.py
+++ b/solution.py
@@ -733,7 +733,7 @@
 
     far = over_inst(after(across, next_outer), 1)
     stacked = across_halo.reshape(comps * 2 * 8, width)
-    far_halo = [over_inst(x, 1) for x in (stacked[:48], stacked[48:])]
+    far_halo = [over_inst(x, 1) for x in (stacked[:16], stacked[16:56], stacked[56:])]
     far_rows, far_part, far_rate = call(
         cells_pitchwise_kernel,
         [on_chip(full)] * 2 + [on_chip(plane)],

time: 26.4 us -> 26.1 us (0.989)
  starting transfers between devices: 13.2 us -> 12.9 us
    ppermute x6, waiting for transfers between devices: 1.9 us -> 1.29 us  [over_space(): lax.ppermute(parts[k - 1], 'space', [(i, partner(i, k, space_total)) for...]
    ppermute x8 -> x9, waiting for transfers between devices: 0.92 us -> 1.49 us  [over_inst(): return lax.ppermute(x, 'inst', [(i, i ^ flip) for i in range(4)])]
    ppermute x6, starting transfers between devices: 8.25 us -> 7.72 us  [over_space(): lax.ppermute(parts[k - 1], 'space', [(i, partner(i, k, space_total)) for...]
    ppermute x8 -> x9, starting transfers between devices: 4.97 us -> 5.19 us  [over_inst(): return lax.ppermute(x, 'inst', [(i, i ^ flip) for i in range(4)])]
  transfers between devices with their start and end apart: 14 -> 15, of which waited for: 3 -> 3; matrix products, arithmetic and copies ran while one was open for 0% -> 0% of each run, Pallas kernels for 27% -> 27%
where the time goes in v7:
time: 26.1 us; the launch traced here: 25.8 us
  starting transfers between devices  12.9 us (49%)
  Pallas kernels  8.62 us (33%)
  waiting for transfers between devices  2.78 us (11%)
  between operations  1.46 us (6%)
    pallas_call x15, Pallas kernels, call(): pl.pallas_call(kernel, out_shape=out, in_specs=specs, out_specs=out_specs...  8.6 us
    ppermute x6, starting transfers between devices, over_space(): lax.ppermute(parts[k - 1], 'space', [(i, partner(i, k, space_total)) for...  7.72 us
    ppermute x9, starting transfers between devices, over_inst(): return lax.ppermute(x, 'inst', [(i, i ^ flip) for i in range(4)])  5.19 us
    ppermute x9, waiting for transfers between devices, over_inst(): return lax.ppermute(x, 'inst', [(i, i ^ flip) for i in range(4)])  1.49 us
    ppermute x6, waiting for transfers between devices, over_space(): lax.ppermute(parts[k - 1], 'space', [(i, partner(i, k, space_total)) for...  1.29 us
  transfers between devices with their start and end apart: 15, of which 3 were waited for; matrix products, arithmetic and copies ran while one was open for 0% of the time, Pallas kernels for 27%

profile of v7, /device:TPU:0, one launch (start us, length us, event | category | flops | bytes accessed | tf_op | source)
XLA Modules:
  0.0 25.8 jit_solution(14001030988002922776)
XLA Ops:
  0.6 3.0 %collective-permute-start.6 = (f32[6,64,256]{2,1,0:T(8,128)}, f32[6,64,256]{2,1,0:T(8,128)S(1)}, u32[]{:S(2)}, u32[]{:S(2)}) collective-permute-start(f32[6,64,256]{2,1,0:T(8,128)} %bitcast.14), channel_id=1, source_target_pairs={{0,8},{4,12},{8,0},{12,4},{1,9},{5,13},{9,1},{13,5},{2,10},{6,14},... | collective-permute-start | bytes 1179656 | tf_op jit(solution)/shard_map/ppermute | solution.py:613
  3.6 1.2 %shard_map.95 = (f32[2,6,64,128]{3,2,1,0:T(8,128)S(1)}, f32[2,64,128]{2,1,0:T(8,128)S(1)}, f32[6,2,8,256]{3,2,1,0:T(8,128)S(1)}, s32[12]{0:T(128)S(4)}, f32[48,2...) custom-call(f32[6,64,256]{2,1,0:T(8,128)} %bitcast.15, f32[64,256]{1,0:T(8,128)} %volume_ref.1, ...), custom_call_target="tpu_custom_call" | custom-call | bytes 3690000 | tf_op jit(solution)/shard_map/pallas_call | solution.py:636
  4.9 0.1 collective-permute-start
  5.0 0.5 %collective-permute-start.1 = (f32[6,64,128]{2,1,0:T(8,128)S(1)}, f32[6,64,128]{2,1,0:T(8,128)S(1)}, u32[]{:S(2)}, u32[]{:S(2)}) collective-permute-start(f32[6,64,128]{2,1,0:T(8,128)S(1)} %get-tuple-element.82), channel_id=1, source_target_pairs={{0,4},{4,0},{8,12},{12,8},{1,5},{5,1},{9,13},{13,9},{2,6},{6,2},{1... | collective-permute-start | bytes 589832 | tf_op jit(solution)/shard_map/ppermute | solution.py:613
  5.4 2.6 %collective-permute-start.2 = (f32[48,256]{1,0:T(8,128)S(1)}, f32[48,256]{1,0:T(8,128)S(1)}, u32[]{:S(2)}, u32[]{:S(2)}) collective-permute-start(f32[48,256]{1,0:T(8,128)S(1)} %get-tuple-element.56), channel_id=1, source_target_pairs={{0,2},{1,3},{2,0},{3,1},{4,6},{5,7},{6,4},{7,5},{8,10},{9,11},{10,... | collective-permute-start | bytes 147464 | tf_op jit(solution)/shard_map/ppermute | solution.py:617
  8.0 1.3 %collective-permute-start.3 = (f32[48,256]{1,0:T(8,128)S(1)}, f32[48,256]{1,0:T(8,128)S(1)}, u32[]{:S(2)}, u32[]{:S(2)}) collective-permute-start(f32[48,256]{1,0:T(8,128)S(1)} %get-tuple-element.57), channel_id=1, source_target_pairs={{0,3},{1,2},{2,1},{3,0},{4,7},{5,6},{6,5},{7,4},{8,11},{9,10},{10,... | collective-permute-start | bytes 147464 | tf_op jit(solution)/shard_map/ppermute | solution.py:617
  9.4 0.0 collective-permute-done.low_ref
  9.4 0.2 collective-permute-start.4
  10.3 1.0 %shard_map.96 = (f32[6,8,8,256]{3,2,1,0:T(8,128)S(1)}, f32[8,8,256]{2,1,0:T(8,128)S(1)}, s32[25]{0:T(128)S(4)}, s32[8,256]{1,0:T(8,128)S(1)}) custom-call(f32[2,6,64,128]{3,2,1,0:T(8,128)S(1)} %get-tuple-element.42.half_ref, f32[2,64,128]{2,1,0:T(8,128)S(1)} %get-tuple-element.43.volume_half_ref, s32[4]{0:T(128)} %counts_in.3, s32[8]{0:T(128)} %place_in.3, ...), custom_call_target="tpu_custom_call" | custom-call | bytes 3690000 | tf_op jit(solution)/shard_map/pallas_call | solution.py:636
  11.3 0.5 %shard_map.99 = (f32[6,8,8,256]{3,2,1,0:T(8,128)S(1)}, f32[8,8,256]{2,1,0:T(8,128)S(1)}) custom-call(f32[8]{0:T(128)S(4)} %shard_map.97.weight_ref, f32[6,8,8,256]{3,2,1,0:T(8,128)S(1)} %get-tuple-element.46.rows_ref, f32[8,8,256]{2,1,0:T(8,128)S(1)} %get-tuple-element.45.vrows_ref), custom_call_target="tpu_custom_call" | custom-call | bytes 1845000 | tf_op jit(solution)/shard_map/pallas_call | solution.py:636
  11.8 0.0 collective-permute-done.1.high_ref
  11.8 0.5 %shard_map.98 = (f32[6,8,8,256]{3,2,1,0:T(8,128)S(1)}, f32[6,8,8,256]{3,2,1,0:T(8,128)S(1)}, f32[8,8,256]{2,1,0:T(8,128)S(1)}) custom-call(f32[8]{0:T(128)S(4)} %shard_map.97.weight_ref, f32[8,8,256]{2,1,0:T(8,128)S(1)} %get-tuple-element.45.vrows_ref, f32[6,64,128]{2,1,0:T(8,128)S(1)} %collective-permute-done.low_ref, ...), custom_call_target="tpu_custom_call" | custom-call | bytes 1845000 | tf_op jit(solution)/shard_map/pallas_call | solution.py:636
  12.4 0.4 %shard_map.100 = (f32[6,8,8,256]{3,2,1,0:T(8,128)S(1)}, f32[6,8,8,256]{3,2,1,0:T(8,128)S(1)}, f32[8,8,256]{2,1,0:T(8,128)S(1)}, f32[8,8,256]{2,1,0:T(8,128)S(1)}) custom-call(f32[8]{0:T(128)S(4)} %shard_map.97.weight_ref, f32[8,8,256]{2,1,0:T(8,128)S(1)} %get-tuple-element.45.vrows_ref, f32[6,8,8,256]{3,2,1,0:T(8,128)S(1)} %get-tuple-element.46.rows_ref, ...), custom_call_target="tpu_custom_call" | custom-call | bytes 1107000 | tf_op jit(solution)/shard_map/pallas_call | solution.py:636
  12.7 0.0 collective-permute-done.2.more_0_
  12.7 1.3 %collective-permute-done.3.more_1_ = f32[48,256]{1,0:T(8,128)S(1)} collective-permute-done((f32[48,256]{1,0:T(8,128)S(1)}, f32[48,256]{1,0:T(8,128)S(1)}, u32[]{:S(2)}, u32[]{:S(2)}) %collective-permute-start.3) | collective-permute-done | bytes 49184 | tf_op jit(solution)/shard_map/ppermute | solution.py:617
  14.0 0.0 collective-permute-done.4.more_2_
  14.0 0.3 %shard_map.101.halo_ref = f32[6,2,8,256]{3,2,1,0:T(8,128)S(1)} custom-call(s32[25]{0:T(128)S(4)} %get-tuple-element.44.table_ref, s32[8,256]{1,0:T(8,128)S(1)} %get-tuple-element.50.index_ref, f32[6,2,8,256]{3,2,1,0:T(8,128)S(1)} %get-tuple-element.51.outer_ref, f32[8,8,256]{2,1,0:T(8,128)S(1)} %get-tuple-element.54._.own_gain_ref, ...), custom_call_target="tpu_custom_call" | custom-call | bytes 1107000 | tf_op jit(solution)/shard_map/pallas_call | solution.py:636
  14.3 0.6 %collective-permute-start.8 = (f32[6,2,8,256]{3,2,1,0:T(8,128)S(1)}, f32[6,2,8,256]{3,2,1,0:T(8,128)S(1)}, u32[]{:S(2)}, u32[]{:S(2)}) collective-permute-start(f32[6,2,8,256]{3,2,1,0:T(8,128)S(1)} %shard_map.101.halo_ref), channel_id=1, source_target_pairs={{0,8},{4,12},{8,0},{12,4},{1,9},{5,13},{9,1},{13,5},{2,10},{6,14},... | collective-permute-start | bytes 294920 | tf_op jit(solution)/shard_map/ppermute | solution.py:613
  14.9 0.0 collective-permute-start.5
  14.9 0.2 shard_map.102
  15.1 1.9 %collective-permute-start.12 = (f32[56,256]{1,0:T(8,128)S(1)}, f32[56,256]{1,0:T(8,128)S(1)}, u32[]{:S(2)}, u32[]{:S(2)}) collective-permute-start(f32[56,256]{1,0:T(8,128)S(1)} %get-tuple-element.75), channel_id=1, source_target_pairs={{0,2},{1,3},{2,0},{3,1},{4,6},{5,7},{6,4},{7,5},{8,10},{9,11},{10,... | collective-permute-start | bytes 172040 | tf_op jit(solution)/shard_map/ppermute | solution.py:617
  17.0 1.1 %collective-permute-start.13 = (f32[56,256]{1,0:T(8,128)S(1)}, f32[56,256]{1,0:T(8,128)S(1)}, u32[]{:S(2)}, u32[]{:S(2)}) collective-permute-start(f32[56,256]{1,0:T(8,128)S(1)} %get-tuple-element.76), channel_id=1, source_target_pairs={{0,3},{1,2},{2,1},{3,0},{4,7},{5,6},{6,5},{7,4},{8,11},{9,10},{10,... | collective-permute-start | bytes 172040 | tf_op jit(solution)/shard_map/ppermute | solution.py:617
  18.1 0.0 collective-permute-done.6.raw_ref
  18.1 0.6 %collective-permute-start.14 = (f32[56,256]{1,0:T(8,128)S(1)}, f32[56,256]{1,0:T(8,128)S(1)}, u32[]{:S(2)}, u32[]{:S(2)}) collective-permute-start(f32[56,256]{1,0:T(8,128)S(1)} %get-tuple-element.77), channel_id=1, source_target_pairs={{0,1},{1,0},{2,3},{3,2},{4,5},{5,4},{6,7},{7,6},{8,9},{9,8},{10,11... | collective-permute-start | bytes 172040 | tf_op jit(solution)/shard_map/ppermute | solution.py:617
  18.7 0.2 collective-permute-done.8.halo_ref.across_ref
  19.0 0.0 collective-permute-start.7
  19.0 0.0 collective-permute-done.5.sibling_halo_ref
  19.0 0.5 %collective-permute-start.9 = (f32[16,256]{1,0:T(8,128)S(1)}, f32[16,256]{1,0:T(8,128)S(1)}, u32[]{:S(2)}, u32[]{:S(2)}) collective-permute-start(f32[16,256]{1,0:T(8,128)S(1)} %slice_bitcast_fusion.2), channel_id=1, source_target_pairs={{0,4},{4,0},{8,12},{12,8},{1,5},{5,1},{9,13},{13,9},{2,6},{6,2},{1... | collective-permute-start | bytes 49160 | tf_op jit(solution)/shard_map/ppermute | solution.py:613
  19.5 1.2 %collective-permute-done.9.more_0_.more_3_ = f32[16,256]{1,0:T(8,128)S(1)} collective-permute-done((f32[16,256]{1,0:T(8,128)S(1)}, f32[16,256]{1,0:T(8,128)S(1)}, u32[]{:S(2)}, u32[]{:S(2)}) %collective-permute-start.9) | collective-permute-done | bytes 16416 | tf_op jit(solution)/shard_map/ppermute | solution.py:613
  20.7 0.1 collective-permute-start.10
  20.9 0.0 collective-permute-done.7.raw_ref
  20.9 0.4 %collective-permute-start.11 = (f32[40,256]{1,0:T(8,128)S(1)}, f32[40,256]{1,0:T(8,128)S(1)}, u32[]{:S(2)}, u32[]{:S(2)}) collective-permute-start(f32[40,256]{1,0:T(8,128)S(1)} %get-tuple-element.84), channel_id=1, source_target_pairs={{0,4},{4,0},{8,12},{12,8},{1,5},{5,1},{9,13},{13,9},{2,6},{6,2},{1... | collective-permute-start | bytes 122888 | tf_op jit(solution)/shard_map/ppermute | solution.py:613
  21.2 0.5 %shard_map.104 = (f32[6,8,8,256]{3,2,1,0:T(8,128)S(1)}, f32[6,8,8,256]{3,2,1,0:T(8,128)S(1)}, f32[8,8,256]{2,1,0:T(8,128)S(1)}) custom-call(f32[8]{0:T(128)S(4)} %shard_map.97.weight_ref, f32[8,8,256]{2,1,0:T(8,128)S(1)} %get-tuple-element.45.vrows_ref, f32[6,64,256]{2,1,0:T(8,128)S(1)} %collective-permute-done.7.raw_ref), custom_call_target="tpu_custom_call" | custom-call | bytes 2214000 | tf_op jit(solution)/shard_map/pallas_call | solution.py:636
  21.8 0.4 %shard_map.105 = (f32[6,8,8,256]{3,2,1,0:T(8,128)S(1)}, f32[6,8,8,256]{3,2,1,0:T(8,128)S(1)}) custom-call(f32[8]{0:T(128)S(4)} %shard_map.97.weight_ref, f32[8,8,256]{2,1,0:T(8,128)S(1)} %get-tuple-element.45.vrows_ref, f32[6,8,8,256]{3,2,1,0:T(8,128)S(1)} %get-tuple-element.46.rows_ref, ...), custom_call_target="tpu_custom_call", output_to_operand_aliasing={{0}: (11, {}), {1}: (12, {})} | custom-call | bytes 1476000 | tf_op jit(solution)/shard_map/pallas_call | solution.py:636
  22.2 1.0 %shard_map.106 = (f32[6,8,8,256]{3,2,1,0:T(8,128)S(1)}, f32[6,8,8,256]{3,2,1,0:T(8,128)S(1)}, f32[6,8,8,256]{3,2,1,0:T(8,128)S(1)}, f32[8,8,256]{2,1,0:T(8,128)S(1)}, f32[8,8,256]{2,1,0:T(8,128)S(1)}) custom-call(f32[8]{0:T(128)S(4)} %shard_map.97.weight_ref, f32[8,8,256]{2,1,0:T(8,128)S(1)} %get-tuple-element.45.vrows_ref, ...), custom_call_target="tpu_custom_call" | custom-call | bytes 3690000 | tf_op jit(solution)/shard_map/pallas_call | solution.py:636
  23.2 0.0 collective-permute-done.10.more_1_.more_4_
  23.2 0.0 collective-permute-done.11.more_2_.more_5_
  23.2 0.5 %shard_map.107 = (f32[6,8,8,256]{3,2,1,0:T(8,128)S(1)}, f32[6,8,8,256]{3,2,1,0:T(8,128)S(1)}) custom-call(f32[8]{0:T(128)S(4)} %shard_map.97.weight_ref, f32[8,8,256]{2,1,0:T(8,128)S(1)} %get-tuple-element.45.vrows_ref, f32[6,8,8,256]{3,2,1,0:T(8,128)S(1)} %get-tuple-element.46.rows_ref, f32[6,8,8,256]{3,2,1,0:T(8,128)S(1)} %get-tuple-element.47.sibling_ref, ...), custom_call_target="tpu_custom_call" | custom-call | bytes 1845000 | tf_op jit(solution)/shard_map/pallas_call | solution.py:636
  23.7 0.5 %shard_map.108 = (f32[6,8,8,256]{3,2,1,0:T(8,128)S(1)}, f32[8,8,256]{2,1,0:T(8,128)S(1)}) custom-call(f32[8]{0:T(128)S(4)} %shard_map.97.weight_ref, f32[6,8,8,256]{3,2,1,0:T(8,128)S(1)} %get-tuple-element.73.rows_ref, f32[8,8,256]{2,1,0:T(8,128)S(1)} %get-tuple-element.45.vrows_ref), custom_call_target="tpu_custom_call" | custom-call | bytes 1845000 | tf_op jit(solution)/shard_map/pallas_call | solution.py:636
  24.2 0.0 collective-permute-done.12.more_0_
  24.2 0.0 collective-permute-done.13.more_1_
  24.2 0.0 collective-permute-done.14.more_2_
  24.2 0.3 %shard_map.109.halo_ref = f32[6,2,8,256]{3,2,1,0:T(8,128)S(1)} custom-call(s32[25]{0:T(128)S(4)} %get-tuple-element.44.table_ref, s32[8,256]{1,0:T(8,128)S(1)} %get-tuple-element.50.index_ref, f32[8]{0:T(128)S(4)} %shard_map.97.weight_ref, f32[7,2,8,256]{3,2,1,0:T(8,128)S(1)} %get-tuple-element.60.more_0_.outer_ref, ...), custom_call_target="tpu_custom_call" | custom-call | bytes 1107000 | tf_op jit(solution)/shard_map/pallas_call | solution.py:636
  24.6 1.3 %shard_map.110 = (f32[6,64,256]{2,1,0:T(8,128)}, f32[6,64,256]{2,1,0:T(8,128)}) custom-call(s32[25]{0:T(128)S(4)} %get-tuple-element.44.table_ref, f32[6,8,8,256]{3,2,1,0:T(8,128)S(1)} %get-tuple-element.73.rows_ref, f32[8,8,256]{2,1,0:T(8,128)S(1)} %get-tuple-element.45.vrows_ref, f32[6,2,8,256]{3,2,1,0:T(8,128)S(1)} %shard_map.109.halo_ref, ...), custom_call_target="tpu_custom_call" | custom-call | bytes 5535000 | tf_op jit(solution)/shard_map/pallas_call | solution.py:636
  (6 shorter events, 0.1 us)
Async XLA Ops:
  0.6 17.5 %collective-permute-start.6 = (f32[6,64,256]{2,1,0:T(8,128)}, f32[6,64,256]{2,1,0:T(8,128)S(1)}, u32[]{:S(2)}, u32[]{:S(2)}) collective-permute-start(f32[6,64,256]{2,1,0:T(8,128)} %bitcast.14), channel_id=1, source_target_pairs={{0,8},{4,12},{8,0},{12,4},{1,9},{5,13},{9,1},{13,5},{2,10},{6,14},... | collective-permute-start | bytes 1179656 | tf_op jit(solution)/shard_map/ppermute | solution.py:613
  4.9 4.5 %collective-permute-start = (f32[6,64,128]{2,1,0:T(8,128)S(1)}, f32[6,64,128]{2,1,0:T(8,128)S(1)}, u32[]{:S(2)}, u32[]{:S(2)}) collective-permute-start(f32[6,64,128]{2,1,0:T(8,128)S(1)} %get-tuple-element.83), channel_id=1, source_target_pairs={{0,4},{4,0},{8,12},{12,8},{1,5},{5,1},{9,13},{13,9},{2,6},{6,2},{1... | collective-permute-start | bytes 589832 | tf_op jit(solution)/shard_map/ppermute | solution.py:613
  5.0 6.9 %collective-permute-start.1 = (f32[6,64,128]{2,1,0:T(8,128)S(1)}, f32[6,64,128]{2,1,0:T(8,128)S(1)}, u32[]{:S(2)}, u32[]{:S(2)}) collective-permute-start(f32[6,64,128]{2,1,0:T(8,128)S(1)} %get-tuple-element.82), channel_id=1, source_target_pairs={{0,4},{4,0},{8,12},{12,8},{1,5},{5,1},{9,13},{13,9},{2,6},{6,2},{1... | collective-permute-start | bytes 589832 | tf_op jit(solution)/shard_map/ppermute | solution.py:613
  5.4 7.3 %collective-permute-start.2 = (f32[48,256]{1,0:T(8,128)S(1)}, f32[48,256]{1,0:T(8,128)S(1)}, u32[]{:S(2)}, u32[]{:S(2)}) collective-permute-start(f32[48,256]{1,0:T(8,128)S(1)} %get-tuple-element.56), channel_id=1, source_target_pairs={{0,2},{1,3},{2,0},{3,1},{4,6},{5,7},{6,4},{7,5},{8,10},{9,11},{10,... | collective-permute-start | bytes 147464 | tf_op jit(solution)/shard_map/ppermute | solution.py:617
  8.0 6.0 %collective-permute-start.3 = (f32[48,256]{1,0:T(8,128)S(1)}, f32[48,256]{1,0:T(8,128)S(1)}, u32[]{:S(2)}, u32[]{:S(2)}) collective-permute-start(f32[48,256]{1,0:T(8,128)S(1)} %get-tuple-element.57), channel_id=1, source_target_pairs={{0,3},{1,2},{2,1},{3,0},{4,7},{5,6},{6,5},{7,4},{8,11},{9,10},{10,... | collective-permute-start | bytes 147464 | tf_op jit(solution)/shard_map/ppermute | solution.py:617
  9.4 4.6 %collective-permute-start.4 = (f32[48,256]{1,0:T(8,128)S(1)}, f32[48,256]{1,0:T(8,128)S(1)}, u32[]{:S(2)}, u32[]{:S(2)}) collective-permute-start(f32[48,256]{1,0:T(8,128)S(1)} %get-tuple-element.58), channel_id=1, source_target_pairs={{0,1},{1,0},{2,3},{3,2},{4,5},{5,4},{6,7},{7,6},{8,9},{9,8},{10,11... | collective-permute-start | bytes 147464 | tf_op jit(solution)/shard_map/ppermute | solution.py:617
  14.3 4.7 %collective-permute-start.8 = (f32[6,2,8,256]{3,2,1,0:T(8,128)S(1)}, f32[6,2,8,256]{3,2,1,0:T(8,128)S(1)}, u32[]{:S(2)}, u32[]{:S(2)}) collective-permute-start(f32[6,2,8,256]{3,2,1,0:T(8,128)S(1)} %shard_map.101.halo_ref), channel_id=1, source_target_pairs={{0,8},{4,12},{8,0},{12,4},{1,9},{5,13},{9,1},{13,5},{2,10},{6,14},... | collective-permute-start | bytes 294920 | tf_op jit(solution)/shard_map/ppermute | solution.py:613
  14.9 4.1 %collective-permute-start.5 = (f32[6,2,8,256]{3,2,1,0:T(8,128)S(1)}, f32[6,2,8,256]{3,2,1,0:T(8,128)S(1)}, u32[]{:S(2)}, u32[]{:S(2)}) collective-permute-start(f32[6,2,8,256]{3,2,1,0:T(8,128)S(1)} %shard_map.101.halo_ref), channel_id=1, source_target_pairs={{0,4},{4,0},{8,12},{12,8},{1,5},{5,1},{9,13},{13,9},{2,6},{6,2},{1... | collective-permute-start | bytes 294920 | tf_op jit(solution)/shard_map/ppermute | solution.py:613
  15.1 9.1 %collective-permute-start.12 = (f32[56,256]{1,0:T(8,128)S(1)}, f32[56,256]{1,0:T(8,128)S(1)}, u32[]{:S(2)}, u32[]{:S(2)}) collective-permute-start(f32[56,256]{1,0:T(8,128)S(1)} %get-tuple-element.75), channel_id=1, source_target_pairs={{0,2},{1,3},{2,0},{3,1},{4,6},{5,7},{6,4},{7,5},{8,10},{9,11},{10,... | collective-permute-start | bytes 172040 | tf_op jit(solution)/shard_map/ppermute | solution.py:617
  17.0 7.2 %collective-permute-start.13 = (f32[56,256]{1,0:T(8,128)S(1)}, f32[56,256]{1,0:T(8,128)S(1)}, u32[]{:S(2)}, u32[]{:S(2)}) collective-permute-start(f32[56,256]{1,0:T(8,128)S(1)} %get-tuple-element.76), channel_id=1, source_target_pairs={{0,3},{1,2},{2,1},{3,0},{4,7},{5,6},{6,5},{7,4},{8,11},{9,10},{10,... | collective-permute-start | bytes 172040 | tf_op jit(solution)/shard_map/ppermute | solution.py:617
  18.1 6.1 %collective-permute-start.14 = (f32[56,256]{1,0:T(8,128)S(1)}, f32[56,256]{1,0:T(8,128)S(1)}, u32[]{:S(2)}, u32[]{:S(2)}) collective-permute-start(f32[56,256]{1,0:T(8,128)S(1)} %get-tuple-element.77), channel_id=1, source_target_pairs={{0,1},{1,0},{2,3},{3,2},{4,5},{5,4},{6,7},{7,6},{8,9},{9,8},{10,11... | collective-permute-start | bytes 172040 | tf_op jit(solution)/shard_map/ppermute | solution.py:617
  19.0 1.9 %collective-permute-start.7 = (f32[6,64,256]{2,1,0:T(8,128)S(1)}, f32[6,64,256]{2,1,0:T(8,128)S(1)}, u32[]{:S(2)}, u32[]{:S(2)}) collective-permute-start(f32[6,64,256]{2,1,0:T(8,128)S(1)} %shard_map.103), channel_id=1, source_target_pairs={{0,4},{4,0},{8,12},{12,8},{1,5},{5,1},{9,13},{13,9},{2,6},{6,2},{1... | collective-permute-start | bytes 1179656 | tf_op jit(solution)/shard_map/ppermute | solution.py:613
  19.0 1.7 %collective-permute-start.9 = (f32[16,256]{1,0:T(8,128)S(1)}, f32[16,256]{1,0:T(8,128)S(1)}, u32[]{:S(2)}, u32[]{:S(2)}) collective-permute-start(f32[16,256]{1,0:T(8,128)S(1)} %slice_bitcast_fusion.2), channel_id=1, source_target_pairs={{0,4},{4,0},{8,12},{12,8},{1,5},{5,1},{9,13},{13,9},{2,6},{6,2},{1... | collective-permute-start | bytes 49160 | tf_op jit(solution)/shard_map/ppermute | solution.py:613
  20.7 2.5 %collective-permute-start.10 = (f32[40,256]{1,0:T(8,128)S(1)}, f32[40,256]{1,0:T(8,128)S(1)}, u32[]{:S(2)}, u32[]{:S(2)}) collective-permute-start(f32[40,256]{1,0:T(8,128)S(1)} %get-tuple-element.85), channel_id=1, source_target_pairs={{0,4},{4,0},{8,12},{12,8},{1,5},{5,1},{9,13},{13,9},{2,6},{6,2},{1... | collective-permute-start | bytes 122888 | tf_op jit(solution)/shard_map/ppermute | solution.py:613
  20.9 2.3 %collective-permute-start.11 = (f32[40,256]{1,0:T(8,128)S(1)}, f32[40,256]{1,0:T(8,128)S(1)}, u32[]{:S(2)}, u32[]{:S(2)}) collective-permute-start(f32[40,256]{1,0:T(8,128)S(1)} %get-tuple-element.84), channel_id=1, source_target_pairs={{0,4},{4,0},{8,12},{12,8},{1,5},{5,1},{9,13},{13,9},{2,6},{6,2},{1... | collective-permute-start | bytes 122888 | tf_op jit(solution)/shard_map/ppermute | solution.py:613

commit v8 on v7

--- a/solution.py
+++ b/solution.py
@@ -381,11 +381,10 @@
         halo_ref[c, l, :, pl.ds(128 * h, 128)] = halo
 
 
-def next_halo_kernel(
-    space_total, cap, table_ref, index_ref, weight_ref, outer_ref, across_ref, _, *more
-):
-    received, halos = more[: space_total - 1], more[space_total - 1 : -4]
-    halo_ref, pool_ref, raw_ref, far_ref = more[-4:]
+def next_halos(
+    space_total, cap, table_ref, index_ref, weight_ref, outer_ref, across_ref, halos, received,
+    halo_ref, pool_ref, raw_ref, far_ref
+):
     join_halos(halos, far_ref)
     omega, w_own, w_across, w_near, w_far = coefficients(weight_ref)
     gain = {}
@@ -565,9 +564,16 @@
 
 
 def last_kernel(
-    space_total, cap, table_ref, rows_ref, vrows_ref, halo_ref, part_ref, rate_ref, term_ref,
-    new_ref, residual_ref, new_half_ref, residual_half_ref, inverse_ref, left
-):
+    space_total, cap, table_ref, index_ref, weight_ref, rows_ref, vrows_ref, part_ref, rate_ref,
+    term_ref, outer_ref, across_ref, *more
+):
+    received, halos = more[: space_total - 1], more[space_total - 1 : -10]
+    new_ref, residual_ref, new_half_ref, residual_half_ref, inverse_ref, left = more[-10:-4]
+    halo_ref, pool_ref, raw_ref, far_ref = more[-4:]
+    next_halos(
+        space_total, cap, table_ref, index_ref, weight_ref, outer_ref, across_ref, halos, received,
+        halo_ref, pool_ref, raw_ref, far_ref,
+    )
     own = Rows(row_loader(lambda c, r: rows_ref[c, r], halo_ref))
     live_slots = table_ref[3 * FACES]
     live = (lax.broadcasted_iota(jnp.int32, vrows_ref.shape[1:], 0) // 2) < live_slots
@@ -769,20 +775,15 @@
         micros=0.5,
     )
     next_part, next_rate = pitch(next_rows)
-    next_halo = call(
-        functools.partial(next_halo_kernel, space_total, cap),
-        on_chip(outer),
-        [SMEM, VMEM, SMEM] + [VMEM] * (2 + space_total + len(far_halo)),
-        (table, index, weights, next_outer, across_halo, next_rate, *next_received, *far_halo),
-        scratch=pool + [pltpu.VMEM(outer, F32)],
-    )
     new, residual = call(
         functools.partial(last_kernel, space_total, cap),
         [jax.ShapeDtypeStruct(state.shape, F32)] * 2,
-        [SMEM] + [VMEM] * 6,
-        (table, next_rows, vrows, next_halo, next_part, next_rate, term),
+        [SMEM, VMEM, SMEM] + [VMEM] * (6 + space_total + len(far_halo)),
+        (table, index, weights, next_rows, vrows, next_part, next_rate, term, next_outer,
+         across_halo, *next_received, *far_halo),
         scratch=[pltpu.VMEM((comps, 2, row_count, 128), F32)] * 2
-        + [pltpu.VMEM(plane, F32), pltpu.SemaphoreType.DMA((4 * comps,))],
+        + [pltpu.VMEM(plane, F32), pltpu.SemaphoreType.DMA((4 * comps,)), pltpu.VMEM(outer, F32)]
+        + pool + [pltpu.VMEM(outer, F32)],
         micros=1.5,
         out_specs=[HBM] * 2,
     )

time: 26.1 us -> 26.1 us (level)
    pallas_call x15 -> x14, Pallas kernels: 8.6 us -> 8.67 us  [call(): pl.pallas_call(kernel, out_shape=out, in_specs=specs, out_specs=out_specs...]
where the time goes in v8:
time: 26.1 us; the launch traced here: 25.9 us
  starting transfers between devices  12.9 us (49%)
  Pallas kernels  8.69 us (33%)
  waiting for transfers between devices  2.78 us (11%)
  between operations  1.46 us (6%)
    pallas_call x14, Pallas kernels, call(): pl.pallas_call(kernel, out_shape=out, in_specs=specs, out_specs=out_specs...  8.67 us
    ppermute x6, starting transfers between devices, over_space(): lax.ppermute(parts[k - 1], 'space', [(i, partner(i, k, space_total)) for...  7.72 us
    ppermute x9, starting transfers between devices, over_inst(): return lax.ppermute(x, 'inst', [(i, i ^ flip) for i in range(4)])  5.19 us
    ppermute x9, waiting for transfers between devices, over_inst(): return lax.ppermute(x, 'inst', [(i, i ^ flip) for i in range(4)])  1.49 us
    ppermute x6, waiting for transfers between devices, over_space(): lax.ppermute(parts[k - 1], 'space', [(i, partner(i, k, space_total)) for...  1.29 us
  transfers between devices with their start and end apart: 15, of which 3 were waited for; matrix products, arithmetic and copies ran while one was open for 0% of the time, Pallas kernels for 27%

profile of v8, /device:TPU:0, one launch (start us, length us, event | category | flops | bytes accessed | tf_op | source)
XLA Modules:
  0.0 25.9 jit_solution(17143651355838528877)
XLA Ops:
  0.6 3.0 %collective-permute-start.6 = (f32[6,64,256]{2,1,0:T(8,128)}, f32[6,64,256]{2,1,0:T(8,128)S(1)}, u32[]{:S(2)}, u32[]{:S(2)}) collective-permute-start(f32[6,64,256]{2,1,0:T(8,128)} %bitcast.14), channel_id=1, source_target_pairs={{0,8},{4,12},{8,0},{12,4},{1,9},{5,13},{9,1},{13,5},{2,10},{6,14},... | collective-permute-start | bytes 1179656 | tf_op jit(solution)/shard_map/ppermute | solution.py:619
  3.6 1.2 %shard_map.95 = (f32[2,6,64,128]{3,2,1,0:T(8,128)S(1)}, f32[2,64,128]{2,1,0:T(8,128)S(1)}, f32[6,2,8,256]{3,2,1,0:T(8,128)S(1)}, s32[12]{0:T(128)S(4)}, f32[48,2...) custom-call(f32[6,64,256]{2,1,0:T(8,128)} %bitcast.15, f32[64,256]{1,0:T(8,128)} %volume_ref.1, ...), custom_call_target="tpu_custom_call" | custom-call | bytes 3690000 | tf_op jit(solution)/shard_map/pallas_call | solution.py:642
  4.9 0.1 collective-permute-start
  5.0 0.5 %collective-permute-start.1 = (f32[6,64,128]{2,1,0:T(8,128)S(1)}, f32[6,64,128]{2,1,0:T(8,128)S(1)}, u32[]{:S(2)}, u32[]{:S(2)}) collective-permute-start(f32[6,64,128]{2,1,0:T(8,128)S(1)} %get-tuple-element.82), channel_id=1, source_target_pairs={{0,4},{4,0},{8,12},{12,8},{1,5},{5,1},{9,13},{13,9},{2,6},{6,2},{1... | collective-permute-start | bytes 589832 | tf_op jit(solution)/shard_map/ppermute | solution.py:619
  5.4 2.6 %collective-permute-start.2 = (f32[48,256]{1,0:T(8,128)S(1)}, f32[48,256]{1,0:T(8,128)S(1)}, u32[]{:S(2)}, u32[]{:S(2)}) collective-permute-start(f32[48,256]{1,0:T(8,128)S(1)} %get-tuple-element.56), channel_id=1, source_target_pairs={{0,2},{1,3},{2,0},{3,1},{4,6},{5,7},{6,4},{7,5},{8,10},{9,11},{10,... | collective-permute-start | bytes 147464 | tf_op jit(solution)/shard_map/ppermute | solution.py:623
  8.0 1.3 %collective-permute-start.3 = (f32[48,256]{1,0:T(8,128)S(1)}, f32[48,256]{1,0:T(8,128)S(1)}, u32[]{:S(2)}, u32[]{:S(2)}) collective-permute-start(f32[48,256]{1,0:T(8,128)S(1)} %get-tuple-element.57), channel_id=1, source_target_pairs={{0,3},{1,2},{2,1},{3,0},{4,7},{5,6},{6,5},{7,4},{8,11},{9,10},{10,... | collective-permute-start | bytes 147464 | tf_op jit(solution)/shard_map/ppermute | solution.py:623
  9.4 0.0 collective-permute-done.low_ref
  9.4 0.2 collective-permute-start.4
  10.3 1.0 %shard_map.96 = (f32[6,8,8,256]{3,2,1,0:T(8,128)S(1)}, f32[8,8,256]{2,1,0:T(8,128)S(1)}, s32[25]{0:T(128)S(4)}, s32[8,256]{1,0:T(8,128)S(1)}) custom-call(f32[2,6,64,128]{3,2,1,0:T(8,128)S(1)} %get-tuple-element.42.half_ref, f32[2,64,128]{2,1,0:T(8,128)S(1)} %get-tuple-element.43.volume_half_ref, s32[4]{0:T(128)} %counts_in.3, s32[8]{0:T(128)} %place_in.3, ...), custom_call_target="tpu_custom_call" | custom-call | bytes 3690000 | tf_op jit(solution)/shard_map/pallas_call | solution.py:642
  11.3 0.5 %shard_map.99 = (f32[6,8,8,256]{3,2,1,0:T(8,128)S(1)}, f32[8,8,256]{2,1,0:T(8,128)S(1)}) custom-call(f32[8]{0:T(128)S(4)} %shard_map.97.weight_ref, f32[6,8,8,256]{3,2,1,0:T(8,128)S(1)} %get-tuple-element.47.rows_ref, f32[8,8,256]{2,1,0:T(8,128)S(1)} %get-tuple-element.46.vrows_ref), custom_call_target="tpu_custom_call" | custom-call | bytes 1845000 | tf_op jit(solution)/shard_map/pallas_call | solution.py:642
  11.8 0.0 collective-permute-done.1.high_ref
  11.8 0.5 %shard_map.98 = (f32[6,8,8,256]{3,2,1,0:T(8,128)S(1)}, f32[6,8,8,256]{3,2,1,0:T(8,128)S(1)}, f32[8,8,256]{2,1,0:T(8,128)S(1)}) custom-call(f32[8]{0:T(128)S(4)} %shard_map.97.weight_ref, f32[8,8,256]{2,1,0:T(8,128)S(1)} %get-tuple-element.46.vrows_ref, f32[6,64,128]{2,1,0:T(8,128)S(1)} %collective-permute-done.low_ref, ...), custom_call_target="tpu_custom_call" | custom-call | bytes 1845000 | tf_op jit(solution)/shard_map/pallas_call | solution.py:642
  12.4 0.4 %shard_map.100 = (f32[6,8,8,256]{3,2,1,0:T(8,128)S(1)}, f32[6,8,8,256]{3,2,1,0:T(8,128)S(1)}, f32[8,8,256]{2,1,0:T(8,128)S(1)}, f32[8,8,256]{2,1,0:T(8,128)S(1)}) custom-call(f32[8]{0:T(128)S(4)} %shard_map.97.weight_ref, f32[8,8,256]{2,1,0:T(8,128)S(1)} %get-tuple-element.46.vrows_ref, f32[6,8,8,256]{3,2,1,0:T(8,128)S(1)} %get-tuple-element.47.rows_ref, ...), custom_call_target="tpu_custom_call" | custom-call | bytes 1107000 | tf_op jit(solution)/shard_map/pallas_call | solution.py:642
  12.7 0.0 collective-permute-done.2.more_0_
  12.7 1.3 %collective-permute-done.3.more_1_ = f32[48,256]{1,0:T(8,128)S(1)} collective-permute-done((f32[48,256]{1,0:T(8,128)S(1)}, f32[48,256]{1,0:T(8,128)S(1)}, u32[]{:S(2)}, u32[]{:S(2)}) %collective-permute-start.3) | collective-permute-done | bytes 49184 | tf_op jit(solution)/shard_map/ppermute | solution.py:623
  14.0 0.0 collective-permute-done.4.more_2_
  14.0 0.3 %shard_map.101.halo_ref = f32[6,2,8,256]{3,2,1,0:T(8,128)S(1)} custom-call(s32[25]{0:T(128)S(4)} %get-tuple-element.44.table_ref, s32[8,256]{1,0:T(8,128)S(1)} %get-tuple-element.45.index_ref, f32[6,2,8,256]{3,2,1,0:T(8,128)S(1)} %get-tuple-element.51.outer_ref, f32[8,8,256]{2,1,0:T(8,128)S(1)} %get-tuple-element.54._.own_gain_ref, ...), custom_call_target="tpu_custom_call" | custom-call | bytes 1107000 | tf_op jit(solution)/shard_map/pallas_call | solution.py:642
  14.3 0.6 %collective-permute-start.8 = (f32[6,2,8,256]{3,2,1,0:T(8,128)S(1)}, f32[6,2,8,256]{3,2,1,0:T(8,128)S(1)}, u32[]{:S(2)}, u32[]{:S(2)}) collective-permute-start(f32[6,2,8,256]{3,2,1,0:T(8,128)S(1)} %shard_map.101.halo_ref), channel_id=1, source_target_pairs={{0,8},{4,12},{8,0},{12,4},{1,9},{5,13},{9,1},{13,5},{2,10},{6,14},... | collective-permute-start | bytes 294920 | tf_op jit(solution)/shard_map/ppermute | solution.py:619
  14.9 0.0 collective-permute-start.5
  14.9 0.2 shard_map.102
  15.1 1.9 %collective-permute-start.12 = (f32[56,256]{1,0:T(8,128)S(1)}, f32[56,256]{1,0:T(8,128)S(1)}, u32[]{:S(2)}, u32[]{:S(2)}) collective-permute-start(f32[56,256]{1,0:T(8,128)S(1)} %get-tuple-element.77), channel_id=1, source_target_pairs={{0,2},{1,3},{2,0},{3,1},{4,6},{5,7},{6,4},{7,5},{8,10},{9,11},{10,... | collective-permute-start | bytes 172040 | tf_op jit(solution)/shard_map/ppermute | solution.py:623
  17.0 1.1 %collective-permute-start.13 = (f32[56,256]{1,0:T(8,128)S(1)}, f32[56,256]{1,0:T(8,128)S(1)}, u32[]{:S(2)}, u32[]{:S(2)}) collective-permute-start(f32[56,256]{1,0:T(8,128)S(1)} %get-tuple-element.78), channel_id=1, source_target_pairs={{0,3},{1,2},{2,1},{3,0},{4,7},{5,6},{6,5},{7,4},{8,11},{9,10},{10,... | collective-permute-start | bytes 172040 | tf_op jit(solution)/shard_map/ppermute | solution.py:623
  18.1 0.0 collective-permute-done.6.raw_ref
  18.1 0.6 %collective-permute-start.14 = (f32[56,256]{1,0:T(8,128)S(1)}, f32[56,256]{1,0:T(8,128)S(1)}, u32[]{:S(2)}, u32[]{:S(2)}) collective-permute-start(f32[56,256]{1,0:T(8,128)S(1)} %get-tuple-element.79), channel_id=1, source_target_pairs={{0,1},{1,0},{2,3},{3,2},{4,5},{5,4},{6,7},{7,6},{8,9},{9,8},{10,11... | collective-permute-start | bytes 172040 | tf_op jit(solution)/shard_map/ppermute | solution.py:623
  18.7 0.2 collective-permute-done.8.halo_ref.across_ref
  19.0 0.0 collective-permute-start.7
  19.0 0.0 collective-permute-done.5.sibling_halo_ref
  19.0 0.5 %collective-permute-start.9 = (f32[16,256]{1,0:T(8,128)S(1)}, f32[16,256]{1,0:T(8,128)S(1)}, u32[]{:S(2)}, u32[]{:S(2)}) collective-permute-start(f32[16,256]{1,0:T(8,128)S(1)} %slice_bitcast_fusion.2), channel_id=1, source_target_pairs={{0,4},{4,0},{8,12},{12,8},{1,5},{5,1},{9,13},{13,9},{2,6},{6,2},{1... | collective-permute-start | bytes 49160 | tf_op jit(solution)/shard_map/ppermute | solution.py:619
  19.5 1.2 %collective-permute-done.9.more_0_.more_3_ = f32[16,256]{1,0:T(8,128)S(1)} collective-permute-done((f32[16,256]{1,0:T(8,128)S(1)}, f32[16,256]{1,0:T(8,128)S(1)}, u32[]{:S(2)}, u32[]{:S(2)}) %collective-permute-start.9) | collective-permute-done | bytes 16416 | tf_op jit(solution)/shard_map/ppermute | solution.py:619
  20.7 0.1 collective-permute-start.10
  20.9 0.0 collective-permute-done.7.raw_ref
  20.9 0.4 %collective-permute-start.11 = (f32[40,256]{1,0:T(8,128)S(1)}, f32[40,256]{1,0:T(8,128)S(1)}, u32[]{:S(2)}, u32[]{:S(2)}) collective-permute-start(f32[40,256]{1,0:T(8,128)S(1)} %get-tuple-element.84), channel_id=1, source_target_pairs={{0,4},{4,0},{8,12},{12,8},{1,5},{5,1},{9,13},{13,9},{2,6},{6,2},{1... | collective-permute-start | bytes 122888 | tf_op jit(solution)/shard_map/ppermute | solution.py:619
  21.2 0.5 %shard_map.104 = (f32[6,8,8,256]{3,2,1,0:T(8,128)S(1)}, f32[6,8,8,256]{3,2,1,0:T(8,128)S(1)}, f32[8,8,256]{2,1,0:T(8,128)S(1)}) custom-call(f32[8]{0:T(128)S(4)} %shard_map.97.weight_ref, f32[8,8,256]{2,1,0:T(8,128)S(1)} %get-tuple-element.46.vrows_ref, f32[6,64,256]{2,1,0:T(8,128)S(1)} %collective-permute-done.7.raw_ref), custom_call_target="tpu_custom_call" | custom-call | bytes 2214000 | tf_op jit(solution)/shard_map/pallas_call | solution.py:642
  21.8 0.4 %shard_map.105 = (f32[6,8,8,256]{3,2,1,0:T(8,128)S(1)}, f32[6,8,8,256]{3,2,1,0:T(8,128)S(1)}) custom-call(f32[8]{0:T(128)S(4)} %shard_map.97.weight_ref, f32[8,8,256]{2,1,0:T(8,128)S(1)} %get-tuple-element.46.vrows_ref, f32[6,8,8,256]{3,2,1,0:T(8,128)S(1)} %get-tuple-element.47.rows_ref, ...), custom_call_target="tpu_custom_call", output_to_operand_aliasing={{0}: (11, {}), {1}: (12, {})} | custom-call | bytes 1476000 | tf_op jit(solution)/shard_map/pallas_call | solution.py:642
  22.2 1.0 %shard_map.106 = (f32[6,8,8,256]{3,2,1,0:T(8,128)S(1)}, f32[6,8,8,256]{3,2,1,0:T(8,128)S(1)}, f32[6,8,8,256]{3,2,1,0:T(8,128)S(1)}, f32[8,8,256]{2,1,0:T(8,128)S(1)}, f32[8,8,256]{2,1,0:T(8,128)S(1)}) custom-call(f32[8]{0:T(128)S(4)} %shard_map.97.weight_ref, f32[8,8,256]{2,1,0:T(8,128)S(1)} %get-tuple-element.46.vrows_ref, ...), custom_call_target="tpu_custom_call" | custom-call | bytes 3690000 | tf_op jit(solution)/shard_map/pallas_call | solution.py:642
  23.2 0.0 collective-permute-done.10.more_1_.more_4_
  23.2 0.0 collective-permute-done.11.more_2_.more_5_
  23.2 0.5 %shard_map.107 = (f32[6,8,8,256]{3,2,1,0:T(8,128)S(1)}, f32[6,8,8,256]{3,2,1,0:T(8,128)S(1)}) custom-call(f32[8]{0:T(128)S(4)} %shard_map.97.weight_ref, f32[8,8,256]{2,1,0:T(8,128)S(1)} %get-tuple-element.46.vrows_ref, f32[6,8,8,256]{3,2,1,0:T(8,128)S(1)} %get-tuple-element.47.rows_ref, f32[6,8,8,256]{3,2,1,0:T(8,128)S(1)} %get-tuple-element.48.sibling_ref, ...), custom_call_target="tpu_custom_call" | custom-call | bytes 1845000 | tf_op jit(solution)/shard_map/pallas_call | solution.py:642
  23.7 0.5 %shard_map.108 = (f32[6,8,8,256]{3,2,1,0:T(8,128)S(1)}, f32[8,8,256]{2,1,0:T(8,128)S(1)}) custom-call(f32[8]{0:T(128)S(4)} %shard_map.97.weight_ref, f32[6,8,8,256]{3,2,1,0:T(8,128)S(1)} %get-tuple-element.73.rows_ref, f32[8,8,256]{2,1,0:T(8,128)S(1)} %get-tuple-element.46.vrows_ref), custom_call_target="tpu_custom_call" | custom-call | bytes 1845000 | tf_op jit(solution)/shard_map/pallas_call | solution.py:642
  24.2 0.0 collective-permute-done.12.more_0_
  24.2 0.0 collective-permute-done.13.more_1_
  24.2 0.0 collective-permute-done.14.more_2_
  24.2 1.7 %shard_map.109 = (f32[6,64,256]{2,1,0:T(8,128)}, f32[6,64,256]{2,1,0:T(8,128)}) custom-call(s32[25]{0:T(128)S(4)} %get-tuple-element.44.table_ref, s32[8,256]{1,0:T(8,128)S(1)} %get-tuple-element.45.index_ref, f32[8]{0:T(128)S(4)} %shard_map.97.weight_ref, f32[6,8,8,256]{3,2,1,0:T(8,128)S(1)} %get-tuple-element.73.rows_ref, ...), custom_call_target="tpu_custom_call" | custom-call | bytes 5535000 | tf_op jit(solution)/shard_map/pallas_call | solution.py:642
  (6 shorter events, 0.1 us)
Async XLA Ops:
  0.6 17.5 %collective-permute-start.6 = (f32[6,64,256]{2,1,0:T(8,128)}, f32[6,64,256]{2,1,0:T(8,128)S(1)}, u32[]{:S(2)}, u32[]{:S(2)}) collective-permute-start(f32[6,64,256]{2,1,0:T(8,128)} %bitcast.14), channel_id=1, source_target_pairs={{0,8},{4,12},{8,0},{12,4},{1,9},{5,13},{9,1},{13,5},{2,10},{6,14},... | collective-permute-start | bytes 1179656 | tf_op jit(solution)/shard_map/ppermute | solution.py:619
  4.9 4.5 %collective-permute-start = (f32[6,64,128]{2,1,0:T(8,128)S(1)}, f32[6,64,128]{2,1,0:T(8,128)S(1)}, u32[]{:S(2)}, u32[]{:S(2)}) collective-permute-start(f32[6,64,128]{2,1,0:T(8,128)S(1)} %get-tuple-element.83), channel_id=1, source_target_pairs={{0,4},{4,0},{8,12},{12,8},{1,5},{5,1},{9,13},{13,9},{2,6},{6,2},{1... | collective-permute-start | bytes 589832 | tf_op jit(solution)/shard_map/ppermute | solution.py:619
  5.0 6.9 %collective-permute-start.1 = (f32[6,64,128]{2,1,0:T(8,128)S(1)}, f32[6,64,128]{2,1,0:T(8,128)S(1)}, u32[]{:S(2)}, u32[]{:S(2)}) collective-permute-start(f32[6,64,128]{2,1,0:T(8,128)S(1)} %get-tuple-element.82), channel_id=1, source_target_pairs={{0,4},{4,0},{8,12},{12,8},{1,5},{5,1},{9,13},{13,9},{2,6},{6,2},{1... | collective-permute-start | bytes 589832 | tf_op jit(solution)/shard_map/ppermute | solution.py:619
  5.4 7.3 %collective-permute-start.2 = (f32[48,256]{1,0:T(8,128)S(1)}, f32[48,256]{1,0:T(8,128)S(1)}, u32[]{:S(2)}, u32[]{:S(2)}) collective-permute-start(f32[48,256]{1,0:T(8,128)S(1)} %get-tuple-element.56), channel_id=1, source_target_pairs={{0,2},{1,3},{2,0},{3,1},{4,6},{5,7},{6,4},{7,5},{8,10},{9,11},{10,... | collective-permute-start | bytes 147464 | tf_op jit(solution)/shard_map/ppermute | solution.py:623
  8.0 6.0 %collective-permute-start.3 = (f32[48,256]{1,0:T(8,128)S(1)}, f32[48,256]{1,0:T(8,128)S(1)}, u32[]{:S(2)}, u32[]{:S(2)}) collective-permute-start(f32[48,256]{1,0:T(8,128)S(1)} %get-tuple-element.57), channel_id=1, source_target_pairs={{0,3},{1,2},{2,1},{3,0},{4,7},{5,6},{6,5},{7,4},{8,11},{9,10},{10,... | collective-permute-start | bytes 147464 | tf_op jit(solution)/shard_map/ppermute | solution.py:623
  9.4 4.6 %collective-permute-start.4 = (f32[48,256]{1,0:T(8,128)S(1)}, f32[48,256]{1,0:T(8,128)S(1)}, u32[]{:S(2)}, u32[]{:S(2)}) collective-permute-start(f32[48,256]{1,0:T(8,128)S(1)} %get-tuple-element.58), channel_id=1, source_target_pairs={{0,1},{1,0},{2,3},{3,2},{4,5},{5,4},{6,7},{7,6},{8,9},{9,8},{10,11... | collective-permute-start | bytes 147464 | tf_op jit(solution)/shard_map/ppermute | solution.py:623
  14.3 4.7 %collective-permute-start.8 = (f32[6,2,8,256]{3,2,1,0:T(8,128)S(1)}, f32[6,2,8,256]{3,2,1,0:T(8,128)S(1)}, u32[]{:S(2)}, u32[]{:S(2)}) collective-permute-start(f32[6,2,8,256]{3,2,1,0:T(8,128)S(1)} %shard_map.101.halo_ref), channel_id=1, source_target_pairs={{0,8},{4,12},{8,0},{12,4},{1,9},{5,13},{9,1},{13,5},{2,10},{6,14},... | collective-permute-start | bytes 294920 | tf_op jit(solution)/shard_map/ppermute | solution.py:619
  14.9 4.1 %collective-permute-start.5 = (f32[6,2,8,256]{3,2,1,0:T(8,128)S(1)}, f32[6,2,8,256]{3,2,1,0:T(8,128)S(1)}, u32[]{:S(2)}, u32[]{:S(2)}) collective-permute-start(f32[6,2,8,256]{3,2,1,0:T(8,128)S(1)} %shard_map.101.halo_ref), channel_id=1, source_target_pairs={{0,4},{4,0},{8,12},{12,8},{1,5},{5,1},{9,13},{13,9},{2,6},{6,2},{1... | collective-permute-start | bytes 294920 | tf_op jit(solution)/shard_map/ppermute | solution.py:619
  15.1 9.1 %collective-permute-start.12 = (f32[56,256]{1,0:T(8,128)S(1)}, f32[56,256]{1,0:T(8,128)S(1)}, u32[]{:S(2)}, u32[]{:S(2)}) collective-permute-start(f32[56,256]{1,0:T(8,128)S(1)} %get-tuple-element.77), channel_id=1, source_target_pairs={{0,2},{1,3},{2,0},{3,1},{4,6},{5,7},{6,4},{7,5},{8,10},{9,11},{10,... | collective-permute-start | bytes 172040 | tf_op jit(solution)/shard_map/ppermute | solution.py:623
  17.0 7.2 %collective-permute-start.13 = (f32[56,256]{1,0:T(8,128)S(1)}, f32[56,256]{1,0:T(8,128)S(1)}, u32[]{:S(2)}, u32[]{:S(2)}) collective-permute-start(f32[56,256]{1,0:T(8,128)S(1)} %get-tuple-element.78), channel_id=1, source_target_pairs={{0,3},{1,2},{2,1},{3,0},{4,7},{5,6},{6,5},{7,4},{8,11},{9,10},{10,... | collective-permute-start | bytes 172040 | tf_op jit(solution)/shard_map/ppermute | solution.py:623
  18.1 6.1 %collective-permute-start.14 = (f32[56,256]{1,0:T(8,128)S(1)}, f32[56,256]{1,0:T(8,128)S(1)}, u32[]{:S(2)}, u32[]{:S(2)}) collective-permute-start(f32[56,256]{1,0:T(8,128)S(1)} %get-tuple-element.79), channel_id=1, source_target_pairs={{0,1},{1,0},{2,3},{3,2},{4,5},{5,4},{6,7},{7,6},{8,9},{9,8},{10,11... | collective-permute-start | bytes 172040 | tf_op jit(solution)/shard_map/ppermute | solution.py:623
  19.0 1.9 %collective-permute-start.7 = (f32[6,64,256]{2,1,0:T(8,128)S(1)}, f32[6,64,256]{2,1,0:T(8,128)S(1)}, u32[]{:S(2)}, u32[]{:S(2)}) collective-permute-start(f32[6,64,256]{2,1,0:T(8,128)S(1)} %shard_map.103), channel_id=1, source_target_pairs={{0,4},{4,0},{8,12},{12,8},{1,5},{5,1},{9,13},{13,9},{2,6},{6,2},{1... | collective-permute-start | bytes 1179656 | tf_op jit(solution)/shard_map/ppermute | solution.py:619
  19.0 1.7 %collective-permute-start.9 = (f32[16,256]{1,0:T(8,128)S(1)}, f32[16,256]{1,0:T(8,128)S(1)}, u32[]{:S(2)}, u32[]{:S(2)}) collective-permute-start(f32[16,256]{1,0:T(8,128)S(1)} %slice_bitcast_fusion.2), channel_id=1, source_target_pairs={{0,4},{4,0},{8,12},{12,8},{1,5},{5,1},{9,13},{13,9},{2,6},{6,2},{1... | collective-permute-start | bytes 49160 | tf_op jit(solution)/shard_map/ppermute | solution.py:619
  20.7 2.5 %collective-permute-start.10 = (f32[40,256]{1,0:T(8,128)S(1)}, f32[40,256]{1,0:T(8,128)S(1)}, u32[]{:S(2)}, u32[]{:S(2)}) collective-permute-start(f32[40,256]{1,0:T(8,128)S(1)} %get-tuple-element.85), channel_id=1, source_target_pairs={{0,4},{4,0},{8,12},{12,8},{1,5},{5,1},{9,13},{13,9},{2,6},{6,2},{1... | collective-permute-start | bytes 122888 | tf_op jit(solution)/shard_map/ppermute | solution.py:619
  20.9 2.3 %collective-permute-start.11 = (f32[40,256]{1,0:T(8,128)S(1)}, f32[40,256]{1,0:T(8,128)S(1)}, u32[]{:S(2)}, u32[]{:S(2)}) collective-permute-start(f32[40,256]{1,0:T(8,128)S(1)} %get-tuple-element.84), channel_id=1, source_target_pairs={{0,4},{4,0},{8,12},{12,8},{1,5},{5,1},{9,13},{13,9},{2,6},{6,2},{1... | collective-permute-start | bytes 122888 | tf_op jit(solution)/shard_map/ppermute | solution.py:619
